TPU v7x, 256 devices: a whole 4x4x8 slice. The times are simulated.
256 devices in a mesh: grp: 4 (over x_lo, core), dp: 64 (over x_hi, y, z).
Axes of the slice: x: 4 (x_hi: 2, x_lo: 2; x = x_hi * 2 + x_lo), y: 4, z: 8, core: 2. Of those that a mesh axis runs over, the one named last changes fastest.
Arguments:
- activations: bfloat16 [2, 131072, 768], P(None, ('grp', 'dp')), may hold values from -300 to 300
- back_grads: bfloat16 [2, 131072, 768], P(None, ('grp', 'dp')), may hold values from -300 to 300
- grads: float32 [2, 768, 768], P(None, 'dp'), may hold values from -6 to 6
- owners: int32 [4], replicated, may hold values from 0 to 3, as said below
Outputs:
- preconditioned: float32 [2, 768, 768], P(None, 'dp', 'grp')
- owner_store: float32 [8, 768, 768], P('grp', 'dp')
Inputs may be any that keep to these rules, and one draw needn't show every extreme that they name: `owners`: one group owns 2 factors, two groups own one factor each, and every other group owns none.
All inputs are finite; a program needn't handle non-finite values. Where the computation divides by a largest or mean magnitude, that divisor is 1e-20 or more.
Results may differ from a plain program's by a relative error of at most 0.004.
Values may be sent and summed in bfloat16 or wider, within the bound.
No kernel may reach another device: no remote copies, remote signals or barrier semaphores. Data moves between devices by JAX's collectives and lax.ppermute only.
A program may use at most 64 MiB of HBM per device.

v0:
```python
import jax
import jax.numpy as jnp
from jax import lax
from jax.sharding import PartitionSpec as P

ITERS = 4
CAP = 2


DAMPING = 0.1
exact_mode = lax.Precision.HIGHEST


def from_root(block, axis, owner):
    block = jnp.where(lax.axis_index(axis) == owner, block, jnp.zeros_like(block))
    return lax.psum(block, axis)


def shards(activations, back_grads, grads, owners):
    groups = lax.axis_size("grp")
    parallel = lax.axis_size("dp")
    group_id = lax.axis_index("grp")
    row_id = lax.axis_index("dp")
    layers, tok_local, feat_width = activations.shape
    nfactor = 2 * layers
    row_count = feat_width // parallel
    columns = feat_width // groups
    total_tokens = tok_local * groups * parallel
    stacked = jnp.stack([activations, back_grads], axis=1).reshape(nfactor, tok_local, feat_width)
    partial_rows = lax.psum_scatter(
        jnp.einsum("ftk,ftn->kfn", stacked, stacked, preferred_element_type=jnp.float32),
        "dp",
        scatter_dimension=0,
        tiled=True,
    )
    summed = lax.psum(partial_rows, "grp")
    factor_rows = jnp.transpose(summed, (1, 0, 2)) / float(total_tokens)
    factor_ids = jnp.arange(nfactor)
    same_owner = owners[:, None] == owners[None, :]
    earlier = factor_ids[None, :] < factor_ids[:, None]
    owner_rank = jnp.sum((same_owner & earlier).astype(jnp.int32), axis=1)
    listed_weights = (
        (owners[None, :] == group_id) & (owner_rank[None, :] == jnp.arange(CAP)[:, None])
    ).astype(jnp.float32)
    slot_count = CAP
    filled = jnp.sum(listed_weights, axis=1)
    chosen = jnp.sum(listed_weights[:, :, None, None] * factor_rows[None], axis=1)
    offsets = row_id * row_count
    eye_rows = (jnp.arange(feat_width)[None, :] == offsets + jnp.arange(row_count)[:, None]).astype(
        jnp.float32
    )
    damped = chosen + DAMPING * eye_rows
    local_bound = jnp.max(jnp.sum(jnp.abs(damped), axis=2), axis=1)
    bound_max = lax.pmax(local_bound, "dp")
    inverse_bound = 1.0 / bound_max
    low_rows = damped.astype(jnp.bfloat16)
    low_scale = inverse_bound.astype(jnp.bfloat16).astype(jnp.float32)
    low_full = lax.all_gather(low_rows, "dp", axis=1, tiled=True)
    identity = jnp.eye(feat_width, dtype=jnp.float32)
    image_low = (low_full.astype(jnp.float32) * low_scale[:, None, None]).astype(jnp.bfloat16)
    iterate = 2.0 * (identity[None] * inverse_bound[:, None, None]) - low_scale[
        :, None, None
    ] * image_low.astype(jnp.float32)
    for sweep in range(1, ITERS):
        iterate_low = iterate.astype(jnp.bfloat16)
        image_low = jnp.einsum(
            "cij,cjk->cik", low_full, iterate_low, preferred_element_type=jnp.float32
        ).astype(jnp.bfloat16)
        iterate = 2.0 * iterate - jnp.einsum(
            "cij,cjk->cik", iterate_low, image_low, preferred_element_type=jnp.float32
        )
    inverse_rows = lax.dynamic_slice_in_dim(iterate, offsets, row_count, 1)
    pieces = []
    for factor in range(nfactor):
        picked_slot = jnp.minimum(owner_rank[factor], slot_count - 1)
        fragment = lax.dynamic_index_in_dim(inverse_rows, picked_slot, 0, keepdims=False)
        pieces.append(from_root(fragment, "grp", owners[factor]))
    spread_rows = jnp.stack(pieces)
    owner_store = inverse_rows * filled[:, None, None]
    input_inv = spread_rows[0::2]
    output_inv = spread_rows[1::2]
    input_cols = lax.dynamic_slice_in_dim(input_inv, group_id * columns, columns, 2)
    window = grads
    mapped = jnp.einsum(
        "lrk,lkc->lrc",
        window,
        lax.all_gather(input_cols, "dp", axis=1, tiled=True),
        precision=exact_mode,
        preferred_element_type=jnp.float32,
    )
    window = output_inv
    result = lax.psum_scatter(
        jnp.einsum(
            "lrk,lrc->klc", window, mapped, precision=exact_mode, preferred_element_type=jnp.float32
        ),
        "dp",
        scatter_dimension=0,
        tiled=True,
    )
    return (jnp.transpose(result, (1, 0, 2)), owner_store)


def solution(mesh):
    return jax.shard_map(
        shards,
        mesh=mesh,
        in_specs=(
            P(None, ("grp", "dp"), None),
            P(None, ("grp", "dp"), None),
            P(None, "dp", None),
            P(),
        ),
        out_specs=(P(None, "dp", "grp"), P("grp", "dp", None)),
        check_vma=False,
    )
```

profile of v0, /device:TPU:2, one launch (start us, length us, event | category | flops | bytes accessed | tf_op | source)
XLA Modules:
  0.0 1888.3 jit_solution(5228984575829886716)
XLA Ops:
  7.2 0.0 all-reduce.10.cloned.1.call-start
  7.2 2.2 pad_maximum_fusion
  9.4 0.2 copy.32
  9.6 5.1 convolution_bitcast_fusion
  14.8 12.1 copy.34
  26.8 0.0 all-reduce.10.cloned.1.call-update
  26.9 0.0 all-reduce.8.cloned.1.call-start
  26.9 0.6 copy-done.3
  27.5 0.6 dynamic-slice
  28.8 0.2 convert_reduce_fusion
  29.0 0.1 fusion.50
  29.0 727.4 %all-reduce.10.cloned.1.call-done = f32[768,4,768]{2,1,0:T(4,128)} async-done(((f32[768,4,768]{2,1,0:T(4,128)}), f32[768,4,768]{2,1,0:T(4,128)}) %all-reduce.10.cloned.1.call-update) | async-done | bytes 9437200
  756.4 1.6 constant_dynamic-slice_fusion.1
  758.0 0.0 all-reduce.8.cloned.1.call-update
  758.0 0.0 all-gather.3.cloned.1.call-start
  758.1 38.5 %all-reduce.8.cloned.1.call-done = f32[12,4,768]{2,1,0:T(4,128)} async-done(((f32[12,4,768]{2,1,0:T(4,128)}), f32[12,4,768]{2,1,0:T(4,128)}) %all-reduce.8.cloned.1.call-update) | async-done | bytes 147472 | tf_op jit(solution)/shard_map/psum | solution.py:36
  796.6 0.9 multiply_bitcast_fusion
  797.6 0.2 multiply_reduce_fusion
  797.8 0.1 add_convert_fusion
  797.9 0.7 copy.36
  798.6 0.0 all-reduce.14.cloned.1.call-start
  798.6 0.6 fusion.56
  801.7 0.7 fusion.55
  804.8 0.2 fusion.7
  805.0 0.1 reduce_max.9
  805.1 183.9 %pmax.7 = f32[2]{0:T(128)S(1)} all-reduce(f32[2]{0:T(128)S(1)} %reduce_max.9), channel_id=1, replica_groups=mesh['grp'=4,'dp'=64] {'dp'}, use_global_device_ids=true, to_apply=%region_6.0 | all-reduce | flops 2 | bytes 16 | tf_op jit(solution)/shard_map/pmax | solution.py:54
  989.1 10.8 multiply_subtract_fusion.2
  999.9 11.9 multiply_subtract_fusion.1
  1011.7 11.2 multiply_subtract_fusion
  1023.0 1.7 dynamic-slice_select_fusion
  1024.7 0.0 all-gather.5.cloned.1.call-start
  1024.7 34.1 %all-reduce.14.cloned.1.call-done = (f32[1,12,768]{2,1,0:T(8,128)}, f32[1,12,768]{2,1,0:T(8,128)}, f32[1,12,768]{2,1,0:T(8,128)}, f32[1,12,768]{2,1,0:T(8,128)}) async-done(((f32[1,12,768]{2,1,0:T(8,128)}, f32[1,12,768]{2,1,0:T(8,128)}, f32[1,12,768]{2,1,0:T(8,128)}, f32[1,12,768]{2,1,0:T(8,128)}), (f32[1,12,768]{2,1,0:T(8,128)}, f32[1,12,768]{2,1,0:T(8,128)}, f32[1,12,768]{2,1,0:T(8,128)}, ...) | async-done | bytes 147472 | tf_op jit(solution)/shard_map/psum | solution.py:16
  1058.8 0.8 constant_dynamic-update-slice_fusion.3
  1059.6 0.8 constant_dynamic-update-slice_fusion.2
  1060.5 0.8 constant_dynamic-update-slice_fusion.1
  1061.3 0.8 constant_dynamic-update-slice_fusion
  1062.1 0.1 constant_dynamic-slice_fusion
  1062.2 0.6 copy.41
  1062.8 0.0 all-reduce.12.cloned.1.call-start
  1062.9 116.9 %all-gather.5.cloned.1.call-done = f32[2,768,192]{2,0,1:T(2,128)} async-done(((f32[2,12,192]{2,0,1:T(2,128)}), f32[2,768,192]{2,0,1:T(2,128)}) %all-gather.5.cloned.1.call-update) | async-done | bytes 1179664 | tf_op jit(solution)/shard_map/all_gather | solution.py:87
  1179.8 2.3 fusion.14
  1182.1 1.1 convolution_bitcast_fusion.1
  1183.3 2.1 copy.44
  1185.4 0.1 fusion.54
  1185.5 1.0 dynamic-slice_multiply_fusion
  1186.5 0.7 copy.45
  1187.2 693.0 %all-reduce.12.cloned.1.call-done = f32[768,2,192]{2,1,0:T(2,128)} async-done(((f32[768,2,192]{2,1,0:T(2,128)}), f32[768,2,192]{2,1,0:T(2,128)}) %all-reduce.12.cloned.1.call-update) | async-done | bytes 1179664
  1880.1 1.3 dynamic-slice_bitcast_fusion
  (17 shorter events, 0.1 us)
Async XLA Ops:
  7.2 1172.6 %copy-start = (f32[2,12,768]{2,0,1:T(2,128)S(1)}, f32[2,12,768]{2,0,1:T(2,128)}, u32[]{:S(2)}) copy-start(f32[2,12,768]{2,0,1:T(2,128)} %param.6) | copy-start | bytes 221188
  7.2 749.2 %all-reduce.10.cloned.1.call-start = ((), (), s32[]{:S(2)}) async-start(), calls=%async_computation.3 | async-start | bytes 18874368
  26.8 0.7 copy-start.3
  26.8 1.9 copy-start.1
  26.9 769.7 %all-reduce.8.cloned.1.call-start = ((), (), s32[]{:S(2)}) async-start(), calls=%async_computation | async-start | bytes 294912 | tf_op jit(solution)/shard_map/psum | solution.py:36
  758.0 231.1 %all-gather.3.cloned.1.call-start = ((), (), s32[]{:S(2)}) async-start(), calls=%async_computation.1 | async-start | bytes 2396160 | tf_op jit(solution)/shard_map/all_gather | solution.py:58
  798.6 260.3 %all-reduce.14.cloned.1.call-start = ((), (), s32[]{:S(2)}) async-start(), calls=%async_computation.5 | async-start | bytes 393216 | tf_op jit(solution)/shard_map/psum | solution.py:16
  999.9 11.9 copy-start.2
  1024.7 155.1 %all-gather.5.cloned.1.call-start = ((), (), s32[]{:S(2)}) async-start(), calls=%async_computation.2 | async-start | bytes 1597440 | tf_op jit(solution)/shard_map/all_gather | solution.py:87
  1062.8 817.3 %all-reduce.12.cloned.1.call-start = ((), (), s32[]{:S(2)}) async-start(), calls=%async_computation.4 | async-start | bytes 3145728
Sparse Core Ops, SparseCore 0:
  27.0 729.3 all-reduce.9
  759.0 37.5 all-reduce.7
  801.5 121.2 all-gather.2
  1024.8 33.9 all-reduce.13
  1062.9 116.7 all-gather.4
  1185.5 694.6 all-reduce.11
where the time goes:
time: 1890 us
  waiting for transfers between devices  1610 us (85%)
  blocking collectives  184 us (10%)
  matrix products  42.5 us (2%)
  local copies, waits for them, and re-layouts  25 us (1%)
  between operations  19.8 us (1%)
    unnamed x8, waiting for transfers between devices  1420 us
    pmax x1, blocking collectives, shards(): bound_max = lax.pmax(local_bound, 'dp')  184 us
    all_gather x1, waiting for transfers between devices, shards(): lax.all_gather(input_cols, 'dp', axis=1, tiled=True)  117 us
    psum x1, waiting for transfers between devices, shards(): summed = lax.psum(partial_rows, 'grp')  38.5 us
  transfers between devices with their start and end apart: 6, of which 5 were waited for; matrix products, arithmetic and copies ran while one was open for 0% of the time, Pallas kernels for 0%

commit v1 on v0

v1 whole, which is shorter than its diff:
```python
import functools
import jax
import jax.numpy as jnp
from jax import lax
from jax.experimental import pallas as pl
from jax.experimental.pallas import tpu as pltpu
from jax.sharding import Mesh
from jax.sharding import PartitionSpec as P

CAP = 2
DAMPING = 0.1
TILE = 128
WIDE = 2 * TILE
X = ("xl", "xh")
XYL = ("xl", "xh", "y", "zl")
Z = ("zh", "zl")
bf16 = jnp.bfloat16
f32 = jnp.float32


def upper(nb):
    return [(i, j) for i in range(nb) for j in range(i, nb)]


def dot(a, b, ca=1, cb=0):
    return lax.dot_general(a, b, (((ca,), (cb,)), ((), ())), preferred_element_type=f32)


def other_layer_kernel(core_ref, act, bg, out, sems):
    copies = []
    for f, src in enumerate((act, bg)):
        copies.append(pltpu.make_async_copy(src.at[1 - core_ref[0]], out.at[f], sems.at[f]))
        copies[f].start()
    for c in copies:
        c.wait()


def factor_kernel(core_ref, act, bg, peer, out, tokens, made, sems):
    tok, feat = act.shape[1:]
    copies = []
    for f, own in enumerate((act, bg)):
        a = pltpu.make_async_copy(own.at[core_ref[0]], tokens.at[f, pl.ds(0, tok)], sems.at[f, 0])
        b = pltpu.make_async_copy(peer.at[f], tokens.at[f, pl.ds(tok, tok)], sems.at[f, 1])
        a.start()
        b.start()
        copies.append((a, b))
    k = 0
    done = []
    for f in range(2):
        for c in copies[f]:
            c.wait()
        for lo in range(0, feat, WIDE):
            r = dot(tokens[f, :, lo : lo + WIDE], tokens[f, :, lo:], 0, 0)
            for top in (0, TILE):
                for left in range(top, feat - lo, TILE):
                    made[k * TILE : (k + 1) * TILE, :] = r[top : top + TILE, left : left + TILE].astype(bf16)
                    k += 1
        part = pl.ds(f * (made.shape[0] // 2), made.shape[0] // 2)
        done.append(pltpu.make_async_copy(made.at[part], out.at[part], sems.at[f, 2]))
        done[f].start()
    for c in done:
        c.wait()


def halves(u):
    hi = u.astype(bf16)
    return jnp.concatenate([hi, (u - hi.astype(f32)).astype(bf16)], axis=0)


def times(two, m):
    r = dot(two, m)
    n = two.shape[0] // 2
    return r[:n] + r[n:]


def chain(u, mats, inv):
    u = 2.0 * u - times(halves(u), mats[0]) * inv
    u = 2.0 * u - times(halves(u), mats[1])
    u = 2.0 * u - times(halves(u), mats[2])
    t = u - times(halves(u), mats[2])
    t = t - times(halves(t), mats[2])
    return (u + t) * inv


def eye_rows(at, count, own, feat):
    r = lax.broadcasted_iota(jnp.int32, (own, feat), 0)
    c = lax.broadcasted_iota(jnp.int32, (own, feat), 1)
    return jnp.where((c == at * count + r) & (r < count), 1.0, 0.0).astype(f32)


def finish_kernel(place, blocks, grads, order, rows_out, pre_out, mats):
    feat = order.shape[0]
    pairs = upper(feat // TILE)

    def put(dst, i, j, block):
        n = block.shape[0]
        dst[i * n : (i + 1) * n, j * n : (j + 1) * n] = block
        if i != j:
            dst[j * n : (j + 1) * n, i * n : (i + 1) * n] = block.T

    def square(src, dst, one, two):
        for i in range(feat // WIDE):
            lo = i * WIDE
            r = dot(src[lo : lo + WIDE, :], src[:, lo:])
            for j in range(i, feat // WIDE):
                old = src[lo : lo + WIDE, j * WIDE : (j + 1) * WIDE].astype(f32)
                new = one * old - two * r[:, (j - i) * WIDE : (j - i + 1) * WIDE]
                put(dst, i, j, new.astype(bf16))

    def matrices(f, mats):
        for n, (i, j) in enumerate(pairs):
            k = f * len(pairs) + n
            put(mats.at[0], i, j, blocks[k * TILE : (k + 1) * TILE, :])
        sums = jnp.sum(jnp.abs(mats[0].astype(f32)), axis=1, keepdims=True)
        inv = 1.0 / jnp.max(sums, axis=0, keepdims=True)
        square(mats.at[0], mats.at[1], 2.0 * inv, inv * inv)
        square(mats.at[1], mats.at[2], 2.0, 1.0)
        return inv

    even, odd = mats.at[0], mats.at[1]
    odd_inv = matrices(1, odd)
    even_inv = matrices(0, even)
    own = rows_out.shape[1]
    eye = eye_rows(place[0], place[2], own, feat)
    rows = chain(jnp.concatenate([eye, eye_rows(place[1], place[2], own, feat)], axis=0), odd, odd_inv)
    rows_out[1] = rows[:own]
    left = dot(halves(rows), order[...]).astype(bf16)
    v = times(left, grads[...])
    both = chain(jnp.concatenate([v, eye], axis=0), even, even_inv)
    pre_out[...] = both[: 2 * own]
    rows_out[0] = both[2 * own :]


def shards(activations, back_grads, grads, owners):
    nxl, ncore, nxh, ny, nzh, nzl = (lax.axis_size(a) for a in ("xl", "core", "xh", "y", "zh", "zl"))
    xl, core, xh, y, zh, zl = (lax.axis_index(a) for a in ("xl", "core", "xh", "y", "zh", "zl"))
    nz = nzh * nzl
    layers, tok, feat = activations.shape
    nb = feat // TILE
    nblk = len(upper(nb))
    nrow = grads.shape[1]
    groups = nxl * ncore
    cols = feat // groups
    total = tok * nxl * ncore * nxh * ny * nz
    group = xl * ncore + core
    dp = (xh * ny + y) * nz + zh * nzl + zl
    params = pltpu.CompilerParams(vmem_limit_bytes=48 << 20)
    sm = pl.BlockSpec(memory_space=pltpu.SMEM)
    vm = pl.BlockSpec(memory_space=pltpu.VMEM)
    anywhere = pl.BlockSpec(memory_space=pl.ANY)

    swap = [(0, 1), (1, 0)]
    send = pl.pallas_call(
        other_layer_kernel,
        out_shape=jax.ShapeDtypeStruct((2, tok, feat), bf16),
        in_specs=[sm, anywhere, anywhere],
        out_specs=vm,
        scratch_shapes=[pltpu.SemaphoreType.DMA((2,))],
        compiler_params=pltpu.CompilerParams(vmem_limit_bytes=60 << 20),
        cost_estimate=pl.CostEstimate(flops=0, bytes_accessed=8 * tok * feat, transcendentals=0),
    )(core.reshape(1), activations, back_grads)
    peer = lax.ppermute(send, "core", swap)
    def along(a, axis):
        size = lax.axis_size(axis)
        return [a] + [lax.ppermute(a, axis, [(i, i ^ e) for i in range(size)]) for e in range(1, size)]

    g = lax.dynamic_index_in_dim(grads, core, 0, keepdims=False).astype(bf16)
    g = along(g, "zh")

    partial = pl.pallas_call(
        factor_kernel,
        out_shape=jax.ShapeDtypeStruct((2 * nblk * TILE, TILE), bf16),
        in_specs=[sm] + [anywhere] * 3,
        out_specs=anywhere,
        scratch_shapes=[
            pltpu.VMEM((2, 2 * tok, feat), bf16),
            pltpu.VMEM((2 * nblk * TILE, TILE), bf16),
            pltpu.SemaphoreType.DMA((2, 3)),
        ],
        compiler_params=pltpu.CompilerParams(vmem_limit_bytes=60 << 20),
        cost_estimate=pl.CostEstimate(flops=4 * tok * 2 * feat * feat, bytes_accessed=8 * tok * feat, transcendentals=0),
    )(core.reshape(1), activations, back_grads, peer)

    share = nxl * nxh * ny * nzl
    rows = 2 * nblk * TILE // share
    partial, g = lax.optimization_barrier((partial, g))
    terms = lax.all_to_all(partial.reshape(share, rows, TILE), XYL, 0, 0, tiled=True)
    g = jnp.stack(g)
    g = [g, lax.ppermute(g, X, [(0, 3), (3, 0), (1, 2), (2, 1)])]
    terms, g = lax.optimization_barrier((terms, g))

    mine = jnp.sum(terms.astype(f32), axis=0).astype(bf16)
    mine = jnp.broadcast_to(mine[None], (nzh, rows, TILE))
    mine, g = lax.optimization_barrier((mine, g))
    stack = lax.all_to_all(mine, "zh", 0, 0, tiled=True)
    g = along(jnp.stack(g), "y")
    stack, g = lax.optimization_barrier((stack, g))
    factor = jnp.sum(stack.astype(f32), axis=0) / float(total)
    at = (((xl * nxh + xh) * ny + y) * nzl + zl) * rows + jnp.arange(rows)
    diagonal = functools.reduce(
        jnp.logical_or, [(at // TILE) % nblk == n for n, (i, j) in enumerate(upper(nb)) if i == j]
    )
    on = diagonal[:, None] & ((at % TILE)[:, None] == jnp.arange(TILE)[None, :])
    damped = (factor + jnp.where(on, DAMPING, 0.0)).astype(bf16)
    blocks = lax.all_to_all(jnp.broadcast_to(damped[None], (share, rows, TILE)), XYL, 0, 0, tiled=True)
    half = feat // nzl
    part = jnp.stack(g).reshape(half, feat)
    k = jnp.arange(half)
    step = k // nrow
    from_zh = (step % nzh) ^ zh
    from_xh = (step // nzh % nxh) ^ xh
    from_y = (step // (nzh * nxh)) ^ y
    to = (((from_xh * ny + from_y) * nzh + from_zh) * nzl + zl) * nrow + k % nrow
    order = (jnp.arange(feat)[:, None] == to[None, :]).astype(bf16)

    own = 16
    inv_rows, pre = pl.pallas_call(
        finish_kernel,
        out_shape=(jax.ShapeDtypeStruct((2, own, feat), f32), jax.ShapeDtypeStruct((2 * own, feat), f32)),
        in_specs=[sm, vm, vm, vm],
        out_specs=(vm, vm),
        scratch_shapes=[pltpu.VMEM((2, 3, feat, feat), bf16)],
        compiler_params=params,
        cost_estimate=pl.CostEstimate(flops=6 * feat**3, bytes_accessed=8 * feat * feat, transcendentals=0),
    )(jnp.stack([dp, dp ^ 1, jnp.int32(nrow)]), blocks.reshape(2 * nblk * TILE, TILE), part, order)
    inv_rows = inv_rows[:, :nrow]

    def columns(rows, of):
        return lax.dynamic_slice_in_dim(rows, (xl * ncore + of) * cols, cols, 1)

    mine, theirs = pre[:nrow], pre[own : own + nrow]
    packed = jnp.concatenate([inv_rows[0], inv_rows[1], columns(mine, 1 - core)], axis=1)
    got = lax.ppermute(packed, "core", swap)
    near = lax.ppermute(columns(theirs, core), "zl", swap)
    cross = lax.ppermute(columns(theirs, 1 - core), ("core", "zl"), [(0, 3), (3, 0), (1, 2), (2, 1)])
    got_rows = jnp.stack([got[:, :feat], got[:, feat : 2 * feat]])
    got_pre = got[:, 2 * feat :] + cross
    mine_pre = columns(mine, core) + near
    first = core == 0
    out = jnp.stack([jnp.where(first, mine_pre, got_pre), jnp.where(first, got_pre, mine_pre)])
    rows_all = jnp.concatenate([jnp.where(first, inv_rows, got_rows), jnp.where(first, got_rows, inv_rows)])
    ids = jnp.arange(2 * layers)
    rank = jnp.sum(((owners[:, None] == owners[None, :]) & (ids[None, :] < ids[:, None])).astype(jnp.int32), axis=1)
    slots = []
    for slot in range(CAP):
        acc = jnp.zeros((nrow, feat), f32)
        for f in range(2 * layers):
            acc = jnp.where((owners[f] == group) & (rank[f] == slot), rows_all[f], acc)
        slots.append(acc)
    return out, jnp.stack(slots)


def solution(mesh):
    split = Mesh(mesh.devices.reshape(2, 2, 2, 4, 4, 2), ("xl", "core", "xh", "y", "zh", "zl"))
    grp, dp = ("xl", "core"), ("xh", "y", "zh", "zl")
    return jax.shard_map(
        shards,
        mesh=split,
        in_specs=(P(None, grp + dp, None), P(None, grp + dp, None), P(None, dp, None), P()),
        out_specs=(P(None, dp, grp), P(grp, dp, None)),
        check_vma=False,
    )
```

time: 1890 us -> 107 us (0.06)
  the two profiles are of different devices: /device:TPU:2 before, /device:TPU:1 now
where the time goes in v1:
time: 107 us; the launch traced here: 106 us
  starting transfers between devices  38.7 us (36%)
  waiting for transfers between devices  38 us (36%)
  Pallas kernels  13.3 us (12%)
  between operations  8.22 us (8%)
  local copies, waits for them, and re-layouts  6.1 us (6%)
  other arithmetic  2.14 us (2%)
    ppermute x1, waiting for transfers between devices, shards(): g = [g, lax.ppermute(g, X, [(0, 3), (3, 0), (1, 2), (2, 1)])]  17.3 us
    ppermute x6, starting transfers between devices, along(): lax.ppermute(a, axis, [(i, i ^ e) for i in range(size)])  10.4 us
    all_to_all x1, waiting for transfers between devices, shards(): lax.all_to_all(jnp.broadcast_to(damped[None], (share, rows, TILE)), XYL,...  9.75 us
    ppermute x6, waiting for transfers between devices, along(): lax.ppermute(a, axis, [(i, i ^ e) for i in range(size)])  9.41 us
    all_to_all x1, starting transfers between devices, shards(): lax.all_to_all(partial.reshape(share, rows, TILE), XYL, 0, 0, tiled=True)  7.5 us
    pallas_call x1, Pallas kernels, shards(): pl.pallas_call(finish_kernel, out_shape=(jax.ShapeDtypeStruct((2, own, fe...  6.41 us
    all_to_all x1, starting transfers between devices, shards(): stack = lax.all_to_all(mine, 'zh', 0, 0, tiled=True)  5.89 us
    all_to_all x1, starting transfers between devices, shards(): lax.all_to_all(jnp.broadcast_to(damped[None], (share, rows, TILE)), XYL,...  4.32 us
  transfers between devices with their start and end apart: 14, of which 7 were waited for; matrix products, arithmetic and copies ran while one was open for 4% of the time, Pallas kernels for 4%

profile of v1, /device:TPU:1, one launch (start us, length us, event | category | flops | bytes accessed | tf_op | source)
XLA Modules:
  0.0 106.4 jit_solution(18293794452456546755)
XLA Ops:
  0.6 0.0 copy-start
  0.7 2.6 %shard_map.59 = bf16[2,512,768]{2,1,0:T(8,128)(2,1)} custom-call(s32[1]{0:T(128)} %bitcast.2.core_ref, bf16[2,512,768]{2,1,0:T(8,128)(2,1)} %act.3, bf16[2,512,768]{2,1,0:T(8,128)(2,1)} %bg.3), custom_call_target="tpu_custom_call" | custom-call | bytes 3145728 | tf_op jit(solution)/shard_map/pallas_call | solution.py:153
  3.2 3.3 %collective-permute-start = (bf16[2,512,768]{2,1,0:T(8,128)(2,1)}, bf16[2,512,768]{2,1,0:T(8,128)(2,1)S(1)}, u32[]{:S(2)}, u32[]{:S(2)}) collective-permute-start(bf16[2,512,768]{2,1,0:T(8,128)(2,1)} %shard_map.59), channel_id=1, source_target_pairs={{0,64},{64,0},{1,65},{65,1},{2,66},{66,2},{3,67},{67,3},{4,68},{68... | collective-permute-start | bytes 4718600 | tf_op jit(solution)/shard_map/ppermute | solution.py:162
  6.6 1.3 %collective-permute-start.1 = (bf16[12,768]{1,0:T(8,128)(2,1)S(1)}, bf16[12,768]{1,0:T(8,128)(2,1)S(1)}, u32[]{:S(2)}, u32[]{:S(2)}) collective-permute-start(bf16[12,768]{1,0:T(8,128)(2,1)S(1)} %bitcast.49), channel_id=1, source_target_pairs={{0,2},{2,0},{4,6},{6,4},{1,3},{3,1},{5,7},{7,5},{8,10},{10,8},{12,... | collective-permute-start | bytes 55304 | tf_op jit(solution)/shard_map/ppermute | solution.py:165
  8.0 5.1 %collective-permute-start.2 = (bf16[12,768]{1,0:T(8,128)(2,1)S(1)}, bf16[12,768]{1,0:T(8,128)(2,1)S(1)}, u32[]{:S(2)}, u32[]{:S(2)}) collective-permute-start(bf16[12,768]{1,0:T(8,128)(2,1)S(1)} %bitcast.50), channel_id=1, source_target_pairs={{0,4},{2,6},{4,0},{6,2},{1,5},{3,7},{5,1},{7,3},{8,12},{10,14},{12... | collective-permute-start | bytes 55304 | tf_op jit(solution)/shard_map/ppermute | solution.py:165
  13.1 0.0 collective-permute-start.3
  13.1 0.0 collective-permute-done.peer
  13.1 1.2 %copy-done.3 = bf16[2,512,768]{2,1,0:T(8,128)(2,1)} copy-done((bf16[2,512,768]{2,1,0:T(8,128)(2,1)}, bf16[2,512,768]{2,1,0:T(8,128)(2,1)S(1)}, u32[]{:S(2)}) %copy-start.3) | copy-done | bytes 1572888
  14.3 4.3 %shard_map.60 = bf16[5376,128]{1,0:T(8,128)(2,1)} custom-call(s32[1]{0:T(128)} %bitcast.2.core_ref, bf16[2,512,768]{2,1,0:T(8,128)(2,1)} %act.3, bf16[2,512,768]{2,1,0:T(8,128)(2,1)} %bg.3, bf16[2,512,768]{2,1,0:T(8,128)(2,1)} %copy-done.3), custom_call_target="tpu_custom_call" | custom-call | flops 2415919104 | bytes 3145728 | tf_op jit(solution)/shard_map/pallas_call | solution.py:170
  18.6 0.0 collective-permute-done.1
  18.6 0.0 collective-permute-done.3
  18.6 7.5 %all-to-all-start = ((bf16[32,168,128]{2,1,0:T(8,128)(2,1)}), bf16[32,168,128]{2,1,0:T(8,128)(2,1)S(1)}, u32[]{:S(2)}, u32[]{:S(2)}) async-start(bf16[32,168,128]{2,1,0:T(8,128)(2,1)} %bitcast.43), calls=%async_computation | async-start | bytes 2752512 | tf_op jit(solution)/shard_map/all_to_all | solution.py:187
  26.1 2.6 %collective-permute-start.4 = (bf16[4,12,768]{2,1,0:T(8,128)(2,1)S(1)}, bf16[4,12,768]{2,1,0:T(8,128)(2,1)S(1)}, u32[]{:S(2)}, u32[]{:S(2)}) collective-permute-start(bf16[4,12,768]{2,1,0:T(8,128)(2,1)S(1)} %pad_maximum_fusion.3), channel_id=1, source_target_pairs={{0,160},{160,0},{32,128},{128,32},{1,161},{161,1},{33,129},{129,33... | collective-permute-start | bytes 221192 | tf_op jit(solution)/shard_map/ppermute | solution.py:189
  28.7 17.3 %collective-permute-done.4 = bf16[4,12,768]{2,1,0:T(8,128)(2,1)S(1)} collective-permute-done((bf16[4,12,768]{2,1,0:T(8,128)(2,1)S(1)}, bf16[4,12,768]{2,1,0:T(8,128)(2,1)S(1)}, u32[]{:S(2)}, u32[]{:S(2)}) %collective-permute-start.4) | collective-permute-done | bytes 73760 | tf_op jit(solution)/shard_map/ppermute | solution.py:189
  46.0 0.5 all-to-all-done
  46.5 0.2 reduce_sum.30
  46.7 0.7 broadcast_in_dim.12
  47.4 5.9 %all-to-all-start.1 = ((bf16[4,168,128]{2,1,0:T(8,128)(2,1)}), bf16[4,168,128]{2,1,0:T(8,128)(2,1)S(1)}, u32[]{:S(2)}, u32[]{:S(2)}) async-start(bf16[4,168,128]{2,1,0:T(8,128)(2,1)} %broadcast_in_dim.12), calls=%async_computation.1 | async-start | bytes 344064 | tf_op jit(solution)/shard_map/all_to_all | solution.py:195
  53.3 0.9 collective-permute-start.5
  54.2 2.0 %collective-permute-start.6 = (bf16[2,4,12,768]{3,2,1,0:T(8,128)(2,1)S(1)}, bf16[2,4,12,768]{3,2,1,0:T(8,128)(2,1)S(1)}, u32[]{:S(2)}, u32[]{:S(2)}) collective-permute-start(bf16[2,4,12,768]{3,2,1,0:T(8,128)(2,1)S(1)} %pad_maximum_fusion.1), channel_id=1, source_target_pairs={{0,16},{8,24},{16,0},{24,8},{1,17},{9,25},{17,1},{25,9},{2,18},{10... | collective-permute-start | bytes 442376 | tf_op jit(solution)/shard_map/ppermute | solution.py:165
  56.2 1.1 %collective-permute-start.7 = (bf16[2,4,12,768]{3,2,1,0:T(8,128)(2,1)S(1)}, bf16[2,4,12,768]{3,2,1,0:T(8,128)(2,1)S(1)}, u32[]{:S(2)}, u32[]{:S(2)}) collective-permute-start(bf16[2,4,12,768]{3,2,1,0:T(8,128)(2,1)S(1)} %pad_maximum_fusion.1), channel_id=1, source_target_pairs={{0,24},{8,16},{16,8},{24,0},{1,25},{9,17},{17,9},{25,1},{2,26},{10... | collective-permute-start | bytes 442376 | tf_op jit(solution)/shard_map/ppermute | solution.py:165
  57.3 0.6 collective-permute-done.5
  57.9 5.6 %collective-permute-done.6 = bf16[2,4,12,768]{3,2,1,0:T(8,128)(2,1)S(1)} collective-permute-done((bf16[2,4,12,768]{3,2,1,0:T(8,128)(2,1)S(1)}, bf16[2,4,12,768]{3,2,1,0:T(8,128)(2,1)S(1)}, u32[]{:S(2)}, u32[]{:S(2)}) %collective-permute-start.6) | collective-permute-done | bytes 147488 | tf_op jit(solution)/shard_map/ppermute | solution.py:165
  63.5 3.2 %collective-permute-done.7 = bf16[2,4,12,768]{3,2,1,0:T(8,128)(2,1)S(1)} collective-permute-done((bf16[2,4,12,768]{3,2,1,0:T(8,128)(2,1)S(1)}, bf16[2,4,12,768]{3,2,1,0:T(8,128)(2,1)S(1)}, u32[]{:S(2)}, u32[]{:S(2)}) %collective-permute-start.7) | collective-permute-done | bytes 147488 | tf_op jit(solution)/shard_map/ppermute | solution.py:165
  66.7 0.0 all-to-all-done.1
  66.7 0.1 add_convert_fusion
  66.8 1.3 %broadcast_in_dim.15 = bf16[32,168,128]{2,1,0:T(8,128)(2,1)} broadcast(bf16[168,128]{1,0:T(8,128)(2,1)S(1)} %add_convert_fusion), dimensions={1,2} | broadcast | bytes 1419264 | tf_op jit(solution)/shard_map/broadcast_in_dim | solution.py:205
  68.1 4.3 %all-to-all-start.2 = ((bf16[32,168,128]{2,1,0:T(8,128)(2,1)}), bf16[32,168,128]{2,1,0:T(8,128)(2,1)S(1)}, u32[]{:S(2)}, u32[]{:S(2)}) async-start(bf16[32,168,128]{2,1,0:T(8,128)(2,1)} %broadcast_in_dim.15), calls=%async_computation.2 | async-start | bytes 2752512 | tf_op jit(solution)/shard_map/all_to_all | solution.py:205
  72.5 0.2 convert_reduce_fusion.1
  72.6 0.7 fusion.26
  78.2 0.6 fusion.27
  81.3 0.1 pad_add_fusion.place
  81.4 0.2 fusion.order
  81.6 1.1 %pad_maximum_fusion = bf16[4,2,4,12,768]{4,3,2,1,0:T(8,128)(2,1)S(1)} fusion(bf16[1,2,4,12,768]{4,3,2,1,0:T(8,128)(2,1)} %bitcast.48, bf16[1,2,4,12,768]{4,3,2,1,0:T(8,128)(2,1)S(1)} %bitcast.47, bf16[1,2,4,12,768]{4,3,2,1,0:T(8,128)(2,1)S(1)} %bitcast.46, bf16[1,2,4,12,768]{4,3,2,1,0:T(8,128)(2,1)S(1)} %bitcast.44), kind=kLoop, calls=%fused_computation.2 | loop fusion | flops 884736 | bytes 1179648 | tf_op jit(solution)/shard_map/stack | solution.py:207
  82.7 0.1 reshape.202.grads
  82.8 9.7 %all-to-all-done.2 = bf16[32,168,128]{2,1,0:T(8,128)(2,1)S(1)} async-done(((bf16[32,168,128]{2,1,0:T(8,128)(2,1)}), bf16[32,168,128]{2,1,0:T(8,128)(2,1)S(1)}, u32[]{:S(2)}, u32[]{:S(2)}) %all-to-all-start.2) | async-done | bytes 1376288 | tf_op jit(solution)/shard_map/all_to_all | solution.py:205
  92.6 6.4 %shard_map.61 = (f32[2,16,768]{2,1,0:T(8,128)S(1)}, f32[32,768]{1,0:T(8,128)S(1)}) custom-call(s32[3]{0:T(128)S(1)} %pad_add_fusion.place, bf16[5376,128]{1,0:T(8,128)(2,1)S(1)} %bitcast.42, bf16[384,768]{1,0:T(8,128)(2,1)S(1)} %reshape.202.grads, bf16[768,384]{1,0:T(8,128)(2,1)S(1)} %fusion.order), custom_call_target="tpu_custom_call" | custom-call | flops 2717908992 | bytes 4718592 | tf_op jit(solution)/shard_map/pallas_call | solution.py:217
  99.0 0.1 constant_dynamic-slice_fusion.1
  99.1 3.3 %collective-permute-start.9 = (f32[12,1728]{1,0:T(8,128)S(1)}, f32[12,1728]{1,0:T(8,128)S(1)}, u32[]{:S(2)}, u32[]{:S(2)}) collective-permute-start(f32[12,1728]{1,0:T(8,128)S(1)} %pad_maximum_fusion.2), channel_id=1, source_target_pairs={{0,64},{64,0},{1,65},{65,1},{2,66},{66,2},{3,67},{67,3},{4,68},{68... | collective-permute-start | bytes 248840 | tf_op jit(solution)/shard_map/ppermute | solution.py:233
  102.4 0.1 constant_dynamic-slice_fusion.2
  102.5 0.0 collective-permute-start.10
  102.6 1.4 %collective-permute-start.8 = (f32[12,192]{1,0:T(8,128)S(1)}, f32[12,192]{1,0:T(8,128)S(1)}, u32[]{:S(2)}, u32[]{:S(2)}) collective-permute-start(f32[12,192]{1,0:T(8,128)S(1)} %get-tuple-element.56), channel_id=1, source_target_pairs={{0,1},{1,0},{2,3},{3,2},{4,5},{5,4},{6,7},{7,6},{8,9},{9,8},{10,11... | collective-permute-start | bytes 27656 | tf_op jit(solution)/shard_map/ppermute | solution.py:234
  103.9 0.0 collective-permute-done.9
  104.0 0.7 copy.13
  104.7 1.0 collective-permute-done.10
  105.7 0.0 collective-permute-done.8
  105.7 0.1 select_bitcast_fusion.1
  105.8 0.6 copy.12
  (23 shorter events, 0.3 us)
Async XLA Ops:
  0.6 5.9 %copy-start = (f32[2,12,768]{2,0,1:T(2,128)S(1)}, f32[2,12,768]{2,0,1:T(2,128)}, u32[]{:S(2)}) copy-start(f32[2,12,768]{2,0,1:T(2,128)} %param.6) | copy-start | bytes 221188
  3.2 9.8 %collective-permute-start = (bf16[2,512,768]{2,1,0:T(8,128)(2,1)}, bf16[2,512,768]{2,1,0:T(8,128)(2,1)S(1)}, u32[]{:S(2)}, u32[]{:S(2)}) collective-permute-start(bf16[2,512,768]{2,1,0:T(8,128)(2,1)} %shard_map.59), channel_id=1, source_target_pairs={{0,64},{64,0},{1,65},{65,1},{2,66},{66,2},{3,67},{67,3},{4,68},{68... | collective-permute-start | bytes 4718600 | tf_op jit(solution)/shard_map/ppermute | solution.py:162
  6.6 11.9 %collective-permute-start.1 = (bf16[12,768]{1,0:T(8,128)(2,1)S(1)}, bf16[12,768]{1,0:T(8,128)(2,1)S(1)}, u32[]{:S(2)}, u32[]{:S(2)}) collective-permute-start(bf16[12,768]{1,0:T(8,128)(2,1)S(1)} %bitcast.49), channel_id=1, source_target_pairs={{0,2},{2,0},{4,6},{6,4},{1,3},{3,1},{5,7},{7,5},{8,10},{10,8},{12,... | collective-permute-start | bytes 55304 | tf_op jit(solution)/shard_map/ppermute | solution.py:165
  8.0 10.6 %collective-permute-start.2 = (bf16[12,768]{1,0:T(8,128)(2,1)S(1)}, bf16[12,768]{1,0:T(8,128)(2,1)S(1)}, u32[]{:S(2)}, u32[]{:S(2)}) collective-permute-start(bf16[12,768]{1,0:T(8,128)(2,1)S(1)} %bitcast.50), channel_id=1, source_target_pairs={{0,4},{2,6},{4,0},{6,2},{1,5},{3,7},{5,1},{7,3},{8,12},{10,14},{12... | collective-permute-start | bytes 55304 | tf_op jit(solution)/shard_map/ppermute | solution.py:165
  13.1 5.5 %collective-permute-start.3 = (bf16[12,768]{1,0:T(8,128)(2,1)S(1)}, bf16[12,768]{1,0:T(8,128)(2,1)S(1)}, u32[]{:S(2)}, u32[]{:S(2)}) collective-permute-start(bf16[12,768]{1,0:T(8,128)(2,1)S(1)} %bitcast.51), channel_id=1, source_target_pairs={{0,6},{2,4},{4,2},{6,0},{1,7},{3,5},{5,3},{7,1},{8,14},{10,12},{12... | collective-permute-start | bytes 55304 | tf_op jit(solution)/shard_map/ppermute | solution.py:165
  13.1 1.2 %copy-start.3 = (bf16[2,512,768]{2,1,0:T(8,128)(2,1)}, bf16[2,512,768]{2,1,0:T(8,128)(2,1)S(1)}, u32[]{:S(2)}) copy-start(bf16[2,512,768]{2,1,0:T(8,128)(2,1)S(1)} %collective-permute-done.peer) | copy-start | bytes 4718596
  18.6 27.9 %all-to-all-start = ((bf16[32,168,128]{2,1,0:T(8,128)(2,1)}), bf16[32,168,128]{2,1,0:T(8,128)(2,1)S(1)}, u32[]{:S(2)}, u32[]{:S(2)}) async-start(bf16[32,168,128]{2,1,0:T(8,128)(2,1)} %bitcast.43), calls=%async_computation | async-start | bytes 2752512 | tf_op jit(solution)/shard_map/all_to_all | solution.py:187
  26.1 19.9 %collective-permute-start.4 = (bf16[4,12,768]{2,1,0:T(8,128)(2,1)S(1)}, bf16[4,12,768]{2,1,0:T(8,128)(2,1)S(1)}, u32[]{:S(2)}, u32[]{:S(2)}) collective-permute-start(bf16[4,12,768]{2,1,0:T(8,128)(2,1)S(1)} %pad_maximum_fusion.3), channel_id=1, source_target_pairs={{0,160},{160,0},{32,128},{128,32},{1,161},{161,1},{33,129},{129,33... | collective-permute-start | bytes 221192 | tf_op jit(solution)/shard_map/ppermute | solution.py:189
  47.4 19.3 %all-to-all-start.1 = ((bf16[4,168,128]{2,1,0:T(8,128)(2,1)}), bf16[4,168,128]{2,1,0:T(8,128)(2,1)S(1)}, u32[]{:S(2)}, u32[]{:S(2)}) async-start(bf16[4,168,128]{2,1,0:T(8,128)(2,1)} %broadcast_in_dim.12), calls=%async_computation.1 | async-start | bytes 344064 | tf_op jit(solution)/shard_map/all_to_all | solution.py:195
  53.3 4.6 %collective-permute-start.5 = (bf16[2,4,12,768]{3,2,1,0:T(8,128)(2,1)S(1)}, bf16[2,4,12,768]{3,2,1,0:T(8,128)(2,1)S(1)}, u32[]{:S(2)}, u32[]{:S(2)}) collective-permute-start(bf16[2,4,12,768]{3,2,1,0:T(8,128)(2,1)S(1)} %pad_maximum_fusion.1), channel_id=1, source_target_pairs={{0,8},{8,0},{16,24},{24,16},{1,9},{9,1},{17,25},{25,17},{2,10},{10... | collective-permute-start | bytes 442376 | tf_op jit(solution)/shard_map/ppermute | solution.py:165
  54.2 9.3 %collective-permute-start.6 = (bf16[2,4,12,768]{3,2,1,0:T(8,128)(2,1)S(1)}, bf16[2,4,12,768]{3,2,1,0:T(8,128)(2,1)S(1)}, u32[]{:S(2)}, u32[]{:S(2)}) collective-permute-start(bf16[2,4,12,768]{3,2,1,0:T(8,128)(2,1)S(1)} %pad_maximum_fusion.1), channel_id=1, source_target_pairs={{0,16},{8,24},{16,0},{24,8},{1,17},{9,25},{17,1},{25,9},{2,18},{10... | collective-permute-start | bytes 442376 | tf_op jit(solution)/shard_map/ppermute | solution.py:165
  56.2 10.5 %collective-permute-start.7 = (bf16[2,4,12,768]{3,2,1,0:T(8,128)(2,1)S(1)}, bf16[2,4,12,768]{3,2,1,0:T(8,128)(2,1)S(1)}, u32[]{:S(2)}, u32[]{:S(2)}) collective-permute-start(bf16[2,4,12,768]{3,2,1,0:T(8,128)(2,1)S(1)} %pad_maximum_fusion.1), channel_id=1, source_target_pairs={{0,24},{8,16},{16,8},{24,0},{1,25},{9,17},{17,9},{25,1},{2,26},{10... | collective-permute-start | bytes 442376 | tf_op jit(solution)/shard_map/ppermute | solution.py:165
  66.7 1.4 %copy-start.1 = (bf16[2,4,12,768]{3,2,1,0:T(8,128)(2,1)}, bf16[2,4,12,768]{3,2,1,0:T(8,128)(2,1)S(1)}, u32[]{:S(2)}) copy-start(bf16[2,4,12,768]{3,2,1,0:T(8,128)(2,1)S(1)} %collective-permute-done.7) | copy-start | bytes 442372
  68.1 4.3 %copy-start.2 = (s32[4]{0:T(128)S(1)}, s32[4]{0:T(128)}, u32[]{:S(2)}) copy-start(s32[4]{0:T(128)} %param.7) | copy-start | bytes 52
  68.1 24.5 %all-to-all-start.2 = ((bf16[32,168,128]{2,1,0:T(8,128)(2,1)}), bf16[32,168,128]{2,1,0:T(8,128)(2,1)S(1)}, u32[]{:S(2)}, u32[]{:S(2)}) async-start(bf16[32,168,128]{2,1,0:T(8,128)(2,1)} %broadcast_in_dim.15), calls=%async_computation.2 | async-start | bytes 2752512 | tf_op jit(solution)/shard_map/all_to_all | solution.py:205
  99.1 4.8 %collective-permute-start.9 = (f32[12,1728]{1,0:T(8,128)S(1)}, f32[12,1728]{1,0:T(8,128)S(1)}, u32[]{:S(2)}, u32[]{:S(2)}) collective-permute-start(f32[12,1728]{1,0:T(8,128)S(1)} %pad_maximum_fusion.2), channel_id=1, source_target_pairs={{0,64},{64,0},{1,65},{65,1},{2,66},{66,2},{3,67},{67,3},{4,68},{68... | collective-permute-start | bytes 248840 | tf_op jit(solution)/shard_map/ppermute | solution.py:233
  102.5 3.2 %collective-permute-start.10 = (f32[12,192]{1,0:T(8,128)S(1)}, f32[12,192]{1,0:T(8,128)S(1)}, u32[]{:S(2)}, u32[]{:S(2)}) collective-permute-start(f32[12,192]{1,0:T(8,128)S(1)} %get-tuple-element.57), channel_id=1, source_target_pairs={{0,65},{65,0},{1,64},{64,1},{2,67},{67,2},{3,66},{66,3},{4,69},{69... | collective-permute-start | bytes 27656 | tf_op jit(solution)/shard_map/ppermute | solution.py:235
  102.6 3.2 %collective-permute-start.8 = (f32[12,192]{1,0:T(8,128)S(1)}, f32[12,192]{1,0:T(8,128)S(1)}, u32[]{:S(2)}, u32[]{:S(2)}) collective-permute-start(f32[12,192]{1,0:T(8,128)S(1)} %get-tuple-element.56), channel_id=1, source_target_pairs={{0,1},{1,0},{2,3},{3,2},{4,5},{5,4},{6,7},{7,6},{8,9},{9,8},{10,11... | collective-permute-start | bytes 27656 | tf_op jit(solution)/shard_map/ppermute | solution.py:234

commit v2 on v1

v2 whole, which is shorter than its diff:
```python
import functools
import jax
import jax.numpy as jnp
from jax import lax
from jax.experimental import pallas as pl
from jax.experimental.pallas import tpu as pltpu
from jax.sharding import Mesh
from jax.sharding import PartitionSpec as P

CAP = 2
DAMPING = 0.1
TILE = 128
WIDE = 2 * TILE
X = ("xl", "xh")
XYL = ("xl", "xh", "y", "zl")
Z = ("zh", "zl")
bf16 = jnp.bfloat16
f32 = jnp.float32


def upper(nb):
    return [(i, j) for i in range(nb) for j in range(i, nb)][:-1]


def dot(a, b, ca=1, cb=0):
    return lax.dot_general(a, b, (((ca,), (cb,)), ((), ())), preferred_element_type=f32)


def factor_kernel(core_ref, act, bg, peer_act, peer_bg, out, tokens, made, sems):
    tok, feat = act.shape[1:]
    copies = []
    for f, (own, peer) in enumerate(((act, peer_act), (bg, peer_bg))):
        a = pltpu.make_async_copy(own.at[core_ref[0]], tokens.at[f, pl.ds(0, tok)], sems.at[f, 0])
        b = pltpu.make_async_copy(peer.at[core_ref[0]], tokens.at[f, pl.ds(tok, tok)], sems.at[f, 1])
        a.start()
        b.start()
        copies.append((a, b))
    pairs = upper(feat // TILE)
    mid = TILE // 2
    done = []
    for f in range(2):
        for c in copies[f]:
            c.wait()
        for lo in range(0, feat, WIDE):
            r = dot(tokens[f, :, lo : lo + WIDE], tokens[f, :, lo:], 0, 0)
            for top in (0, TILE):
                for left in range(top, feat - lo, TILE):
                    at = (lo + top) // TILE, (lo + left) // TILE
                    block = r[top : top + TILE, left : left + TILE].astype(bf16)
                    if at in pairs:
                        k = f * len(pairs) + pairs.index(at)
                        made[k * TILE : (k + 1) * TILE, :] = block
        for n, quarter in enumerate((block[:mid, :mid], block[mid:, mid:], block[:mid, mid:])):
            k = f * len(pairs) + pairs.index((n, n))
            made[k * TILE + mid : (k + 1) * TILE, :mid] = quarter
        part = pl.ds(f * (made.shape[0] // 2), made.shape[0] // 2)
        done.append(pltpu.make_async_copy(made.at[part], out.at[part], sems.at[f, 2]))
        done[f].start()
    for c in done:
        c.wait()


def halves(u):
    hi = u.astype(bf16)
    return jnp.concatenate([hi, (u - hi.astype(f32)).astype(bf16)], axis=0)


def times(two, m):
    r = dot(two, m)
    n = two.shape[0] // 2
    return r[:n] + r[n:]


def chain(u, mats, inv):
    u = 2.0 * u - times(halves(u), mats[0]) * inv
    u = 2.0 * u - times(halves(u), mats[1])
    u = 2.0 * u - times(halves(u), mats[2])
    t = u - times(halves(u), mats[2])
    t = t - times(halves(t), mats[2])
    return (u + t) * inv


def eye_rows(at, count, own, feat):
    r = lax.broadcasted_iota(jnp.int32, (own, feat), 0)
    c = lax.broadcasted_iota(jnp.int32, (own, feat), 1)
    return jnp.where((c == at * count + r) & (r < count), 1.0, 0.0).astype(f32)


def finish_kernel(place, blocks, grads, order, packed, mine_out, near_out, cross_out, mats):
    feat = order.shape[0]
    pairs = upper(feat // TILE)
    mid = TILE // 2

    def put(dst, i, j, block):
        n = block.shape[0]
        dst[i * n : (i + 1) * n, j * n : (j + 1) * n] = block
        if i != j:
            dst[j * n : (j + 1) * n, i * n : (i + 1) * n] = block.T

    def square(src, dst, one, two):
        for i in range(feat // WIDE):
            lo = i * WIDE
            r = dot(src[lo : lo + WIDE, :], src[:, lo:])
            for j in range(i, feat // WIDE):
                old = src[lo : lo + WIDE, j * WIDE : (j + 1) * WIDE].astype(f32)
                new = one * old - two * r[:, (j - i) * WIDE : (j - i + 1) * WIDE]
                put(dst, i, j, new.astype(bf16))

    def matrices(f, mats):
        corner = []
        for n, (i, j) in enumerate(pairs):
            k = f * len(pairs) + n
            block = blocks[k * TILE : (k + 1) * TILE, :]
            if i == j and i < 3:
                up = block[:mid, mid:]
                corner.append(block[mid:, :mid])
                low = jnp.concatenate([up.T, block[mid:, mid:]], axis=1)
                block = jnp.concatenate([block[:mid], low], axis=0)
            put(mats.at[0], i, j, block)
        first, last, up = corner
        low = jnp.concatenate([up.T, last], axis=1)
        block = jnp.concatenate([jnp.concatenate([first, up], axis=1), low], axis=0)
        put(mats.at[0], feat // TILE - 1, feat // TILE - 1, block)
        sums = jnp.sum(jnp.abs(mats[0].astype(f32)), axis=1, keepdims=True)
        inv = 1.0 / jnp.max(sums, axis=0, keepdims=True)
        square(mats.at[0], mats.at[1], 2.0 * inv, inv * inv)
        square(mats.at[1], mats.at[2], 2.0, 1.0)
        return inv

    even, odd = mats.at[0], mats.at[1]
    odd_inv = matrices(1, odd)
    own = packed.shape[0]
    cols = mine_out.shape[1]
    eye = eye_rows(place[0], place[2], own, feat)
    rows = chain(jnp.concatenate([eye, eye_rows(place[1], place[2], own, feat)], axis=0), odd, odd_inv)
    packed[:, feat : 2 * feat] = rows[:own]
    even_inv = matrices(0, even)
    left = dot(halves(rows), order[...]).astype(bf16)
    v = times(left, grads[...])
    both = chain(jnp.concatenate([v, eye], axis=0), even, even_inv)
    packed[:, :feat] = both[2 * own :]

    def columns(group):
        out = both[: 2 * own, :cols]
        for n in range(1, feat // cols):
            out = jnp.where(group == n, both[: 2 * own, n * cols : (n + 1) * cols], out)
        return out

    here, there = columns(place[3]), columns(place[4])
    mine_out[...] = here[:own]
    near_out[...] = here[own:]
    cross_out[...] = there[own:]
    packed[:, 2 * feat :] = there[:own]


def output_kernel(owners, place, packed, got, mine, near, cross, result, store):
    nrow, slots, feat = store.shape
    first = place[5] == 0
    own = mine[:nrow] + near[:nrow]
    other = got[:nrow, 2 * feat :] + cross[:nrow]
    result[:, 0, :] = jnp.where(first, own, other)
    result[:, 1, :] = jnp.where(first, other, own)
    rows = []
    for l in range(2):
        for i in range(2):
            a, b = (packed, got) if l == 0 else (got, packed)
            part = slice(i * feat, (i + 1) * feat)
            rows.append(jnp.where(first, a[:nrow, part], b[:nrow, part]))
    for slot in range(slots):
        acc = jnp.zeros((nrow, feat), f32)
        for f, block in enumerate(rows):
            rank = sum(((owners[e] == owners[f]).astype(jnp.int32) for e in range(f)), jnp.int32(0))
            acc = jnp.where((owners[f] == place[3]) & (rank == slot), block, acc)
        store[:, slot, :] = acc


def shards(activations, back_grads, grads, owners):
    nxl, ncore, nxh, ny, nzh, nzl = (lax.axis_size(a) for a in ("xl", "core", "xh", "y", "zh", "zl"))
    xl, core, xh, y, zh, zl = (lax.axis_index(a) for a in ("xl", "core", "xh", "y", "zh", "zl"))
    nz = nzh * nzl
    layers, tok, feat = activations.shape
    nb = feat // TILE
    nblk = len(upper(nb))
    nrow = grads.shape[1]
    groups = nxl * ncore
    cols = feat // groups
    total = tok * nxl * ncore * nxh * ny * nz
    group = xl * ncore + core
    dp = (xh * ny + y) * nz + zh * nzl + zl
    params = pltpu.CompilerParams(vmem_limit_bytes=48 << 20)
    sm = pl.BlockSpec(memory_space=pltpu.SMEM)
    vm = pl.BlockSpec(memory_space=pltpu.VMEM)
    anywhere = pl.BlockSpec(memory_space=pl.ANY)

    swap = [(0, 1), (1, 0)]
    peer = [lax.ppermute(a, "core", swap) for a in (activations, back_grads)]
    def along(a, axis):
        size = lax.axis_size(axis)
        return [a] + [lax.ppermute(a, axis, [(i, i ^ e) for i in range(size)]) for e in range(1, size)]

    g = lax.dynamic_index_in_dim(grads, core, 0, keepdims=False).astype(bf16)
    g = along(g, "zh")

    partial = pl.pallas_call(
        factor_kernel,
        out_shape=jax.ShapeDtypeStruct((2 * nblk * TILE, TILE), bf16),
        in_specs=[sm] + [anywhere] * 4,
        out_specs=anywhere,
        scratch_shapes=[
            pltpu.VMEM((2, 2 * tok, feat), bf16),
            pltpu.VMEM((2 * nblk * TILE, TILE), bf16),
            pltpu.SemaphoreType.DMA((2, 3)),
        ],
        compiler_params=pltpu.CompilerParams(vmem_limit_bytes=60 << 20),
        cost_estimate=pl.CostEstimate(flops=4 * tok * 2 * feat * feat, bytes_accessed=8 * tok * feat, transcendentals=0),
    )(core.reshape(1), activations, back_grads, *peer)

    share = nxl * nxh * ny * nzl
    rows = 2 * nblk * TILE // share
    partial, g = lax.optimization_barrier((partial, g))
    terms = lax.all_to_all(partial.reshape(share, rows, TILE), XYL, 0, 0, tiled=True)
    g = along(jnp.stack(g), "y")
    terms, g = lax.optimization_barrier((terms, g))

    mine = jnp.sum(terms.astype(f32), axis=0).astype(bf16)
    mine, g = lax.optimization_barrier((mine, g))
    stack = along(mine, "zh")
    g = jnp.stack(g)
    g = [g, lax.ppermute(g, X, [(0, 3), (3, 0), (1, 2), (2, 1)])]
    stack, g = lax.optimization_barrier((stack, g))
    pair = [a.astype(f32) + b.astype(f32) for a, b in zip(stack[0::2], stack[1::2])]
    factor = (pair[0] + pair[1]) / float(total)
    at = (((xl * nxh + xh) * ny + y) * nzl + zl) * rows + jnp.arange(rows)
    pairs = upper(nb)

    def within(blocks):
        return functools.reduce(jnp.logical_or, [(at // TILE) % nblk == pairs.index((n, n)) for n in blocks])

    spot = jnp.arange(TILE)[None, :]
    on = within(range(nb - 1))[:, None] & ((at % TILE)[:, None] == spot)
    on |= within((0, 1))[:, None] & ((at % TILE - TILE // 2)[:, None] == spot)
    damped = (factor + jnp.where(on, DAMPING, 0.0)).astype(bf16)
    blocks = lax.all_to_all(jnp.broadcast_to(damped[None], (share, rows, TILE)), XYL, 0, 0, tiled=True)
    half = feat // nzl
    part = jnp.stack(g).reshape(half, feat)
    k = jnp.arange(half)
    step = k // nrow
    from_zh = (step % nzh) ^ zh
    from_y = (step // nzh % ny) ^ y
    from_xh = (step // (nzh * ny)) ^ xh
    to = (((from_xh * ny + from_y) * nzh + from_zh) * nzl + zl) * nrow + k % nrow
    order = (jnp.arange(feat)[:, None] == to[None, :]).astype(bf16)

    own = 16
    place = jnp.stack([dp, dp ^ 1, jnp.int32(nrow), group, xl * ncore + 1 - core, core])
    packed, mine, near, cross = pl.pallas_call(
        finish_kernel,
        out_shape=[jax.ShapeDtypeStruct((own, n), f32) for n in (2 * feat + cols, cols, cols, cols)],
        in_specs=[sm, vm, vm, vm],
        out_specs=[vm] * 4,
        scratch_shapes=[pltpu.VMEM((2, 3, feat, feat), bf16)],
        compiler_params=params,
        cost_estimate=pl.CostEstimate(flops=6 * feat**3, bytes_accessed=8 * feat * feat, transcendentals=0),
    )(place, blocks.reshape(2 * nblk * TILE, TILE), part, order)

    got = lax.ppermute(packed, "core", swap)
    near = lax.ppermute(near, "zl", swap)
    cross = lax.ppermute(cross, ("core", "zl"), [(0, 3), (3, 0), (1, 2), (2, 1)])
    result, store = pl.pallas_call(
        output_kernel,
        out_shape=[jax.ShapeDtypeStruct((nrow, layers, cols), f32), jax.ShapeDtypeStruct((nrow, CAP, feat), f32)],
        in_specs=[sm, sm] + [vm] * 5,
        out_specs=[vm, vm],
        compiler_params=params,
    )(owners, place, packed, got, mine, near, cross)
    return jnp.transpose(result, (1, 0, 2)), jnp.transpose(store, (1, 0, 2))


def solution(mesh):
    split = Mesh(mesh.devices.reshape(2, 2, 2, 4, 4, 2), ("xl", "core", "xh", "y", "zh", "zl"))
    grp, dp = ("xl", "core"), ("xh", "y", "zh", "zl")
    return jax.shard_map(
        shards,
        mesh=split,
        in_specs=(P(None, grp + dp, None), P(None, grp + dp, None), P(None, dp, None), P()),
        out_specs=(P(None, dp, grp), P(grp, dp, None)),
        check_vma=False,
    )
```

time: 107 us -> 98.8 us (0.923)
  between operations: 8.22 us -> 0.81 us
  waiting for transfers between devices: 38 us -> 43.5 us
  local copies, waits for them, and re-layouts: 6.1 us -> 2.65 us
  Pallas kernels: 13.3 us -> 12.1 us
  starting transfers between devices: 38.7 us -> 37.6 us
    ppermute x1, waiting for transfers between devices: 17.3 us -> 0.01 us  [shards(): g = [g, lax.ppermute(g, X, [(0, 3), (3, 0), (1, 2), (2, 1)])]]
    ppermute x6 -> x9, waiting for transfers between devices: 9.41 us -> 24.8 us  [along(): lax.ppermute(a, axis, [(i, i ^ e) for i in range(size)])]
    all_to_all x1, waiting for transfers between devices: 9.75 us -> 16.8 us  [shards(): lax.all_to_all(jnp.broadcast_to(damped[None], (share, rows, TILE)), XYL,...]
    all_to_all x1 -> x0, starting transfers between devices: 5.89 us -> none  [shards(): stack = lax.all_to_all(mine, 'zh', 0, 0, tiled=True)]
    ppermute x6 -> x9, starting transfers between devices: 10.4 us -> 16.1 us  [along(): lax.ppermute(a, axis, [(i, i ^ e) for i in range(size)])]
    ppermute x1, starting transfers between devices: 2.57 us -> 0.76 us  [shards(): g = [g, lax.ppermute(g, X, [(0, 3), (3, 0), (1, 2), (2, 1)])]]
    unnamed x11 -> x9, local copies, waits for them, and re-layouts: 2.51 us -> 1.16 us
    pallas_call x2, Pallas kernels: 8.99 us -> 7.66 us  [the longest x1 6.43 us: shards(): pl.pallas_call(finish_kernel, out_shape=[jax.ShapeDtypeStruct((own, n), f...]
  transfers between devices with their start and end apart: 14 -> 17, of which waited for: 7 -> 8; matrix products, arithmetic and copies ran while one was open for 4% -> 2% of each run, Pallas kernels for 4% -> 4%
where the time goes in v2:
time: 98.8 us; the launch traced here: 98.5 us
  waiting for transfers between devices  43.5 us (44%)
  starting transfers between devices  37.6 us (38%)
  Pallas kernels  12.1 us (12%)
  local copies, waits for them, and re-layouts  2.65 us (3%)
  other arithmetic  1.8 us (2%)
    ppermute x9, waiting for transfers between devices, along(): lax.ppermute(a, axis, [(i, i ^ e) for i in range(size)])  24.8 us
    all_to_all x1, waiting for transfers between devices, shards(): lax.all_to_all(jnp.broadcast_to(damped[None], (share, rows, TILE)), XYL,...  16.8 us
    ppermute x9, starting transfers between devices, along(): lax.ppermute(a, axis, [(i, i ^ e) for i in range(size)])  16.1 us
    all_to_all x1, starting transfers between devices, shards(): lax.all_to_all(partial.reshape(share, rows, TILE), XYL, 0, 0, tiled=True)  7.51 us
    pallas_call x1, Pallas kernels, shards(): pl.pallas_call(finish_kernel, out_shape=[jax.ShapeDtypeStruct((own, n), f...  6.43 us
    pallas_call x1, Pallas kernels, shards(): pl.pallas_call(factor_kernel, out_shape=jax.ShapeDtypeStruct((2 * nblk *...  4.42 us
    all_to_all x1, starting transfers between devices, shards(): lax.all_to_all(jnp.broadcast_to(damped[None], (share, rows, TILE)), XYL,...  4.37 us
    ppermute x1, starting transfers between devices, shards(): got = lax.ppermute(packed, 'core', swap)  3.66 us
  transfers between devices with their start and end apart: 17, of which 8 were waited for; matrix products, arithmetic and copies ran while one was open for 2% of the time, Pallas kernels for 4%

profile of v2, /device:TPU:1, one launch (start us, length us, event | category | flops | bytes accessed | tf_op | source)
XLA Modules:
  0.0 98.5 jit_solution(14498549546645959353)
XLA Ops:
  0.6 0.0 copy-start
  0.6 3.3 %collective-permute-start = (bf16[2,512,768]{2,1,0:T(8,128)(2,1)}, bf16[2,512,768]{2,1,0:T(8,128)(2,1)S(1)}, u32[]{:S(2)}, u32[]{:S(2)}) collective-permute-start(bf16[2,512,768]{2,1,0:T(8,128)(2,1)} %act.1), channel_id=1, source_target_pairs={{0,64},{64,0},{1,65},{65,1},{2,66},{66,2},{3,67},{67,3},{4,68},{68... | collective-permute-start | bytes 4718600 | tf_op jit(solution)/shard_map/ppermute | solution.py:196
  4.0 0.1 collective-permute-start.1
  4.1 1.3 %collective-permute-start.2 = (bf16[12,768]{1,0:T(8,128)(2,1)S(1)}, bf16[12,768]{1,0:T(8,128)(2,1)S(1)}, u32[]{:S(2)}, u32[]{:S(2)}) collective-permute-start(bf16[12,768]{1,0:T(8,128)(2,1)S(1)} %bitcast.30), channel_id=1, source_target_pairs={{0,2},{2,0},{4,6},{6,4},{1,3},{3,1},{5,7},{7,5},{8,10},{10,8},{12,... | collective-permute-start | bytes 55304 | tf_op jit(solution)/shard_map/ppermute | solution.py:199
  5.5 5.1 %collective-permute-start.3 = (bf16[12,768]{1,0:T(8,128)(2,1)S(1)}, bf16[12,768]{1,0:T(8,128)(2,1)S(1)}, u32[]{:S(2)}, u32[]{:S(2)}) collective-permute-start(bf16[12,768]{1,0:T(8,128)(2,1)S(1)} %bitcast.31), channel_id=1, source_target_pairs={{0,4},{2,6},{4,0},{6,2},{1,5},{3,7},{5,1},{7,3},{8,12},{10,14},{12... | collective-permute-start | bytes 55304 | tf_op jit(solution)/shard_map/ppermute | solution.py:199
  10.6 0.0 collective-permute-start.4
  10.6 0.0 collective-permute-done.peer_act
  10.6 0.0 collective-permute-done.1.peer_bg
  10.6 1.1 %copy-done.3 = bf16[2,512,768]{2,1,0:T(8,128)(2,1)} copy-done((bf16[2,512,768]{2,1,0:T(8,128)(2,1)}, bf16[2,512,768]{2,1,0:T(8,128)(2,1)S(1)}, u32[]{:S(2)}) %copy-start.3) | copy-done | bytes 1572888
  11.8 4.4 %shard_map.59 = bf16[5120,128]{1,0:T(8,128)(2,1)} custom-call(s32[1]{0:T(128)} %bitcast.4.core_ref, bf16[2,512,768]{2,1,0:T(8,128)(2,1)} %act.1, bf16[2,512,768]{2,1,0:T(8,128)(2,1)} %bg.1, bf16[2,512,768]{2,1,0:T(8,128)(2,1)} %copy-done.3, bf16[2,512,768]{2,1,0:T(8,128)(2,1)} %collective-permute-done.1.peer_bg), custom_call_target="tpu_custom_call" | custom-call | flops 2415919104 | bytes 3145728 | tf_op jit(solution)/shard_map/pallas_call | solution.py:204
  16.2 0.0 collective-permute-done.2
  16.2 0.0 collective-permute-done.3
  16.2 0.0 collective-permute-done.4
  16.2 7.5 %all-to-all-start = ((bf16[32,160,128]{2,1,0:T(8,128)(2,1)}), bf16[32,160,128]{2,1,0:T(8,128)(2,1)S(1)}, u32[]{:S(2)}, u32[]{:S(2)}) async-start(bf16[32,160,128]{2,1,0:T(8,128)(2,1)} %bitcast.24), calls=%async_computation | async-start | bytes 2621440 | tf_op jit(solution)/shard_map/all_to_all | solution.py:221
  23.8 1.3 %collective-permute-start.5 = (bf16[4,12,768]{2,1,0:T(8,128)(2,1)S(1)}, bf16[4,12,768]{2,1,0:T(8,128)(2,1)S(1)}, u32[]{:S(2)}, u32[]{:S(2)}) collective-permute-start(bf16[4,12,768]{2,1,0:T(8,128)(2,1)S(1)} %pad_maximum_fusion.2), channel_id=1, source_target_pairs={{0,8},{8,0},{16,24},{24,16},{1,9},{9,1},{17,25},{25,17},{2,10},{10... | collective-permute-start | bytes 221192 | tf_op jit(solution)/shard_map/ppermute | solution.py:199
  25.1 2.4 %collective-permute-start.6 = (bf16[4,12,768]{2,1,0:T(8,128)(2,1)S(1)}, bf16[4,12,768]{2,1,0:T(8,128)(2,1)S(1)}, u32[]{:S(2)}, u32[]{:S(2)}) collective-permute-start(bf16[4,12,768]{2,1,0:T(8,128)(2,1)S(1)} %pad_maximum_fusion.2), channel_id=1, source_target_pairs={{0,16},{8,24},{16,0},{24,8},{1,17},{9,25},{17,1},{25,9},{2,18},{10... | collective-permute-start | bytes 221192 | tf_op jit(solution)/shard_map/ppermute | solution.py:199
  27.5 0.2 collective-permute-start.7
  27.7 8.9 %collective-permute-done.5 = bf16[4,12,768]{2,1,0:T(8,128)(2,1)S(1)} collective-permute-done((bf16[4,12,768]{2,1,0:T(8,128)(2,1)S(1)}, bf16[4,12,768]{2,1,0:T(8,128)(2,1)S(1)}, u32[]{:S(2)}, u32[]{:S(2)}) %collective-permute-start.5) | collective-permute-done | bytes 73760 | tf_op jit(solution)/shard_map/ppermute | solution.py:199
  36.6 6.5 %collective-permute-done.6 = bf16[4,12,768]{2,1,0:T(8,128)(2,1)S(1)} collective-permute-done((bf16[4,12,768]{2,1,0:T(8,128)(2,1)S(1)}, bf16[4,12,768]{2,1,0:T(8,128)(2,1)S(1)}, u32[]{:S(2)}, u32[]{:S(2)}) %collective-permute-start.6) | collective-permute-done | bytes 73760 | tf_op jit(solution)/shard_map/ppermute | solution.py:199
  43.2 3.9 %collective-permute-done.7 = bf16[4,12,768]{2,1,0:T(8,128)(2,1)S(1)} collective-permute-done((bf16[4,12,768]{2,1,0:T(8,128)(2,1)S(1)}, bf16[4,12,768]{2,1,0:T(8,128)(2,1)S(1)}, u32[]{:S(2)}, u32[]{:S(2)}) %collective-permute-start.7) | collective-permute-done | bytes 73760 | tf_op jit(solution)/shard_map/ppermute | solution.py:199
  47.1 0.0 all-to-all-done
  47.1 0.2 reduce_sum.12
  47.3 0.1 pad_maximum_fusion.1
  47.4 0.8 collective-permute-start.11
  48.2 1.5 %collective-permute-start.8 = (bf16[160,128]{1,0:T(8,128)(2,1)S(1)}, bf16[160,128]{1,0:T(8,128)(2,1)S(1)}, u32[]{:S(2)}, u32[]{:S(2)}) collective-permute-start(bf16[160,128]{1,0:T(8,128)(2,1)S(1)} %reduce_sum.12), channel_id=1, source_target_pairs={{0,2},{2,0},{4,6},{6,4},{1,3},{3,1},{5,7},{7,5},{8,10},{10,8},{12,... | collective-permute-start | bytes 122888 | tf_op jit(solution)/shard_map/ppermute | solution.py:199
  49.7 4.2 %collective-permute-start.9 = (bf16[160,128]{1,0:T(8,128)(2,1)S(1)}, bf16[160,128]{1,0:T(8,128)(2,1)S(1)}, u32[]{:S(2)}, u32[]{:S(2)}) collective-permute-start(bf16[160,128]{1,0:T(8,128)(2,1)S(1)} %reduce_sum.12), channel_id=1, source_target_pairs={{0,4},{2,6},{4,0},{6,2},{1,5},{3,7},{5,1},{7,3},{8,12},{10,14},{12... | collective-permute-start | bytes 122888 | tf_op jit(solution)/shard_map/ppermute | solution.py:199
  53.9 0.0 collective-permute-start.10
  53.9 0.0 collective-permute-done.8
  54.0 2.5 %collective-permute-done.9 = bf16[160,128]{1,0:T(8,128)(2,1)S(1)} collective-permute-done((bf16[160,128]{1,0:T(8,128)(2,1)S(1)}, bf16[160,128]{1,0:T(8,128)(2,1)S(1)}, u32[]{:S(2)}, u32[]{:S(2)}) %collective-permute-start.9) | collective-permute-done | bytes 40992 | tf_op jit(solution)/shard_map/ppermute | solution.py:199
  56.5 2.9 %collective-permute-done.10 = bf16[160,128]{1,0:T(8,128)(2,1)S(1)} collective-permute-done((bf16[160,128]{1,0:T(8,128)(2,1)S(1)}, bf16[160,128]{1,0:T(8,128)(2,1)S(1)}, u32[]{:S(2)}, u32[]{:S(2)}) %collective-permute-start.10) | collective-permute-done | bytes 40992 | tf_op jit(solution)/shard_map/ppermute | solution.py:199
  59.4 0.0 collective-permute-done.11
  59.4 0.2 add_convert_fusion
  59.5 1.2 %broadcast_in_dim.12 = bf16[32,160,128]{2,1,0:T(8,128)(2,1)} broadcast(bf16[160,128]{1,0:T(8,128)(2,1)S(1)} %add_convert_fusion), dimensions={1,2} | broadcast | bytes 1351680 | tf_op jit(solution)/shard_map/broadcast_in_dim | solution.py:243
  60.8 4.4 %all-to-all-start.1 = ((bf16[32,160,128]{2,1,0:T(8,128)(2,1)}), bf16[32,160,128]{2,1,0:T(8,128)(2,1)S(1)}, u32[]{:S(2)}, u32[]{:S(2)}) async-start(bf16[32,160,128]{2,1,0:T(8,128)(2,1)} %broadcast_in_dim.12), calls=%async_computation.1 | async-start | bytes 2621440 | tf_op jit(solution)/shard_map/all_to_all | solution.py:243
  65.2 0.1 stack.62.place
  65.3 0.2 fusion.order
  65.5 1.1 %pad_maximum_fusion = bf16[2,4,4,12,768]{4,3,2,1,0:T(8,128)(2,1)S(1)} fusion(bf16[1,4,4,12,768]{4,3,2,1,0:T(8,128)(2,1)} %bitcast.26, bf16[1,4,4,12,768]{4,3,2,1,0:T(8,128)(2,1)S(1)} %bitcast.23), kind=kLoop, calls=%fused_computation.2 | loop fusion | flops 294912 | bytes 1179648 | tf_op jit(solution)/shard_map/stack | solution.py:245
  66.6 0.1 reshape.145.grads
  66.7 16.8 %all-to-all-done.1 = bf16[32,160,128]{2,1,0:T(8,128)(2,1)S(1)} async-done(((bf16[32,160,128]{2,1,0:T(8,128)(2,1)}), bf16[32,160,128]{2,1,0:T(8,128)(2,1)S(1)}, u32[]{:S(2)}, u32[]{:S(2)}) %all-to-all-start.1) | async-done | bytes 1310752 | tf_op jit(solution)/shard_map/all_to_all | solution.py:243
  83.5 6.4 %shard_map.60 = (f32[16,1728]{1,0:T(8,128)S(1)}, f32[16,192]{1,0:T(8,128)S(1)}, f32[16,192]{1,0:T(8,128)S(1)}, f32[16,192]{1,0:T(8,128)S(1)}) custom-call(s32[6]{0:T(128)S(1)} %stack.62.place, bf16[5120,128]{1,0:T(8,128)(2,1)S(1)} %bitcast.22, bf16[384,768]{1,0:T(8,128)(2,1)S(1)} %reshape.145.grads, bf16[768,384]{1,0:T(8,128)(2,1)S(1)} %fusion.order), custom_call_target="tpu_custom_call" | custom-call | flops 2717908992 | bytes 4718592 | tf_op jit(solution)/shard_map/pallas_call | solution.py:256
  90.0 3.7 %collective-permute-start.12 = (f32[16,1728]{1,0:T(8,128)S(1)}, f32[16,1728]{1,0:T(8,128)S(1)}, u32[]{:S(2)}, u32[]{:S(2)}) collective-permute-start(f32[16,1728]{1,0:T(8,128)S(1)} %get-tuple-element.50.packed), channel_id=1, source_target_pairs={{0,64},{64,0},{1,65},{65,1},{2,66},{66,2},{3,67},{67,3},{4,68},{68... | collective-permute-start | bytes 331784 | tf_op jit(solution)/shard_map/ppermute | solution.py:266
  93.6 0.3 collective-permute-start.13
  93.9 1.4 %collective-permute-start.14 = (f32[16,192]{1,0:T(8,128)S(1)}, f32[16,192]{1,0:T(8,128)S(1)}, u32[]{:S(2)}, u32[]{:S(2)}) collective-permute-start(f32[16,192]{1,0:T(8,128)S(1)} %get-tuple-element.53), channel_id=1, source_target_pairs={{0,65},{65,0},{1,64},{64,1},{2,67},{67,2},{3,66},{66,3},{4,69},{69... | collective-permute-start | bytes 36872 | tf_op jit(solution)/shard_map/ppermute | solution.py:268
  95.3 0.9 collective-permute-done.13.near
  96.2 1.0 %collective-permute-done.14.cross = f32[16,192]{1,0:T(8,128)S(1)} collective-permute-done((f32[16,192]{1,0:T(8,128)S(1)}, f32[16,192]{1,0:T(8,128)S(1)}, u32[]{:S(2)}, u32[]{:S(2)}) %collective-permute-start.14) | collective-permute-done | bytes 12320 | tf_op jit(solution)/shard_map/ppermute | solution.py:268
  97.2 0.0 collective-permute-done.12.got
  97.2 0.0 copy-done.1
  97.2 1.2 %shard_map.61 = (f32[12,2,192]{2,1,0:T(2,128)}, f32[12,2,768]{2,1,0:T(2,128)}) custom-call(s32[4]{0:T(128)S(1)} %copy-done.1, s32[6]{0:T(128)S(1)} %stack.62.place, f32[16,1728]{1,0:T(8,128)S(1)} %get-tuple-element.50.packed, f32[16,1728]{1,0:T(8,128)S(1)} %collective-permute-done.12.got, f32[16,192]{1,0:T(8,128)S(1)} %get-tuple-element.51.mine, ...), custom_call_target="tpu_custom_call" | custom-call | tf_op jit(solution)/shard_map/pallas_call | solution.py:269
  (11 shorter events, 0.1 us)
Async XLA Ops:
  0.6 3.4 %copy-start = (f32[2,12,768]{2,0,1:T(2,128)S(1)}, f32[2,12,768]{2,0,1:T(2,128)}, u32[]{:S(2)}) copy-start(f32[2,12,768]{2,0,1:T(2,128)} %param.6) | copy-start | bytes 221188
  0.6 10.0 %collective-permute-start = (bf16[2,512,768]{2,1,0:T(8,128)(2,1)}, bf16[2,512,768]{2,1,0:T(8,128)(2,1)S(1)}, u32[]{:S(2)}, u32[]{:S(2)}) collective-permute-start(bf16[2,512,768]{2,1,0:T(8,128)(2,1)} %act.1), channel_id=1, source_target_pairs={{0,64},{64,0},{1,65},{65,1},{2,66},{66,2},{3,67},{67,3},{4,68},{68... | collective-permute-start | bytes 4718600 | tf_op jit(solution)/shard_map/ppermute | solution.py:196
  4.0 6.6 %collective-permute-start.1 = (bf16[2,512,768]{2,1,0:T(8,128)(2,1)}, bf16[2,512,768]{2,1,0:T(8,128)(2,1)}, u32[]{:S(2)}, u32[]{:S(2)}) collective-permute-start(bf16[2,512,768]{2,1,0:T(8,128)(2,1)} %bg.1), channel_id=1, source_target_pairs={{0,64},{64,0},{1,65},{65,1},{2,66},{66,2},{3,67},{67,3},{4,68},{68... | collective-permute-start | bytes 4718600 | tf_op jit(solution)/shard_map/ppermute | solution.py:196
  4.1 12.0 %collective-permute-start.2 = (bf16[12,768]{1,0:T(8,128)(2,1)S(1)}, bf16[12,768]{1,0:T(8,128)(2,1)S(1)}, u32[]{:S(2)}, u32[]{:S(2)}) collective-permute-start(bf16[12,768]{1,0:T(8,128)(2,1)S(1)} %bitcast.30), channel_id=1, source_target_pairs={{0,2},{2,0},{4,6},{6,4},{1,3},{3,1},{5,7},{7,5},{8,10},{10,8},{12,... | collective-permute-start | bytes 55304 | tf_op jit(solution)/shard_map/ppermute | solution.py:199
  5.5 10.7 %collective-permute-start.3 = (bf16[12,768]{1,0:T(8,128)(2,1)S(1)}, bf16[12,768]{1,0:T(8,128)(2,1)S(1)}, u32[]{:S(2)}, u32[]{:S(2)}) collective-permute-start(bf16[12,768]{1,0:T(8,128)(2,1)S(1)} %bitcast.31), channel_id=1, source_target_pairs={{0,4},{2,6},{4,0},{6,2},{1,5},{3,7},{5,1},{7,3},{8,12},{10,14},{12... | collective-permute-start | bytes 55304 | tf_op jit(solution)/shard_map/ppermute | solution.py:199
  10.6 5.6 %collective-permute-start.4 = (bf16[12,768]{1,0:T(8,128)(2,1)S(1)}, bf16[12,768]{1,0:T(8,128)(2,1)S(1)}, u32[]{:S(2)}, u32[]{:S(2)}) collective-permute-start(bf16[12,768]{1,0:T(8,128)(2,1)S(1)} %bitcast.32), channel_id=1, source_target_pairs={{0,6},{2,4},{4,2},{6,0},{1,7},{3,5},{5,3},{7,1},{8,14},{10,12},{12... | collective-permute-start | bytes 55304 | tf_op jit(solution)/shard_map/ppermute | solution.py:199
  10.6 1.1 %copy-start.3 = (bf16[2,512,768]{2,1,0:T(8,128)(2,1)}, bf16[2,512,768]{2,1,0:T(8,128)(2,1)S(1)}, u32[]{:S(2)}) copy-start(bf16[2,512,768]{2,1,0:T(8,128)(2,1)S(1)} %collective-permute-done.peer_act) | copy-start | bytes 4718596
  16.2 30.9 %all-to-all-start = ((bf16[32,160,128]{2,1,0:T(8,128)(2,1)}), bf16[32,160,128]{2,1,0:T(8,128)(2,1)S(1)}, u32[]{:S(2)}, u32[]{:S(2)}) async-start(bf16[32,160,128]{2,1,0:T(8,128)(2,1)} %bitcast.24), calls=%async_computation | async-start | bytes 2621440 | tf_op jit(solution)/shard_map/all_to_all | solution.py:221
  23.8 12.9 %collective-permute-start.5 = (bf16[4,12,768]{2,1,0:T(8,128)(2,1)S(1)}, bf16[4,12,768]{2,1,0:T(8,128)(2,1)S(1)}, u32[]{:S(2)}, u32[]{:S(2)}) collective-permute-start(bf16[4,12,768]{2,1,0:T(8,128)(2,1)S(1)} %pad_maximum_fusion.2), channel_id=1, source_target_pairs={{0,8},{8,0},{16,24},{24,16},{1,9},{9,1},{17,25},{25,17},{2,10},{10... | collective-permute-start | bytes 221192 | tf_op jit(solution)/shard_map/ppermute | solution.py:199
  25.1 18.1 %collective-permute-start.6 = (bf16[4,12,768]{2,1,0:T(8,128)(2,1)S(1)}, bf16[4,12,768]{2,1,0:T(8,128)(2,1)S(1)}, u32[]{:S(2)}, u32[]{:S(2)}) collective-permute-start(bf16[4,12,768]{2,1,0:T(8,128)(2,1)S(1)} %pad_maximum_fusion.2), channel_id=1, source_target_pairs={{0,16},{8,24},{16,0},{24,8},{1,17},{9,25},{17,1},{25,9},{2,18},{10... | collective-permute-start | bytes 221192 | tf_op jit(solution)/shard_map/ppermute | solution.py:199
  27.5 19.7 %collective-permute-start.7 = (bf16[4,12,768]{2,1,0:T(8,128)(2,1)S(1)}, bf16[4,12,768]{2,1,0:T(8,128)(2,1)S(1)}, u32[]{:S(2)}, u32[]{:S(2)}) collective-permute-start(bf16[4,12,768]{2,1,0:T(8,128)(2,1)S(1)} %pad_maximum_fusion.2), channel_id=1, source_target_pairs={{0,24},{8,16},{16,8},{24,0},{1,25},{9,17},{17,9},{25,1},{2,26},{10... | collective-permute-start | bytes 221192 | tf_op jit(solution)/shard_map/ppermute | solution.py:199
  47.4 12.0 %collective-permute-start.11 = (bf16[4,4,12,768]{3,2,1,0:T(8,128)(2,1)S(1)}, bf16[4,4,12,768]{3,2,1,0:T(8,128)(2,1)S(1)}, u32[]{:S(2)}, u32[]{:S(2)}) collective-permute-start(bf16[4,4,12,768]{3,2,1,0:T(8,128)(2,1)S(1)} %pad_maximum_fusion.1), channel_id=1, source_target_pairs={{0,160},{160,0},{32,128},{128,32},{1,161},{161,1},{33,129},{129,33... | collective-permute-start | bytes 884744 | tf_op jit(solution)/shard_map/ppermute | solution.py:229
  48.2 5.8 %collective-permute-start.8 = (bf16[160,128]{1,0:T(8,128)(2,1)S(1)}, bf16[160,128]{1,0:T(8,128)(2,1)S(1)}, u32[]{:S(2)}, u32[]{:S(2)}) collective-permute-start(bf16[160,128]{1,0:T(8,128)(2,1)S(1)} %reduce_sum.12), channel_id=1, source_target_pairs={{0,2},{2,0},{4,6},{6,4},{1,3},{3,1},{5,7},{7,5},{8,10},{10,8},{12,... | collective-permute-start | bytes 122888 | tf_op jit(solution)/shard_map/ppermute | solution.py:199
  49.7 6.8 %collective-permute-start.9 = (bf16[160,128]{1,0:T(8,128)(2,1)S(1)}, bf16[160,128]{1,0:T(8,128)(2,1)S(1)}, u32[]{:S(2)}, u32[]{:S(2)}) collective-permute-start(bf16[160,128]{1,0:T(8,128)(2,1)S(1)} %reduce_sum.12), channel_id=1, source_target_pairs={{0,4},{2,6},{4,0},{6,2},{1,5},{3,7},{5,1},{7,3},{8,12},{10,14},{12... | collective-permute-start | bytes 122888 | tf_op jit(solution)/shard_map/ppermute | solution.py:199
  53.9 5.4 %collective-permute-start.10 = (bf16[160,128]{1,0:T(8,128)(2,1)S(1)}, bf16[160,128]{1,0:T(8,128)(2,1)S(1)}, u32[]{:S(2)}, u32[]{:S(2)}) collective-permute-start(bf16[160,128]{1,0:T(8,128)(2,1)S(1)} %reduce_sum.12), channel_id=1, source_target_pairs={{0,6},{2,4},{4,2},{6,0},{1,7},{3,5},{5,3},{7,1},{8,14},{10,12},{12... | collective-permute-start | bytes 122888 | tf_op jit(solution)/shard_map/ppermute | solution.py:199
  59.4 6.1 %copy-start.2 = (bf16[4,4,12,768]{3,2,1,0:T(8,128)(2,1)}, bf16[4,4,12,768]{3,2,1,0:T(8,128)(2,1)S(1)}, u32[]{:S(2)}) copy-start(bf16[4,4,12,768]{3,2,1,0:T(8,128)(2,1)S(1)} %collective-permute-done.11) | copy-start | bytes 884740
  60.8 22.8 %all-to-all-start.1 = ((bf16[32,160,128]{2,1,0:T(8,128)(2,1)}), bf16[32,160,128]{2,1,0:T(8,128)(2,1)S(1)}, u32[]{:S(2)}, u32[]{:S(2)}) async-start(bf16[32,160,128]{2,1,0:T(8,128)(2,1)} %broadcast_in_dim.12), calls=%async_computation.1 | async-start | bytes 2621440 | tf_op jit(solution)/shard_map/all_to_all | solution.py:243
  83.5 13.7 %copy-start.1 = (s32[4]{0:T(128)S(1)}, s32[4]{0:T(128)}, u32[]{:S(2)}) copy-start(s32[4]{0:T(128)} %owners.1) | copy-start | bytes 52
  90.0 7.3 %collective-permute-start.12 = (f32[16,1728]{1,0:T(8,128)S(1)}, f32[16,1728]{1,0:T(8,128)S(1)}, u32[]{:S(2)}, u32[]{:S(2)}) collective-permute-start(f32[16,1728]{1,0:T(8,128)S(1)} %get-tuple-element.50.packed), channel_id=1, source_target_pairs={{0,64},{64,0},{1,65},{65,1},{2,66},{66,2},{3,67},{67,3},{4,68},{68... | collective-permute-start | bytes 331784 | tf_op jit(solution)/shard_map/ppermute | solution.py:266
  93.6 2.6 %collective-permute-start.13 = (f32[16,192]{1,0:T(8,128)S(1)}, f32[16,192]{1,0:T(8,128)S(1)}, u32[]{:S(2)}, u32[]{:S(2)}) collective-permute-start(f32[16,192]{1,0:T(8,128)S(1)} %get-tuple-element.52), channel_id=1, source_target_pairs={{0,1},{1,0},{2,3},{3,2},{4,5},{5,4},{6,7},{7,6},{8,9},{9,8},{10,11... | collective-permute-start | bytes 36872 | tf_op jit(solution)/shard_map/ppermute | solution.py:267
  93.9 3.3 %collective-permute-start.14 = (f32[16,192]{1,0:T(8,128)S(1)}, f32[16,192]{1,0:T(8,128)S(1)}, u32[]{:S(2)}, u32[]{:S(2)}) collective-permute-start(f32[16,192]{1,0:T(8,128)S(1)} %get-tuple-element.53), channel_id=1, source_target_pairs={{0,65},{65,0},{1,64},{64,1},{2,67},{67,2},{3,66},{66,3},{4,69},{69... | collective-permute-start | bytes 36872 | tf_op jit(solution)/shard_map/ppermute | solution.py:268

commit v3 on v2

--- a/solution.py
+++ b/solution.py
@@ -199,7 +199,7 @@
         return [a] + [lax.ppermute(a, axis, [(i, i ^ e) for i in range(size)]) for e in range(1, size)]
 
     g = lax.dynamic_index_in_dim(grads, core, 0, keepdims=False).astype(bf16)
-    g = along(g, "zh")
+    g = along(g.reshape(nrow * feat // TILE, TILE), "zh")
 
     partial = pl.pallas_call(
         factor_kernel,
@@ -211,7 +211,7 @@
             pltpu.VMEM((2 * nblk * TILE, TILE), bf16),
             pltpu.SemaphoreType.DMA((2, 3)),
         ],
-        compiler_params=pltpu.CompilerParams(vmem_limit_bytes=60 << 20),
+        compiler_params=pltpu.CompilerParams(vmem_limit_bytes=63 << 20),
         cost_estimate=pl.CostEstimate(flops=4 * tok * 2 * feat * feat, bytes_accessed=8 * tok * feat, transcendentals=0),
     )(core.reshape(1), activations, back_grads, *peer)
 

time: 98.8 us -> 96.7 us (0.979)
  other arithmetic: 1.8 us -> 0.72 us
    unnamed x9 -> x4, local copies, waits for them, and re-layouts: 1.16 us -> 0.01 us
    ppermute x9, waiting for transfers between devices: 24.8 us -> 23.7 us  [along(): lax.ppermute(a, axis, [(i, i ^ e) for i in range(size)])]
    another operation x1, other arithmetic: 1.1 us -> 0.06 us  [shards(): part = jnp.stack(g).reshape(half, feat)]
  transfers between devices with their start and end apart: 17 -> 17, of which waited for: 8 -> 9; matrix products, arithmetic and copies ran while one was open for 2% -> 1% of each run, Pallas kernels for 4% -> 5%
where the time goes in v3:
time: 96.7 us; the launch traced here: 96.4 us
  waiting for transfers between devices  43.2 us (45%)
  starting transfers between devices  37.6 us (39%)
  Pallas kernels  12.1 us (13%)
  local copies, waits for them, and re-layouts  2.02 us (2%)
    ppermute x9, waiting for transfers between devices, along(): lax.ppermute(a, axis, [(i, i ^ e) for i in range(size)])  23.7 us
    all_to_all x1, waiting for transfers between devices, shards(): lax.all_to_all(jnp.broadcast_to(damped[None], (share, rows, TILE)), XYL,...  17.6 us
    ppermute x9, starting transfers between devices, along(): lax.ppermute(a, axis, [(i, i ^ e) for i in range(size)])  16.2 us
    all_to_all x1, starting transfers between devices, shards(): lax.all_to_all(partial.reshape(share, rows, TILE), XYL, 0, 0, tiled=True)  7.49 us
    pallas_call x1, Pallas kernels, shards(): pl.pallas_call(finish_kernel, out_shape=[jax.ShapeDtypeStruct((own, n), f...  6.44 us
    pallas_call x1, Pallas kernels, shards(): pl.pallas_call(factor_kernel, out_shape=jax.ShapeDtypeStruct((2 * nblk *...  4.42 us
    all_to_all x1, starting transfers between devices, shards(): lax.all_to_all(jnp.broadcast_to(damped[None], (share, rows, TILE)), XYL,...  4.29 us
    ppermute x1, starting transfers between devices, shards(): got = lax.ppermute(packed, 'core', swap)  3.59 us
  transfers between devices with their start and end apart: 17, of which 9 were waited for; matrix products, arithmetic and copies ran while one was open for 1% of the time, Pallas kernels for 5%

profile of v3, /device:TPU:1, one launch (start us, length us, event | category | flops | bytes accessed | tf_op | source)
XLA Modules:
  0.0 96.4 jit_solution(15293349925538851610)
XLA Ops:
  0.6 0.0 copy-start
  0.6 3.3 %collective-permute-start = (bf16[2,512,768]{2,1,0:T(8,128)(2,1)}, bf16[2,512,768]{2,1,0:T(8,128)(2,1)}, u32[]{:S(2)}, u32[]{:S(2)}) collective-permute-start(bf16[2,512,768]{2,1,0:T(8,128)(2,1)} %act.1), channel_id=1, source_target_pairs={{0,64},{64,0},{1,65},{65,1},{2,66},{66,2},{3,67},{67,3},{4,68},{68... | collective-permute-start | bytes 4718600 | tf_op jit(solution)/shard_map/ppermute | solution.py:196
  4.0 0.1 collective-permute-start.1
  4.1 0.0 copy-done
  4.1 0.1 convert_reduce_fusion
  4.2 1.3 %collective-permute-start.2 = (bf16[72,128]{1,0:T(8,128)(2,1)S(1)}, bf16[72,128]{1,0:T(8,128)(2,1)S(1)}, u32[]{:S(2)}, u32[]{:S(2)}) collective-permute-start(bf16[72,128]{1,0:T(8,128)(2,1)S(1)} %convert_element_type.28), channel_id=1, source_target_pairs={{0,2},{2,0},{4,6},{6,4},{1,3},{3,1},{5,7},{7,5},{8,10},{10,8},{12,... | collective-permute-start | bytes 55304 | tf_op jit(solution)/shard_map/ppermute | solution.py:199
  5.6 5.1 %collective-permute-start.3 = (bf16[72,128]{1,0:T(8,128)(2,1)S(1)}, bf16[72,128]{1,0:T(8,128)(2,1)S(1)}, u32[]{:S(2)}, u32[]{:S(2)}) collective-permute-start(bf16[72,128]{1,0:T(8,128)(2,1)S(1)} %convert_element_type.28), channel_id=1, source_target_pairs={{0,4},{2,6},{4,0},{6,2},{1,5},{3,7},{5,1},{7,3},{8,12},{10,14},{12... | collective-permute-start | bytes 55304 | tf_op jit(solution)/shard_map/ppermute | solution.py:199
  10.7 0.0 collective-permute-start.4
  10.7 0.0 collective-permute-done.peer_act
  10.7 0.0 collective-permute-done.1.peer_bg
  10.7 4.4 %shard_map.59 = bf16[5120,128]{1,0:T(8,128)(2,1)} custom-call(s32[1]{0:T(128)} %bitcast.4.core_ref, bf16[2,512,768]{2,1,0:T(8,128)(2,1)} %act.1, bf16[2,512,768]{2,1,0:T(8,128)(2,1)} %bg.1, bf16[2,512,768]{2,1,0:T(8,128)(2,1)} %collective-permute-done.peer_act, bf16[2,512,768]{2,1,0:T(8,128)(2,1)} %collective-permute-done.1.peer_bg), custom_call_target="tpu_custom_call" | custom-call | flops 2415919104 | bytes 3145728 | tf_op jit(solution)/shard_map/pallas_call | solution.py:204
  15.1 0.0 collective-permute-done.2
  15.1 0.0 collective-permute-done.3
  15.2 0.3 collective-permute-done.4
  15.4 7.5 %all-to-all-start = ((bf16[32,160,128]{2,1,0:T(8,128)(2,1)}), bf16[32,160,128]{2,1,0:T(8,128)(2,1)S(1)}, u32[]{:S(2)}, u32[]{:S(2)}) async-start(bf16[32,160,128]{2,1,0:T(8,128)(2,1)} %bitcast.22), calls=%async_computation | async-start | bytes 2621440 | tf_op jit(solution)/shard_map/all_to_all | solution.py:221
  22.9 1.3 %collective-permute-start.5 = (bf16[4,72,128]{2,1,0:T(8,128)(2,1)S(1)}, bf16[4,72,128]{2,1,0:T(8,128)(2,1)S(1)}, u32[]{:S(2)}, u32[]{:S(2)}) collective-permute-start(bf16[4,72,128]{2,1,0:T(8,128)(2,1)S(1)} %pad_maximum_fusion.2), channel_id=1, source_target_pairs={{0,8},{8,0},{16,24},{24,16},{1,9},{9,1},{17,25},{25,17},{2,10},{10... | collective-permute-start | bytes 221192 | tf_op jit(solution)/shard_map/ppermute | solution.py:199
  24.3 2.4 %collective-permute-start.6 = (bf16[4,72,128]{2,1,0:T(8,128)(2,1)S(1)}, bf16[4,72,128]{2,1,0:T(8,128)(2,1)S(1)}, u32[]{:S(2)}, u32[]{:S(2)}) collective-permute-start(bf16[4,72,128]{2,1,0:T(8,128)(2,1)S(1)} %pad_maximum_fusion.2), channel_id=1, source_target_pairs={{0,16},{8,24},{16,0},{24,8},{1,17},{9,25},{17,1},{25,9},{2,18},{10... | collective-permute-start | bytes 221192 | tf_op jit(solution)/shard_map/ppermute | solution.py:199
  26.7 0.2 collective-permute-start.7
  26.9 5.4 %collective-permute-done.5 = bf16[4,72,128]{2,1,0:T(8,128)(2,1)S(1)} collective-permute-done((bf16[4,72,128]{2,1,0:T(8,128)(2,1)S(1)}, bf16[4,72,128]{2,1,0:T(8,128)(2,1)S(1)}, u32[]{:S(2)}, u32[]{:S(2)}) %collective-permute-start.5) | collective-permute-done | bytes 73760 | tf_op jit(solution)/shard_map/ppermute | solution.py:199
  32.3 8.0 %collective-permute-done.6 = bf16[4,72,128]{2,1,0:T(8,128)(2,1)S(1)} collective-permute-done((bf16[4,72,128]{2,1,0:T(8,128)(2,1)S(1)}, bf16[4,72,128]{2,1,0:T(8,128)(2,1)S(1)}, u32[]{:S(2)}, u32[]{:S(2)}) %collective-permute-start.6) | collective-permute-done | bytes 73760 | tf_op jit(solution)/shard_map/ppermute | solution.py:199
  40.2 4.9 %collective-permute-done.7 = bf16[4,72,128]{2,1,0:T(8,128)(2,1)S(1)} collective-permute-done((bf16[4,72,128]{2,1,0:T(8,128)(2,1)S(1)}, bf16[4,72,128]{2,1,0:T(8,128)(2,1)S(1)}, u32[]{:S(2)}, u32[]{:S(2)}) %collective-permute-start.7) | collective-permute-done | bytes 73760 | tf_op jit(solution)/shard_map/ppermute | solution.py:199
  45.1 0.0 all-to-all-done
  45.1 0.2 reduce_sum.12
  45.3 0.9 collective-permute-start.11
  46.2 1.3 %collective-permute-start.8 = (bf16[160,128]{1,0:T(8,128)(2,1)S(1)}, bf16[160,128]{1,0:T(8,128)(2,1)S(1)}, u32[]{:S(2)}, u32[]{:S(2)}) collective-permute-start(bf16[160,128]{1,0:T(8,128)(2,1)S(1)} %reduce_sum.12), channel_id=1, source_target_pairs={{0,2},{2,0},{4,6},{6,4},{1,3},{3,1},{5,7},{7,5},{8,10},{10,8},{12,... | collective-permute-start | bytes 122888 | tf_op jit(solution)/shard_map/ppermute | solution.py:199
  47.5 4.5 %collective-permute-start.9 = (bf16[160,128]{1,0:T(8,128)(2,1)S(1)}, bf16[160,128]{1,0:T(8,128)(2,1)S(1)}, u32[]{:S(2)}, u32[]{:S(2)}) collective-permute-start(bf16[160,128]{1,0:T(8,128)(2,1)S(1)} %reduce_sum.12), channel_id=1, source_target_pairs={{0,4},{2,6},{4,0},{6,2},{1,5},{3,7},{5,1},{7,3},{8,12},{10,14},{12... | collective-permute-start | bytes 122888 | tf_op jit(solution)/shard_map/ppermute | solution.py:199
  52.0 0.0 collective-permute-start.10
  52.1 0.0 collective-permute-done.8
  52.1 2.2 %collective-permute-done.9 = bf16[160,128]{1,0:T(8,128)(2,1)S(1)} collective-permute-done((bf16[160,128]{1,0:T(8,128)(2,1)S(1)}, bf16[160,128]{1,0:T(8,128)(2,1)S(1)}, u32[]{:S(2)}, u32[]{:S(2)}) %collective-permute-start.9) | collective-permute-done | bytes 40992 | tf_op jit(solution)/shard_map/ppermute | solution.py:199
  54.3 3.1 %collective-permute-done.10 = bf16[160,128]{1,0:T(8,128)(2,1)S(1)} collective-permute-done((bf16[160,128]{1,0:T(8,128)(2,1)S(1)}, bf16[160,128]{1,0:T(8,128)(2,1)S(1)}, u32[]{:S(2)}, u32[]{:S(2)}) %collective-permute-start.10) | collective-permute-done | bytes 40992 | tf_op jit(solution)/shard_map/ppermute | solution.py:199
  57.3 0.0 collective-permute-done.11
  57.3 0.2 add_convert_fusion
  57.5 1.3 %broadcast_in_dim.12 = bf16[32,160,128]{2,1,0:T(8,128)(2,1)} broadcast(bf16[160,128]{1,0:T(8,128)(2,1)S(1)} %add_convert_fusion), dimensions={1,2} | broadcast | bytes 1351680 | tf_op jit(solution)/shard_map/broadcast_in_dim | solution.py:243
  58.8 4.3 %all-to-all-start.1 = ((bf16[32,160,128]{2,1,0:T(8,128)(2,1)}), bf16[32,160,128]{2,1,0:T(8,128)(2,1)S(1)}, u32[]{:S(2)}, u32[]{:S(2)}) async-start(bf16[32,160,128]{2,1,0:T(8,128)(2,1)} %broadcast_in_dim.12), calls=%async_computation.1 | async-start | bytes 2621440 | tf_op jit(solution)/shard_map/all_to_all | solution.py:243
  63.1 0.1 stack.62.place
  63.2 0.2 fusion.order
  63.4 0.1 pad_maximum_fusion
  63.5 0.5 reshape.147.grads
  64.0 17.6 %all-to-all-done.1 = bf16[32,160,128]{2,1,0:T(8,128)(2,1)S(1)} async-done(((bf16[32,160,128]{2,1,0:T(8,128)(2,1)}), bf16[32,160,128]{2,1,0:T(8,128)(2,1)S(1)}, u32[]{:S(2)}, u32[]{:S(2)}) %all-to-all-start.1) | async-done | bytes 1310752 | tf_op jit(solution)/shard_map/all_to_all | solution.py:243
  81.6 6.4 %shard_map.60 = (f32[16,1728]{1,0:T(8,128)S(1)}, f32[16,192]{1,0:T(8,128)S(1)}, f32[16,192]{1,0:T(8,128)S(1)}, f32[16,192]{1,0:T(8,128)S(1)}) custom-call(s32[6]{0:T(128)S(1)} %stack.62.place, bf16[5120,128]{1,0:T(8,128)(2,1)S(1)} %bitcast.21, bf16[384,768]{1,0:T(8,128)(2,1)S(1)} %reshape.147.grads, bf16[768,384]{1,0:T(8,128)(2,1)S(1)} %fusion.order), custom_call_target="tpu_custom_call" | custom-call | flops 2717908992 | bytes 4718592 | tf_op jit(solution)/shard_map/pallas_call | solution.py:256
  88.0 3.6 %collective-permute-start.12 = (f32[16,1728]{1,0:T(8,128)S(1)}, f32[16,1728]{1,0:T(8,128)S(1)}, u32[]{:S(2)}, u32[]{:S(2)}) collective-permute-start(f32[16,1728]{1,0:T(8,128)S(1)} %get-tuple-element.50.packed), channel_id=1, source_target_pairs={{0,64},{64,0},{1,65},{65,1},{2,66},{66,2},{3,67},{67,3},{4,68},{68... | collective-permute-start | bytes 331784 | tf_op jit(solution)/shard_map/ppermute | solution.py:266
  91.6 0.3 collective-permute-start.13
  91.9 1.5 %collective-permute-start.14 = (f32[16,192]{1,0:T(8,128)S(1)}, f32[16,192]{1,0:T(8,128)S(1)}, u32[]{:S(2)}, u32[]{:S(2)}) collective-permute-start(f32[16,192]{1,0:T(8,128)S(1)} %get-tuple-element.53), channel_id=1, source_target_pairs={{0,65},{65,0},{1,64},{64,1},{2,67},{67,2},{3,66},{66,3},{4,69},{69... | collective-permute-start | bytes 36872 | tf_op jit(solution)/shard_map/ppermute | solution.py:268
  93.3 0.9 collective-permute-done.13.near
  94.2 1.0 collective-permute-done.14.cross
  95.2 0.0 collective-permute-done.12.got
  95.2 0.0 copy-done.1
  95.2 1.2 %shard_map.61 = (f32[12,2,192]{2,1,0:T(2,128)}, f32[12,2,768]{2,1,0:T(2,128)}) custom-call(s32[4]{0:T(128)S(1)} %copy-done.1, s32[6]{0:T(128)S(1)} %stack.62.place, f32[16,1728]{1,0:T(8,128)S(1)} %get-tuple-element.50.packed, f32[16,1728]{1,0:T(8,128)S(1)} %collective-permute-done.12.got, f32[16,192]{1,0:T(8,128)S(1)} %get-tuple-element.51.mine, ...), custom_call_target="tpu_custom_call" | custom-call | tf_op jit(solution)/shard_map/pallas_call | solution.py:269
  (7 shorter events, 0.2 us)
Async XLA Ops:
  0.6 3.4 %copy-start = (f32[2,12,768]{2,0,1:T(2,128)S(1)}, f32[2,12,768]{2,0,1:T(2,128)}, u32[]{:S(2)}) copy-start(f32[2,12,768]{2,0,1:T(2,128)} %param.6) | copy-start | bytes 221188
  0.6 10.1 %collective-permute-start = (bf16[2,512,768]{2,1,0:T(8,128)(2,1)}, bf16[2,512,768]{2,1,0:T(8,128)(2,1)}, u32[]{:S(2)}, u32[]{:S(2)}) collective-permute-start(bf16[2,512,768]{2,1,0:T(8,128)(2,1)} %act.1), channel_id=1, source_target_pairs={{0,64},{64,0},{1,65},{65,1},{2,66},{66,2},{3,67},{67,3},{4,68},{68... | collective-permute-start | bytes 4718600 | tf_op jit(solution)/shard_map/ppermute | solution.py:196
  4.0 6.7 %collective-permute-start.1 = (bf16[2,512,768]{2,1,0:T(8,128)(2,1)}, bf16[2,512,768]{2,1,0:T(8,128)(2,1)}, u32[]{:S(2)}, u32[]{:S(2)}) collective-permute-start(bf16[2,512,768]{2,1,0:T(8,128)(2,1)} %bg.1), channel_id=1, source_target_pairs={{0,64},{64,0},{1,65},{65,1},{2,66},{66,2},{3,67},{67,3},{4,68},{68... | collective-permute-start | bytes 4718600 | tf_op jit(solution)/shard_map/ppermute | solution.py:196
  4.2 10.9 %collective-permute-start.2 = (bf16[72,128]{1,0:T(8,128)(2,1)S(1)}, bf16[72,128]{1,0:T(8,128)(2,1)S(1)}, u32[]{:S(2)}, u32[]{:S(2)}) collective-permute-start(bf16[72,128]{1,0:T(8,128)(2,1)S(1)} %convert_element_type.28), channel_id=1, source_target_pairs={{0,2},{2,0},{4,6},{6,4},{1,3},{3,1},{5,7},{7,5},{8,10},{10,8},{12,... | collective-permute-start | bytes 55304 | tf_op jit(solution)/shard_map/ppermute | solution.py:199
  5.6 9.6 %collective-permute-start.3 = (bf16[72,128]{1,0:T(8,128)(2,1)S(1)}, bf16[72,128]{1,0:T(8,128)(2,1)S(1)}, u32[]{:S(2)}, u32[]{:S(2)}) collective-permute-start(bf16[72,128]{1,0:T(8,128)(2,1)S(1)} %convert_element_type.28), channel_id=1, source_target_pairs={{0,4},{2,6},{4,0},{6,2},{1,5},{3,7},{5,1},{7,3},{8,12},{10,14},{12... | collective-permute-start | bytes 55304 | tf_op jit(solution)/shard_map/ppermute | solution.py:199
  10.7 4.7 %collective-permute-start.4 = (bf16[72,128]{1,0:T(8,128)(2,1)S(1)}, bf16[72,128]{1,0:T(8,128)(2,1)S(1)}, u32[]{:S(2)}, u32[]{:S(2)}) collective-permute-start(bf16[72,128]{1,0:T(8,128)(2,1)S(1)} %convert_element_type.28), channel_id=1, source_target_pairs={{0,6},{2,4},{4,2},{6,0},{1,7},{3,5},{5,3},{7,1},{8,14},{10,12},{12... | collective-permute-start | bytes 55304 | tf_op jit(solution)/shard_map/ppermute | solution.py:199
  15.4 29.7 %all-to-all-start = ((bf16[32,160,128]{2,1,0:T(8,128)(2,1)}), bf16[32,160,128]{2,1,0:T(8,128)(2,1)S(1)}, u32[]{:S(2)}, u32[]{:S(2)}) async-start(bf16[32,160,128]{2,1,0:T(8,128)(2,1)} %bitcast.22), calls=%async_computation | async-start | bytes 2621440 | tf_op jit(solution)/shard_map/all_to_all | solution.py:221
  22.9 9.3 %collective-permute-start.5 = (bf16[4,72,128]{2,1,0:T(8,128)(2,1)S(1)}, bf16[4,72,128]{2,1,0:T(8,128)(2,1)S(1)}, u32[]{:S(2)}, u32[]{:S(2)}) collective-permute-start(bf16[4,72,128]{2,1,0:T(8,128)(2,1)S(1)} %pad_maximum_fusion.2), channel_id=1, source_target_pairs={{0,8},{8,0},{16,24},{24,16},{1,9},{9,1},{17,25},{25,17},{2,10},{10... | collective-permute-start | bytes 221192 | tf_op jit(solution)/shard_map/ppermute | solution.py:199
  24.3 16.0 %collective-permute-start.6 = (bf16[4,72,128]{2,1,0:T(8,128)(2,1)S(1)}, bf16[4,72,128]{2,1,0:T(8,128)(2,1)S(1)}, u32[]{:S(2)}, u32[]{:S(2)}) collective-permute-start(bf16[4,72,128]{2,1,0:T(8,128)(2,1)S(1)} %pad_maximum_fusion.2), channel_id=1, source_target_pairs={{0,16},{8,24},{16,0},{24,8},{1,17},{9,25},{17,1},{25,9},{2,18},{10... | collective-permute-start | bytes 221192 | tf_op jit(solution)/shard_map/ppermute | solution.py:199
  26.7 18.5 %collective-permute-start.7 = (bf16[4,72,128]{2,1,0:T(8,128)(2,1)S(1)}, bf16[4,72,128]{2,1,0:T(8,128)(2,1)S(1)}, u32[]{:S(2)}, u32[]{:S(2)}) collective-permute-start(bf16[4,72,128]{2,1,0:T(8,128)(2,1)S(1)} %pad_maximum_fusion.2), channel_id=1, source_target_pairs={{0,24},{8,16},{16,8},{24,0},{1,25},{9,17},{17,9},{25,1},{2,26},{10... | collective-permute-start | bytes 221192 | tf_op jit(solution)/shard_map/ppermute | solution.py:199
  45.3 12.0 %collective-permute-start.11 = (bf16[4,4,72,128]{3,2,1,0:T(8,128)(2,1)S(1)}, bf16[4,4,72,128]{3,2,1,0:T(8,128)(2,1)S(1)}, u32[]{:S(2)}, u32[]{:S(2)}) collective-permute-start(bf16[4,4,72,128]{3,2,1,0:T(8,128)(2,1)S(1)} %pad_maximum_fusion.1), channel_id=1, source_target_pairs={{0,160},{160,0},{32,128},{128,32},{1,161},{161,1},{33,129},{129,33... | collective-permute-start | bytes 884744 | tf_op jit(solution)/shard_map/ppermute | solution.py:229
  46.2 5.9 %collective-permute-start.8 = (bf16[160,128]{1,0:T(8,128)(2,1)S(1)}, bf16[160,128]{1,0:T(8,128)(2,1)S(1)}, u32[]{:S(2)}, u32[]{:S(2)}) collective-permute-start(bf16[160,128]{1,0:T(8,128)(2,1)S(1)} %reduce_sum.12), channel_id=1, source_target_pairs={{0,2},{2,0},{4,6},{6,4},{1,3},{3,1},{5,7},{7,5},{8,10},{10,8},{12,... | collective-permute-start | bytes 122888 | tf_op jit(solution)/shard_map/ppermute | solution.py:199
  47.5 6.8 %collective-permute-start.9 = (bf16[160,128]{1,0:T(8,128)(2,1)S(1)}, bf16[160,128]{1,0:T(8,128)(2,1)S(1)}, u32[]{:S(2)}, u32[]{:S(2)}) collective-permute-start(bf16[160,128]{1,0:T(8,128)(2,1)S(1)} %reduce_sum.12), channel_id=1, source_target_pairs={{0,4},{2,6},{4,0},{6,2},{1,5},{3,7},{5,1},{7,3},{8,12},{10,14},{12... | collective-permute-start | bytes 122888 | tf_op jit(solution)/shard_map/ppermute | solution.py:199
  52.0 5.3 %collective-permute-start.10 = (bf16[160,128]{1,0:T(8,128)(2,1)S(1)}, bf16[160,128]{1,0:T(8,128)(2,1)S(1)}, u32[]{:S(2)}, u32[]{:S(2)}) collective-permute-start(bf16[160,128]{1,0:T(8,128)(2,1)S(1)} %reduce_sum.12), channel_id=1, source_target_pairs={{0,6},{2,4},{4,2},{6,0},{1,7},{3,5},{5,3},{7,1},{8,14},{10,12},{12... | collective-permute-start | bytes 122888 | tf_op jit(solution)/shard_map/ppermute | solution.py:199
  58.8 22.8 %all-to-all-start.1 = ((bf16[32,160,128]{2,1,0:T(8,128)(2,1)}), bf16[32,160,128]{2,1,0:T(8,128)(2,1)S(1)}, u32[]{:S(2)}, u32[]{:S(2)}) async-start(bf16[32,160,128]{2,1,0:T(8,128)(2,1)} %broadcast_in_dim.12), calls=%async_computation.1 | async-start | bytes 2621440 | tf_op jit(solution)/shard_map/all_to_all | solution.py:243
  81.6 13.6 %copy-start.1 = (s32[4]{0:T(128)S(1)}, s32[4]{0:T(128)}, u32[]{:S(2)}) copy-start(s32[4]{0:T(128)} %owners.1) | copy-start | bytes 52
  88.0 7.2 %collective-permute-start.12 = (f32[16,1728]{1,0:T(8,128)S(1)}, f32[16,1728]{1,0:T(8,128)S(1)}, u32[]{:S(2)}, u32[]{:S(2)}) collective-permute-start(f32[16,1728]{1,0:T(8,128)S(1)} %get-tuple-element.50.packed), channel_id=1, source_target_pairs={{0,64},{64,0},{1,65},{65,1},{2,66},{66,2},{3,67},{67,3},{4,68},{68... | collective-permute-start | bytes 331784 | tf_op jit(solution)/shard_map/ppermute | solution.py:266
  91.6 2.6 %collective-permute-start.13 = (f32[16,192]{1,0:T(8,128)S(1)}, f32[16,192]{1,0:T(8,128)S(1)}, u32[]{:S(2)}, u32[]{:S(2)}) collective-permute-start(f32[16,192]{1,0:T(8,128)S(1)} %get-tuple-element.52), channel_id=1, source_target_pairs={{0,1},{1,0},{2,3},{3,2},{4,5},{5,4},{6,7},{7,6},{8,9},{9,8},{10,11... | collective-permute-start | bytes 36872 | tf_op jit(solution)/shard_map/ppermute | solution.py:267
  91.9 3.3 %collective-permute-start.14 = (f32[16,192]{1,0:T(8,128)S(1)}, f32[16,192]{1,0:T(8,128)S(1)}, u32[]{:S(2)}, u32[]{:S(2)}) collective-permute-start(f32[16,192]{1,0:T(8,128)S(1)} %get-tuple-element.53), channel_id=1, source_target_pairs={{0,65},{65,0},{1,64},{64,1},{2,67},{67,2},{3,66},{66,3},{4,69},{69... | collective-permute-start | bytes 36872 | tf_op jit(solution)/shard_map/ppermute | solution.py:268

commit v4 on v3

--- a/solution.py
+++ b/solution.py
@@ -220,10 +220,8 @@
     partial, g = lax.optimization_barrier((partial, g))
     terms = lax.all_to_all(partial.reshape(share, rows, TILE), XYL, 0, 0, tiled=True)
     g = along(jnp.stack(g), "y")
-    terms, g = lax.optimization_barrier((terms, g))
 
     mine = jnp.sum(terms.astype(f32), axis=0).astype(bf16)
-    mine, g = lax.optimization_barrier((mine, g))
     stack = along(mine, "zh")
     g = jnp.stack(g)
     g = [g, lax.ppermute(g, X, [(0, 3), (3, 0), (1, 2), (2, 1)])]

time: 96.7 us -> 96.2 us (level)
  waiting for transfers between devices: 43.2 us -> 41.4 us
  starting transfers between devices: 37.6 us -> 38.8 us
    ppermute x1, starting transfers between devices: 0.86 us -> 2.17 us  [shards(): g = [g, lax.ppermute(g, X, [(0, 3), (3, 0), (1, 2), (2, 1)])]]
    ppermute x9, waiting for transfers between devices: 23.7 us -> 22.5 us  [along(): lax.ppermute(a, axis, [(i, i ^ e) for i in range(size)])]
  transfers between devices with their start and end apart: 17 -> 17, of which waited for: 9 -> 8; matrix products, arithmetic and copies ran while one was open for 1% -> 1% of each run, Pallas kernels for 5% -> 5%
where the time goes in v4:
time: 96.2 us; the launch traced here: 95.9 us
  waiting for transfers between devices  41.4 us (43%)
  starting transfers between devices  38.8 us (40%)
  Pallas kernels  12.1 us (13%)
  local copies, waits for them, and re-layouts  2.01 us (2%)
    ppermute x9, waiting for transfers between devices, along(): lax.ppermute(a, axis, [(i, i ^ e) for i in range(size)])  22.5 us
    all_to_all x1, waiting for transfers between devices, shards(): lax.all_to_all(jnp.broadcast_to(damped[None], (share, rows, TILE)), XYL,...  16.9 us
    ppermute x9, starting transfers between devices, along(): lax.ppermute(a, axis, [(i, i ^ e) for i in range(size)])  15.5 us
    all_to_all x1, starting transfers between devices, shards(): lax.all_to_all(partial.reshape(share, rows, TILE), XYL, 0, 0, tiled=True)  7.49 us
    pallas_call x1, Pallas kernels, shards(): pl.pallas_call(finish_kernel, out_shape=[jax.ShapeDtypeStruct((own, n), f...  6.44 us
    all_to_all x1, starting transfers between devices, shards(): lax.all_to_all(jnp.broadcast_to(damped[None], (share, rows, TILE)), XYL,...  4.58 us
    pallas_call x1, Pallas kernels, shards(): pl.pallas_call(factor_kernel, out_shape=jax.ShapeDtypeStruct((2 * nblk *...  4.44 us
    ppermute x1, starting transfers between devices, shards(): got = lax.ppermute(packed, 'core', swap)  3.88 us
  transfers between devices with their start and end apart: 17, of which 8 were waited for; matrix products, arithmetic and copies ran while one was open for 1% of the time, Pallas kernels for 5%

profile of v4, /device:TPU:1, one launch (start us, length us, event | category | flops | bytes accessed | tf_op | source)
XLA Modules:
  0.0 95.9 jit_solution(16147867331220457940)
XLA Ops:
  0.6 0.0 copy-start
  0.6 3.3 %collective-permute-start = (bf16[2,512,768]{2,1,0:T(8,128)(2,1)}, bf16[2,512,768]{2,1,0:T(8,128)(2,1)}, u32[]{:S(2)}, u32[]{:S(2)}) collective-permute-start(bf16[2,512,768]{2,1,0:T(8,128)(2,1)} %act.1), channel_id=1, source_target_pairs={{0,64},{64,0},{1,65},{65,1},{2,66},{66,2},{3,67},{67,3},{4,68},{68... | collective-permute-start | bytes 4718600 | tf_op jit(solution)/shard_map/ppermute | solution.py:196
  4.0 0.1 collective-permute-start.1
  4.1 0.0 copy-done
  4.1 0.1 convert_reduce_fusion
  4.2 1.3 %collective-permute-start.2 = (bf16[72,128]{1,0:T(8,128)(2,1)S(1)}, bf16[72,128]{1,0:T(8,128)(2,1)S(1)}, u32[]{:S(2)}, u32[]{:S(2)}) collective-permute-start(bf16[72,128]{1,0:T(8,128)(2,1)S(1)} %convert_element_type.28), channel_id=1, source_target_pairs={{0,2},{2,0},{4,6},{6,4},{1,3},{3,1},{5,7},{7,5},{8,10},{10,8},{12,... | collective-permute-start | bytes 55304 | tf_op jit(solution)/shard_map/ppermute | solution.py:199
  5.6 5.1 %collective-permute-start.3 = (bf16[72,128]{1,0:T(8,128)(2,1)S(1)}, bf16[72,128]{1,0:T(8,128)(2,1)S(1)}, u32[]{:S(2)}, u32[]{:S(2)}) collective-permute-start(bf16[72,128]{1,0:T(8,128)(2,1)S(1)} %convert_element_type.28), channel_id=1, source_target_pairs={{0,4},{2,6},{4,0},{6,2},{1,5},{3,7},{5,1},{7,3},{8,12},{10,14},{12... | collective-permute-start | bytes 55304 | tf_op jit(solution)/shard_map/ppermute | solution.py:199
  10.7 0.0 collective-permute-start.4
  10.7 0.0 collective-permute-done.peer_act
  10.7 0.0 collective-permute-done.1.peer_bg
  10.7 4.4 %shard_map.59 = bf16[5120,128]{1,0:T(8,128)(2,1)} custom-call(s32[1]{0:T(128)} %bitcast.4.core_ref, bf16[2,512,768]{2,1,0:T(8,128)(2,1)} %act.1, bf16[2,512,768]{2,1,0:T(8,128)(2,1)} %bg.1, bf16[2,512,768]{2,1,0:T(8,128)(2,1)} %collective-permute-done.peer_act, bf16[2,512,768]{2,1,0:T(8,128)(2,1)} %collective-permute-done.1.peer_bg), custom_call_target="tpu_custom_call" | custom-call | flops 2415919104 | bytes 3145728 | tf_op jit(solution)/shard_map/pallas_call | solution.py:204
  15.2 0.0 collective-permute-done.2
  15.2 0.0 collective-permute-done.3
  15.2 0.2 collective-permute-done.4
  15.4 7.5 %all-to-all-start = ((bf16[32,160,128]{2,1,0:T(8,128)(2,1)}), bf16[32,160,128]{2,1,0:T(8,128)(2,1)S(1)}, u32[]{:S(2)}, u32[]{:S(2)}) async-start(bf16[32,160,128]{2,1,0:T(8,128)(2,1)} %bitcast.23), calls=%async_computation | async-start | bytes 2621440 | tf_op jit(solution)/shard_map/all_to_all | solution.py:221
  22.9 2.5 %collective-permute-start.10 = (bf16[4,72,128]{2,1,0:T(8,128)(2,1)S(1)}, bf16[4,72,128]{2,1,0:T(8,128)(2,1)S(1)}, u32[]{:S(2)}, u32[]{:S(2)}) collective-permute-start(bf16[4,72,128]{2,1,0:T(8,128)(2,1)S(1)} %get-tuple-element.37), channel_id=1, source_target_pairs={{0,24},{8,16},{16,8},{24,0},{1,25},{9,17},{17,9},{25,1},{2,26},{10... | collective-permute-start | bytes 221192 | tf_op jit(solution)/shard_map/ppermute | solution.py:199
  25.5 0.6 collective-permute-start.9
  26.0 0.2 collective-permute-start.8
  26.3 12.5 %collective-permute-done.10 = bf16[4,72,128]{2,1,0:T(8,128)(2,1)S(1)} collective-permute-done((bf16[4,72,128]{2,1,0:T(8,128)(2,1)S(1)}, bf16[4,72,128]{2,1,0:T(8,128)(2,1)S(1)}, u32[]{:S(2)}, u32[]{:S(2)}) %collective-permute-start.10) | collective-permute-done | bytes 73760 | tf_op jit(solution)/shard_map/ppermute | solution.py:199
  38.8 3.7 %collective-permute-done.9 = bf16[4,72,128]{2,1,0:T(8,128)(2,1)S(1)} collective-permute-done((bf16[4,72,128]{2,1,0:T(8,128)(2,1)S(1)}, bf16[4,72,128]{2,1,0:T(8,128)(2,1)S(1)}, u32[]{:S(2)}, u32[]{:S(2)}) %collective-permute-start.9) | collective-permute-done | bytes 73760 | tf_op jit(solution)/shard_map/ppermute | solution.py:199
  42.5 0.0 collective-permute-done.8
  42.6 2.2 %collective-permute-start.11 = (bf16[4,4,72,128]{3,2,1,0:T(8,128)(2,1)S(1)}, bf16[4,4,72,128]{3,2,1,0:T(8,128)(2,1)S(1)}, u32[]{:S(2)}, u32[]{:S(2)}) collective-permute-start(bf16[4,4,72,128]{3,2,1,0:T(8,128)(2,1)S(1)} %pad_maximum_fusion.1), channel_id=1, source_target_pairs={{0,160},{160,0},{32,128},{128,32},{1,161},{161,1},{33,129},{129,33... | collective-permute-start | bytes 884744 | tf_op jit(solution)/shard_map/ppermute | solution.py:227
  44.7 0.0 all-to-all-done
  44.7 0.2 reduce_sum.12
  44.9 1.3 %collective-permute-start.5 = (bf16[160,128]{1,0:T(8,128)(2,1)S(1)}, bf16[160,128]{1,0:T(8,128)(2,1)S(1)}, u32[]{:S(2)}, u32[]{:S(2)}) collective-permute-start(bf16[160,128]{1,0:T(8,128)(2,1)S(1)} %reduce_sum.12), channel_id=1, source_target_pairs={{0,2},{2,0},{4,6},{6,4},{1,3},{3,1},{5,7},{7,5},{8,10},{10,8},{12,... | collective-permute-start | bytes 122888 | tf_op jit(solution)/shard_map/ppermute | solution.py:199
  46.2 4.2 %collective-permute-start.6 = (bf16[160,128]{1,0:T(8,128)(2,1)S(1)}, bf16[160,128]{1,0:T(8,128)(2,1)S(1)}, u32[]{:S(2)}, u32[]{:S(2)}) collective-permute-start(bf16[160,128]{1,0:T(8,128)(2,1)S(1)} %reduce_sum.12), channel_id=1, source_target_pairs={{0,4},{2,6},{4,0},{6,2},{1,5},{3,7},{5,1},{7,3},{8,12},{10,14},{12... | collective-permute-start | bytes 122888 | tf_op jit(solution)/shard_map/ppermute | solution.py:199
  50.5 0.2 collective-permute-start.7
  50.7 0.0 collective-permute-done.11
  50.7 0.0 collective-permute-done.5
  50.7 2.3 %collective-permute-done.6 = bf16[160,128]{1,0:T(8,128)(2,1)S(1)} collective-permute-done((bf16[160,128]{1,0:T(8,128)(2,1)S(1)}, bf16[160,128]{1,0:T(8,128)(2,1)S(1)}, u32[]{:S(2)}, u32[]{:S(2)}) %collective-permute-start.6) | collective-permute-done | bytes 40992 | tf_op jit(solution)/shard_map/ppermute | solution.py:199
  53.0 3.8 %collective-permute-done.7 = bf16[160,128]{1,0:T(8,128)(2,1)S(1)} collective-permute-done((bf16[160,128]{1,0:T(8,128)(2,1)S(1)}, bf16[160,128]{1,0:T(8,128)(2,1)S(1)}, u32[]{:S(2)}, u32[]{:S(2)}) %collective-permute-start.7) | collective-permute-done | bytes 40992 | tf_op jit(solution)/shard_map/ppermute | solution.py:199
  56.8 0.2 add_convert_fusion
  56.9 1.3 %broadcast_in_dim.12 = bf16[32,160,128]{2,1,0:T(8,128)(2,1)} broadcast(bf16[160,128]{1,0:T(8,128)(2,1)S(1)} %add_convert_fusion), dimensions={1,2} | broadcast | bytes 1351680 | tf_op jit(solution)/shard_map/broadcast_in_dim | solution.py:241
  58.2 4.6 %all-to-all-start.1 = ((bf16[32,160,128]{2,1,0:T(8,128)(2,1)}), bf16[32,160,128]{2,1,0:T(8,128)(2,1)S(1)}, u32[]{:S(2)}, u32[]{:S(2)}) async-start(bf16[32,160,128]{2,1,0:T(8,128)(2,1)} %broadcast_in_dim.12), calls=%async_computation.1 | async-start | bytes 2621440 | tf_op jit(solution)/shard_map/all_to_all | solution.py:241
  62.8 0.1 stack.62.place
  62.9 0.2 fusion.order
  63.1 0.1 pad_maximum_fusion
  63.2 0.5 reshape.147.grads
  63.7 16.9 %all-to-all-done.1 = bf16[32,160,128]{2,1,0:T(8,128)(2,1)S(1)} async-done(((bf16[32,160,128]{2,1,0:T(8,128)(2,1)}), bf16[32,160,128]{2,1,0:T(8,128)(2,1)S(1)}, u32[]{:S(2)}, u32[]{:S(2)}) %all-to-all-start.1) | async-done | bytes 1310752 | tf_op jit(solution)/shard_map/all_to_all | solution.py:241
  80.6 6.4 %shard_map.60 = (f32[16,1728]{1,0:T(8,128)S(1)}, f32[16,192]{1,0:T(8,128)S(1)}, f32[16,192]{1,0:T(8,128)S(1)}, f32[16,192]{1,0:T(8,128)S(1)}) custom-call(s32[6]{0:T(128)S(1)} %stack.62.place, bf16[5120,128]{1,0:T(8,128)(2,1)S(1)} %bitcast.22, bf16[384,768]{1,0:T(8,128)(2,1)S(1)} %reshape.147.grads, bf16[768,384]{1,0:T(8,128)(2,1)S(1)} %fusion.order), custom_call_target="tpu_custom_call" | custom-call | flops 2717908992 | bytes 4718592 | tf_op jit(solution)/shard_map/pallas_call | solution.py:254
  87.1 3.9 %collective-permute-start.12 = (f32[16,1728]{1,0:T(8,128)S(1)}, f32[16,1728]{1,0:T(8,128)S(1)}, u32[]{:S(2)}, u32[]{:S(2)}) collective-permute-start(f32[16,1728]{1,0:T(8,128)S(1)} %get-tuple-element.30.packed), channel_id=1, source_target_pairs={{0,64},{64,0},{1,65},{65,1},{2,66},{66,2},{3,67},{67,3},{4,68},{68... | collective-permute-start | bytes 331784 | tf_op jit(solution)/shard_map/ppermute | solution.py:264
  91.0 0.5 collective-permute-start.13
  91.5 1.2 %collective-permute-start.14 = (f32[16,192]{1,0:T(8,128)S(1)}, f32[16,192]{1,0:T(8,128)S(1)}, u32[]{:S(2)}, u32[]{:S(2)}) collective-permute-start(f32[16,192]{1,0:T(8,128)S(1)} %get-tuple-element.33), channel_id=1, source_target_pairs={{0,65},{65,0},{1,64},{64,1},{2,67},{67,2},{3,66},{66,3},{4,69},{69... | collective-permute-start | bytes 36872 | tf_op jit(solution)/shard_map/ppermute | solution.py:266
  92.7 0.9 collective-permute-done.13.near
  93.6 1.1 %collective-permute-done.14.cross = f32[16,192]{1,0:T(8,128)S(1)} collective-permute-done((f32[16,192]{1,0:T(8,128)S(1)}, f32[16,192]{1,0:T(8,128)S(1)}, u32[]{:S(2)}, u32[]{:S(2)}) %collective-permute-start.14) | collective-permute-done | bytes 12320 | tf_op jit(solution)/shard_map/ppermute | solution.py:266
  94.6 0.0 collective-permute-done.12.got
  94.6 0.0 copy-done.1
  94.6 1.2 %shard_map.61 = (f32[12,2,192]{2,1,0:T(2,128)}, f32[12,2,768]{2,1,0:T(2,128)}) custom-call(s32[4]{0:T(128)S(1)} %copy-done.1, s32[6]{0:T(128)S(1)} %stack.62.place, f32[16,1728]{1,0:T(8,128)S(1)} %get-tuple-element.30.packed, f32[16,1728]{1,0:T(8,128)S(1)} %collective-permute-done.12.got, f32[16,192]{1,0:T(8,128)S(1)} %get-tuple-element.31.mine, ...), custom_call_target="tpu_custom_call" | custom-call | tf_op jit(solution)/shard_map/pallas_call | solution.py:267
  (7 shorter events, 0.2 us)
Async XLA Ops:
  0.6 3.4 %copy-start = (f32[2,12,768]{2,0,1:T(2,128)S(1)}, f32[2,12,768]{2,0,1:T(2,128)}, u32[]{:S(2)}) copy-start(f32[2,12,768]{2,0,1:T(2,128)} %param.6) | copy-start | bytes 221188
  0.6 10.1 %collective-permute-start = (bf16[2,512,768]{2,1,0:T(8,128)(2,1)}, bf16[2,512,768]{2,1,0:T(8,128)(2,1)}, u32[]{:S(2)}, u32[]{:S(2)}) collective-permute-start(bf16[2,512,768]{2,1,0:T(8,128)(2,1)} %act.1), channel_id=1, source_target_pairs={{0,64},{64,0},{1,65},{65,1},{2,66},{66,2},{3,67},{67,3},{4,68},{68... | collective-permute-start | bytes 4718600 | tf_op jit(solution)/shard_map/ppermute | solution.py:196
  4.0 6.7 %collective-permute-start.1 = (bf16[2,512,768]{2,1,0:T(8,128)(2,1)}, bf16[2,512,768]{2,1,0:T(8,128)(2,1)}, u32[]{:S(2)}, u32[]{:S(2)}) collective-permute-start(bf16[2,512,768]{2,1,0:T(8,128)(2,1)} %bg.1), channel_id=1, source_target_pairs={{0,64},{64,0},{1,65},{65,1},{2,66},{66,2},{3,67},{67,3},{4,68},{68... | collective-permute-start | bytes 4718600 | tf_op jit(solution)/shard_map/ppermute | solution.py:196
  4.2 10.9 %collective-permute-start.2 = (bf16[72,128]{1,0:T(8,128)(2,1)S(1)}, bf16[72,128]{1,0:T(8,128)(2,1)S(1)}, u32[]{:S(2)}, u32[]{:S(2)}) collective-permute-start(bf16[72,128]{1,0:T(8,128)(2,1)S(1)} %convert_element_type.28), channel_id=1, source_target_pairs={{0,2},{2,0},{4,6},{6,4},{1,3},{3,1},{5,7},{7,5},{8,10},{10,8},{12,... | collective-permute-start | bytes 55304 | tf_op jit(solution)/shard_map/ppermute | solution.py:199
  5.6 9.6 %collective-permute-start.3 = (bf16[72,128]{1,0:T(8,128)(2,1)S(1)}, bf16[72,128]{1,0:T(8,128)(2,1)S(1)}, u32[]{:S(2)}, u32[]{:S(2)}) collective-permute-start(bf16[72,128]{1,0:T(8,128)(2,1)S(1)} %convert_element_type.28), channel_id=1, source_target_pairs={{0,4},{2,6},{4,0},{6,2},{1,5},{3,7},{5,1},{7,3},{8,12},{10,14},{12... | collective-permute-start | bytes 55304 | tf_op jit(solution)/shard_map/ppermute | solution.py:199
  10.7 4.7 %collective-permute-start.4 = (bf16[72,128]{1,0:T(8,128)(2,1)S(1)}, bf16[72,128]{1,0:T(8,128)(2,1)S(1)}, u32[]{:S(2)}, u32[]{:S(2)}) collective-permute-start(bf16[72,128]{1,0:T(8,128)(2,1)S(1)} %convert_element_type.28), channel_id=1, source_target_pairs={{0,6},{2,4},{4,2},{6,0},{1,7},{3,5},{5,3},{7,1},{8,14},{10,12},{12... | collective-permute-start | bytes 55304 | tf_op jit(solution)/shard_map/ppermute | solution.py:199
  15.4 29.3 %all-to-all-start = ((bf16[32,160,128]{2,1,0:T(8,128)(2,1)}), bf16[32,160,128]{2,1,0:T(8,128)(2,1)S(1)}, u32[]{:S(2)}, u32[]{:S(2)}) async-start(bf16[32,160,128]{2,1,0:T(8,128)(2,1)} %bitcast.23), calls=%async_computation | async-start | bytes 2621440 | tf_op jit(solution)/shard_map/all_to_all | solution.py:221
  22.9 15.9 %collective-permute-start.10 = (bf16[4,72,128]{2,1,0:T(8,128)(2,1)S(1)}, bf16[4,72,128]{2,1,0:T(8,128)(2,1)S(1)}, u32[]{:S(2)}, u32[]{:S(2)}) collective-permute-start(bf16[4,72,128]{2,1,0:T(8,128)(2,1)S(1)} %get-tuple-element.37), channel_id=1, source_target_pairs={{0,24},{8,16},{16,8},{24,0},{1,25},{9,17},{17,9},{25,1},{2,26},{10... | collective-permute-start | bytes 221192 | tf_op jit(solution)/shard_map/ppermute | solution.py:199
  25.5 17.0 %collective-permute-start.9 = (bf16[4,72,128]{2,1,0:T(8,128)(2,1)S(1)}, bf16[4,72,128]{2,1,0:T(8,128)(2,1)S(1)}, u32[]{:S(2)}, u32[]{:S(2)}) collective-permute-start(bf16[4,72,128]{2,1,0:T(8,128)(2,1)S(1)} %get-tuple-element.37), channel_id=1, source_target_pairs={{0,16},{8,24},{16,0},{24,8},{1,17},{9,25},{17,1},{25,9},{2,18},{10... | collective-permute-start | bytes 221192 | tf_op jit(solution)/shard_map/ppermute | solution.py:199
  26.0 16.5 %collective-permute-start.8 = (bf16[4,72,128]{2,1,0:T(8,128)(2,1)S(1)}, bf16[4,72,128]{2,1,0:T(8,128)(2,1)S(1)}, u32[]{:S(2)}, u32[]{:S(2)}) collective-permute-start(bf16[4,72,128]{2,1,0:T(8,128)(2,1)S(1)} %get-tuple-element.37), channel_id=1, source_target_pairs={{0,8},{8,0},{16,24},{24,16},{1,9},{9,1},{17,25},{25,17},{2,10},{10... | collective-permute-start | bytes 221192 | tf_op jit(solution)/shard_map/ppermute | solution.py:199
  42.6 8.2 %collective-permute-start.11 = (bf16[4,4,72,128]{3,2,1,0:T(8,128)(2,1)S(1)}, bf16[4,4,72,128]{3,2,1,0:T(8,128)(2,1)S(1)}, u32[]{:S(2)}, u32[]{:S(2)}) collective-permute-start(bf16[4,4,72,128]{3,2,1,0:T(8,128)(2,1)S(1)} %pad_maximum_fusion.1), channel_id=1, source_target_pairs={{0,160},{160,0},{32,128},{128,32},{1,161},{161,1},{33,129},{129,33... | collective-permute-start | bytes 884744 | tf_op jit(solution)/shard_map/ppermute | solution.py:227
  44.9 5.8 %collective-permute-start.5 = (bf16[160,128]{1,0:T(8,128)(2,1)S(1)}, bf16[160,128]{1,0:T(8,128)(2,1)S(1)}, u32[]{:S(2)}, u32[]{:S(2)}) collective-permute-start(bf16[160,128]{1,0:T(8,128)(2,1)S(1)} %reduce_sum.12), channel_id=1, source_target_pairs={{0,2},{2,0},{4,6},{6,4},{1,3},{3,1},{5,7},{7,5},{8,10},{10,8},{12,... | collective-permute-start | bytes 122888 | tf_op jit(solution)/shard_map/ppermute | solution.py:199
  46.2 6.8 %collective-permute-start.6 = (bf16[160,128]{1,0:T(8,128)(2,1)S(1)}, bf16[160,128]{1,0:T(8,128)(2,1)S(1)}, u32[]{:S(2)}, u32[]{:S(2)}) collective-permute-start(bf16[160,128]{1,0:T(8,128)(2,1)S(1)} %reduce_sum.12), channel_id=1, source_target_pairs={{0,4},{2,6},{4,0},{6,2},{1,5},{3,7},{5,1},{7,3},{8,12},{10,14},{12... | collective-permute-start | bytes 122888 | tf_op jit(solution)/shard_map/ppermute | solution.py:199
  50.5 6.3 %collective-permute-start.7 = (bf16[160,128]{1,0:T(8,128)(2,1)S(1)}, bf16[160,128]{1,0:T(8,128)(2,1)S(1)}, u32[]{:S(2)}, u32[]{:S(2)}) collective-permute-start(bf16[160,128]{1,0:T(8,128)(2,1)S(1)} %reduce_sum.12), channel_id=1, source_target_pairs={{0,6},{2,4},{4,2},{6,0},{1,7},{3,5},{5,3},{7,1},{8,14},{10,12},{12... | collective-permute-start | bytes 122888 | tf_op jit(solution)/shard_map/ppermute | solution.py:199
  58.2 22.5 %all-to-all-start.1 = ((bf16[32,160,128]{2,1,0:T(8,128)(2,1)}), bf16[32,160,128]{2,1,0:T(8,128)(2,1)S(1)}, u32[]{:S(2)}, u32[]{:S(2)}) async-start(bf16[32,160,128]{2,1,0:T(8,128)(2,1)} %broadcast_in_dim.12), calls=%async_computation.1 | async-start | bytes 2621440 | tf_op jit(solution)/shard_map/all_to_all | solution.py:241
  80.6 14.0 %copy-start.1 = (s32[4]{0:T(128)S(1)}, s32[4]{0:T(128)}, u32[]{:S(2)}) copy-start(s32[4]{0:T(128)} %owners.1) | copy-start | bytes 52
  87.1 7.5 %collective-permute-start.12 = (f32[16,1728]{1,0:T(8,128)S(1)}, f32[16,1728]{1,0:T(8,128)S(1)}, u32[]{:S(2)}, u32[]{:S(2)}) collective-permute-start(f32[16,1728]{1,0:T(8,128)S(1)} %get-tuple-element.30.packed), channel_id=1, source_target_pairs={{0,64},{64,0},{1,65},{65,1},{2,66},{66,2},{3,67},{67,3},{4,68},{68... | collective-permute-start | bytes 331784 | tf_op jit(solution)/shard_map/ppermute | solution.py:264
  91.0 2.6 %collective-permute-start.13 = (f32[16,192]{1,0:T(8,128)S(1)}, f32[16,192]{1,0:T(8,128)S(1)}, u32[]{:S(2)}, u32[]{:S(2)}) collective-permute-start(f32[16,192]{1,0:T(8,128)S(1)} %get-tuple-element.32), channel_id=1, source_target_pairs={{0,1},{1,0},{2,3},{3,2},{4,5},{5,4},{6,7},{7,6},{8,9},{9,8},{10,11... | collective-permute-start | bytes 36872 | tf_op jit(solution)/shard_map/ppermute | solution.py:265
  91.5 3.2 %collective-permute-start.14 = (f32[16,192]{1,0:T(8,128)S(1)}, f32[16,192]{1,0:T(8,128)S(1)}, u32[]{:S(2)}, u32[]{:S(2)}) collective-permute-start(f32[16,192]{1,0:T(8,128)S(1)} %get-tuple-element.33), channel_id=1, source_target_pairs={{0,65},{65,0},{1,64},{64,1},{2,67},{67,2},{3,66},{66,3},{4,69},{69... | collective-permute-start | bytes 36872 | tf_op jit(solution)/shard_map/ppermute | solution.py:266

commit v5 on v4

--- a/solution.py
+++ b/solution.py
@@ -86,8 +86,8 @@
     return jnp.where((c == at * count + r) & (r < count), 1.0, 0.0).astype(f32)
 
 
-def finish_kernel(place, blocks, grads, order, packed, mine_out, near_out, cross_out, mats):
-    feat = order.shape[0]
+def finish_kernel(place, blocks, grads, packed, mine_out, near_out, cross_out, mats):
+    feat = grads.shape[0]
     pairs = upper(feat // TILE)
     mid = TILE // 2
 
@@ -135,8 +135,7 @@
     rows = chain(jnp.concatenate([eye, eye_rows(place[1], place[2], own, feat)], axis=0), odd, odd_inv)
     packed[:, feat : 2 * feat] = rows[:own]
     even_inv = matrices(0, even)
-    left = dot(halves(rows), order[...]).astype(bf16)
-    v = times(left, grads[...])
+    v = times(halves(rows), grads[...])
     both = chain(jnp.concatenate([v, eye], axis=0), even, even_inv)
     packed[:, :feat] = both[2 * own :]
 
@@ -248,18 +247,19 @@
     from_xh = (step // (nzh * ny)) ^ xh
     to = (((from_xh * ny + from_y) * nzh + from_zh) * nzl + zl) * nrow + k % nrow
     order = (jnp.arange(feat)[:, None] == to[None, :]).astype(bf16)
+    whole = dot(order, part).astype(bf16)
 
     own = 16
     place = jnp.stack([dp, dp ^ 1, jnp.int32(nrow), group, xl * ncore + 1 - core, core])
     packed, mine, near, cross = pl.pallas_call(
         finish_kernel,
         out_shape=[jax.ShapeDtypeStruct((own, n), f32) for n in (2 * feat + cols, cols, cols, cols)],
-        in_specs=[sm, vm, vm, vm],
+        in_specs=[sm, vm, vm],
         out_specs=[vm] * 4,
         scratch_shapes=[pltpu.VMEM((2, 3, feat, feat), bf16)],
         compiler_params=params,
         cost_estimate=pl.CostEstimate(flops=6 * feat**3, bytes_accessed=8 * feat * feat, transcendentals=0),
-    )(place, blocks.reshape(2 * nblk * TILE, TILE), part, order)
+    )(place, blocks.reshape(2 * nblk * TILE, TILE), whole)
 
     got = lax.ppermute(packed, "core", swap)
     near = lax.ppermute(near, "zl", swap)

time: 96.2 us -> 96.1 us (level)
  transfers between devices with their start and end apart: 17 -> 17, of which waited for: 8 -> 8; matrix products, arithmetic and copies ran while one was open for 1% -> 2% of each run, Pallas kernels for 5% -> 5%
where the time goes in v5:
time: 96.1 us; the launch traced here: 95.8 us
  waiting for transfers between devices  40.8 us (42%)
  starting transfers between devices  38.8 us (40%)
  Pallas kernels  12 us (12%)
  local copies, waits for them, and re-layouts  2.01 us (2%)
    ppermute x9, waiting for transfers between devices, along(): lax.ppermute(a, axis, [(i, i ^ e) for i in range(size)])  22.5 us
    all_to_all x1, waiting for transfers between devices, shards(): lax.all_to_all(jnp.broadcast_to(damped[None], (share, rows, TILE)), XYL,...  16.4 us
    ppermute x9, starting transfers between devices, along(): lax.ppermute(a, axis, [(i, i ^ e) for i in range(size)])  15.5 us
    all_to_all x1, starting transfers between devices, shards(): lax.all_to_all(partial.reshape(share, rows, TILE), XYL, 0, 0, tiled=True)  7.49 us
    pallas_call x1, Pallas kernels, shards(): pl.pallas_call(finish_kernel, out_shape=[jax.ShapeDtypeStruct((own, n), f...  6.32 us
    all_to_all x1, starting transfers between devices, shards(): lax.all_to_all(jnp.broadcast_to(damped[None], (share, rows, TILE)), XYL,...  4.58 us
    pallas_call x1, Pallas kernels, shards(): pl.pallas_call(factor_kernel, out_shape=jax.ShapeDtypeStruct((2 * nblk *...  4.44 us
    ppermute x1, starting transfers between devices, shards(): got = lax.ppermute(packed, 'core', swap)  3.88 us
  transfers between devices with their start and end apart: 17, of which 8 were waited for; matrix products, arithmetic and copies ran while one was open for 2% of the time, Pallas kernels for 5%

profile of v5, /device:TPU:1, one launch (start us, length us, event | category | flops | bytes accessed | tf_op | source)
XLA Modules:
  0.0 95.8 jit_solution(17512654709141996088)
XLA Ops:
  0.6 0.0 copy-start
  0.6 3.3 %collective-permute-start = (bf16[2,512,768]{2,1,0:T(8,128)(2,1)}, bf16[2,512,768]{2,1,0:T(8,128)(2,1)}, u32[]{:S(2)}, u32[]{:S(2)}) collective-permute-start(bf16[2,512,768]{2,1,0:T(8,128)(2,1)} %act.1), channel_id=1, source_target_pairs={{0,64},{64,0},{1,65},{65,1},{2,66},{66,2},{3,67},{67,3},{4,68},{68... | collective-permute-start | bytes 4718600 | tf_op jit(solution)/shard_map/ppermute | solution.py:195
  4.0 0.1 collective-permute-start.1
  4.1 0.0 copy-done
  4.1 0.1 convert_reduce_fusion
  4.2 1.3 %collective-permute-start.2 = (bf16[72,128]{1,0:T(8,128)(2,1)S(1)}, bf16[72,128]{1,0:T(8,128)(2,1)S(1)}, u32[]{:S(2)}, u32[]{:S(2)}) collective-permute-start(bf16[72,128]{1,0:T(8,128)(2,1)S(1)} %convert_element_type.29), channel_id=1, source_target_pairs={{0,2},{2,0},{4,6},{6,4},{1,3},{3,1},{5,7},{7,5},{8,10},{10,8},{12,... | collective-permute-start | bytes 55304 | tf_op jit(solution)/shard_map/ppermute | solution.py:198
  5.6 5.1 %collective-permute-start.3 = (bf16[72,128]{1,0:T(8,128)(2,1)S(1)}, bf16[72,128]{1,0:T(8,128)(2,1)S(1)}, u32[]{:S(2)}, u32[]{:S(2)}) collective-permute-start(bf16[72,128]{1,0:T(8,128)(2,1)S(1)} %convert_element_type.29), channel_id=1, source_target_pairs={{0,4},{2,6},{4,0},{6,2},{1,5},{3,7},{5,1},{7,3},{8,12},{10,14},{12... | collective-permute-start | bytes 55304 | tf_op jit(solution)/shard_map/ppermute | solution.py:198
  10.7 0.0 collective-permute-start.4
  10.7 0.0 collective-permute-done.peer_act
  10.7 0.0 collective-permute-done.1.peer_bg
  10.7 4.4 %shard_map.59 = bf16[5120,128]{1,0:T(8,128)(2,1)} custom-call(s32[1]{0:T(128)} %bitcast.4.core_ref, bf16[2,512,768]{2,1,0:T(8,128)(2,1)} %act.1, bf16[2,512,768]{2,1,0:T(8,128)(2,1)} %bg.1, bf16[2,512,768]{2,1,0:T(8,128)(2,1)} %collective-permute-done.peer_act, bf16[2,512,768]{2,1,0:T(8,128)(2,1)} %collective-permute-done.1.peer_bg), custom_call_target="tpu_custom_call" | custom-call | flops 2415919104 | bytes 3145728 | tf_op jit(solution)/shard_map/pallas_call | solution.py:203
  15.2 0.0 collective-permute-done.2
  15.2 0.0 collective-permute-done.3
  15.2 0.2 collective-permute-done.4
  15.4 7.5 %all-to-all-start = ((bf16[32,160,128]{2,1,0:T(8,128)(2,1)}), bf16[32,160,128]{2,1,0:T(8,128)(2,1)S(1)}, u32[]{:S(2)}, u32[]{:S(2)}) async-start(bf16[32,160,128]{2,1,0:T(8,128)(2,1)} %bitcast.24), calls=%async_computation | async-start | bytes 2621440 | tf_op jit(solution)/shard_map/all_to_all | solution.py:220
  22.9 2.5 %collective-permute-start.10 = (bf16[4,72,128]{2,1,0:T(8,128)(2,1)S(1)}, bf16[4,72,128]{2,1,0:T(8,128)(2,1)S(1)}, u32[]{:S(2)}, u32[]{:S(2)}) collective-permute-start(bf16[4,72,128]{2,1,0:T(8,128)(2,1)S(1)} %get-tuple-element.37), channel_id=1, source_target_pairs={{0,24},{8,16},{16,8},{24,0},{1,25},{9,17},{17,9},{25,1},{2,26},{10... | collective-permute-start | bytes 221192 | tf_op jit(solution)/shard_map/ppermute | solution.py:198
  25.5 0.6 collective-permute-start.9
  26.0 0.2 collective-permute-start.8
  26.3 12.5 %collective-permute-done.10 = bf16[4,72,128]{2,1,0:T(8,128)(2,1)S(1)} collective-permute-done((bf16[4,72,128]{2,1,0:T(8,128)(2,1)S(1)}, bf16[4,72,128]{2,1,0:T(8,128)(2,1)S(1)}, u32[]{:S(2)}, u32[]{:S(2)}) %collective-permute-start.10) | collective-permute-done | bytes 73760 | tf_op jit(solution)/shard_map/ppermute | solution.py:198
  38.8 3.7 %collective-permute-done.9 = bf16[4,72,128]{2,1,0:T(8,128)(2,1)S(1)} collective-permute-done((bf16[4,72,128]{2,1,0:T(8,128)(2,1)S(1)}, bf16[4,72,128]{2,1,0:T(8,128)(2,1)S(1)}, u32[]{:S(2)}, u32[]{:S(2)}) %collective-permute-start.9) | collective-permute-done | bytes 73760 | tf_op jit(solution)/shard_map/ppermute | solution.py:198
  42.5 0.0 collective-permute-done.8
  42.6 2.2 %collective-permute-start.11 = (bf16[4,4,72,128]{3,2,1,0:T(8,128)(2,1)S(1)}, bf16[4,4,72,128]{3,2,1,0:T(8,128)(2,1)S(1)}, u32[]{:S(2)}, u32[]{:S(2)}) collective-permute-start(bf16[4,4,72,128]{3,2,1,0:T(8,128)(2,1)S(1)} %pad_maximum_fusion.1), channel_id=1, source_target_pairs={{0,160},{160,0},{32,128},{128,32},{1,161},{161,1},{33,129},{129,33... | collective-permute-start | bytes 884744 | tf_op jit(solution)/shard_map/ppermute | solution.py:226
  44.7 0.0 all-to-all-done
  44.7 0.2 reduce_sum.12
  44.9 1.3 %collective-permute-start.5 = (bf16[160,128]{1,0:T(8,128)(2,1)S(1)}, bf16[160,128]{1,0:T(8,128)(2,1)S(1)}, u32[]{:S(2)}, u32[]{:S(2)}) collective-permute-start(bf16[160,128]{1,0:T(8,128)(2,1)S(1)} %reduce_sum.12), channel_id=1, source_target_pairs={{0,2},{2,0},{4,6},{6,4},{1,3},{3,1},{5,7},{7,5},{8,10},{10,8},{12,... | collective-permute-start | bytes 122888 | tf_op jit(solution)/shard_map/ppermute | solution.py:198
  46.2 4.2 %collective-permute-start.6 = (bf16[160,128]{1,0:T(8,128)(2,1)S(1)}, bf16[160,128]{1,0:T(8,128)(2,1)S(1)}, u32[]{:S(2)}, u32[]{:S(2)}) collective-permute-start(bf16[160,128]{1,0:T(8,128)(2,1)S(1)} %reduce_sum.12), channel_id=1, source_target_pairs={{0,4},{2,6},{4,0},{6,2},{1,5},{3,7},{5,1},{7,3},{8,12},{10,14},{12... | collective-permute-start | bytes 122888 | tf_op jit(solution)/shard_map/ppermute | solution.py:198
  50.5 0.2 collective-permute-start.7
  50.7 0.0 collective-permute-done.11
  50.7 0.0 collective-permute-done.5
  50.7 2.3 %collective-permute-done.6 = bf16[160,128]{1,0:T(8,128)(2,1)S(1)} collective-permute-done((bf16[160,128]{1,0:T(8,128)(2,1)S(1)}, bf16[160,128]{1,0:T(8,128)(2,1)S(1)}, u32[]{:S(2)}, u32[]{:S(2)}) %collective-permute-start.6) | collective-permute-done | bytes 40992 | tf_op jit(solution)/shard_map/ppermute | solution.py:198
  53.0 3.8 %collective-permute-done.7 = bf16[160,128]{1,0:T(8,128)(2,1)S(1)} collective-permute-done((bf16[160,128]{1,0:T(8,128)(2,1)S(1)}, bf16[160,128]{1,0:T(8,128)(2,1)S(1)}, u32[]{:S(2)}, u32[]{:S(2)}) %collective-permute-start.7) | collective-permute-done | bytes 40992 | tf_op jit(solution)/shard_map/ppermute | solution.py:198
  56.8 0.2 add_convert_fusion
  56.9 1.3 %broadcast_in_dim.12 = bf16[32,160,128]{2,1,0:T(8,128)(2,1)} broadcast(bf16[160,128]{1,0:T(8,128)(2,1)S(1)} %add_convert_fusion), dimensions={1,2} | broadcast | bytes 1351680 | tf_op jit(solution)/shard_map/broadcast_in_dim | solution.py:240
  58.2 4.6 %all-to-all-start.1 = ((bf16[32,160,128]{2,1,0:T(8,128)(2,1)}), bf16[32,160,128]{2,1,0:T(8,128)(2,1)S(1)}, u32[]{:S(2)}, u32[]{:S(2)}) async-start(bf16[32,160,128]{2,1,0:T(8,128)(2,1)} %broadcast_in_dim.12), calls=%async_computation.1 | async-start | bytes 2621440 | tf_op jit(solution)/shard_map/all_to_all | solution.py:240
  62.8 0.1 stack.62.place
  62.9 0.1 pad_maximum_fusion
  63.0 0.5 reshape.147
  63.5 0.8 convolution_convert_fusion.grads
  64.3 16.4 %all-to-all-done.1 = bf16[32,160,128]{2,1,0:T(8,128)(2,1)S(1)} async-done(((bf16[32,160,128]{2,1,0:T(8,128)(2,1)}), bf16[32,160,128]{2,1,0:T(8,128)(2,1)S(1)}, u32[]{:S(2)}, u32[]{:S(2)}) %all-to-all-start.1) | async-done | bytes 1310752 | tf_op jit(solution)/shard_map/all_to_all | solution.py:240
  80.6 6.3 %shard_map.60 = (f32[16,1728]{1,0:T(8,128)S(1)}, f32[16,192]{1,0:T(8,128)S(1)}, f32[16,192]{1,0:T(8,128)S(1)}, f32[16,192]{1,0:T(8,128)S(1)}) custom-call(s32[6]{0:T(128)S(1)} %stack.62.place, bf16[5120,128]{1,0:T(8,128)(2,1)S(1)} %bitcast.23, bf16[768,768]{1,0:T(8,128)(2,1)S(1)} %convolution_convert_fusion.grads), custom_call_target="tpu_custom_call" | custom-call | flops 2717908992 | bytes 4718592 | tf_op jit(solution)/shard_map/pallas_call | solution.py:254
  87.0 3.9 %collective-permute-start.12 = (f32[16,1728]{1,0:T(8,128)S(1)}, f32[16,1728]{1,0:T(8,128)S(1)}, u32[]{:S(2)}, u32[]{:S(2)}) collective-permute-start(f32[16,1728]{1,0:T(8,128)S(1)} %get-tuple-element.30.packed), channel_id=1, source_target_pairs={{0,64},{64,0},{1,65},{65,1},{2,66},{66,2},{3,67},{67,3},{4,68},{68... | collective-permute-start | bytes 331784 | tf_op jit(solution)/shard_map/ppermute | solution.py:264
  90.9 0.5 collective-permute-start.13
  91.4 1.2 %collective-permute-start.14 = (f32[16,192]{1,0:T(8,128)S(1)}, f32[16,192]{1,0:T(8,128)S(1)}, u32[]{:S(2)}, u32[]{:S(2)}) collective-permute-start(f32[16,192]{1,0:T(8,128)S(1)} %get-tuple-element.33), channel_id=1, source_target_pairs={{0,65},{65,0},{1,64},{64,1},{2,67},{67,2},{3,66},{66,3},{4,69},{69... | collective-permute-start | bytes 36872 | tf_op jit(solution)/shard_map/ppermute | solution.py:266
  92.6 0.9 collective-permute-done.13.near
  93.5 1.1 %collective-permute-done.14.cross = f32[16,192]{1,0:T(8,128)S(1)} collective-permute-done((f32[16,192]{1,0:T(8,128)S(1)}, f32[16,192]{1,0:T(8,128)S(1)}, u32[]{:S(2)}, u32[]{:S(2)}) %collective-permute-start.14) | collective-permute-done | bytes 12320 | tf_op jit(solution)/shard_map/ppermute | solution.py:266
  94.5 0.0 collective-permute-done.12.got
  94.5 0.0 copy-done.1
  94.5 1.2 %shard_map.61 = (f32[12,2,192]{2,1,0:T(2,128)}, f32[12,2,768]{2,1,0:T(2,128)}) custom-call(s32[4]{0:T(128)S(1)} %copy-done.1, s32[6]{0:T(128)S(1)} %stack.62.place, f32[16,1728]{1,0:T(8,128)S(1)} %get-tuple-element.30.packed, f32[16,1728]{1,0:T(8,128)S(1)} %collective-permute-done.12.got, f32[16,192]{1,0:T(8,128)S(1)} %get-tuple-element.31.mine, ...), custom_call_target="tpu_custom_call" | custom-call | tf_op jit(solution)/shard_map/pallas_call | solution.py:267
  (7 shorter events, 0.2 us)
Async XLA Ops:
  0.6 3.4 %copy-start = (f32[2,12,768]{2,0,1:T(2,128)S(1)}, f32[2,12,768]{2,0,1:T(2,128)}, u32[]{:S(2)}) copy-start(f32[2,12,768]{2,0,1:T(2,128)} %param.6) | copy-start | bytes 221188
  0.6 10.1 %collective-permute-start = (bf16[2,512,768]{2,1,0:T(8,128)(2,1)}, bf16[2,512,768]{2,1,0:T(8,128)(2,1)}, u32[]{:S(2)}, u32[]{:S(2)}) collective-permute-start(bf16[2,512,768]{2,1,0:T(8,128)(2,1)} %act.1), channel_id=1, source_target_pairs={{0,64},{64,0},{1,65},{65,1},{2,66},{66,2},{3,67},{67,3},{4,68},{68... | collective-permute-start | bytes 4718600 | tf_op jit(solution)/shard_map/ppermute | solution.py:195
  4.0 6.7 %collective-permute-start.1 = (bf16[2,512,768]{2,1,0:T(8,128)(2,1)}, bf16[2,512,768]{2,1,0:T(8,128)(2,1)}, u32[]{:S(2)}, u32[]{:S(2)}) collective-permute-start(bf16[2,512,768]{2,1,0:T(8,128)(2,1)} %bg.1), channel_id=1, source_target_pairs={{0,64},{64,0},{1,65},{65,1},{2,66},{66,2},{3,67},{67,3},{4,68},{68... | collective-permute-start | bytes 4718600 | tf_op jit(solution)/shard_map/ppermute | solution.py:195
  4.2 10.9 %collective-permute-start.2 = (bf16[72,128]{1,0:T(8,128)(2,1)S(1)}, bf16[72,128]{1,0:T(8,128)(2,1)S(1)}, u32[]{:S(2)}, u32[]{:S(2)}) collective-permute-start(bf16[72,128]{1,0:T(8,128)(2,1)S(1)} %convert_element_type.29), channel_id=1, source_target_pairs={{0,2},{2,0},{4,6},{6,4},{1,3},{3,1},{5,7},{7,5},{8,10},{10,8},{12,... | collective-permute-start | bytes 55304 | tf_op jit(solution)/shard_map/ppermute | solution.py:198
  5.6 9.6 %collective-permute-start.3 = (bf16[72,128]{1,0:T(8,128)(2,1)S(1)}, bf16[72,128]{1,0:T(8,128)(2,1)S(1)}, u32[]{:S(2)}, u32[]{:S(2)}) collective-permute-start(bf16[72,128]{1,0:T(8,128)(2,1)S(1)} %convert_element_type.29), channel_id=1, source_target_pairs={{0,4},{2,6},{4,0},{6,2},{1,5},{3,7},{5,1},{7,3},{8,12},{10,14},{12... | collective-permute-start | bytes 55304 | tf_op jit(solution)/shard_map/ppermute | solution.py:198
  10.7 4.7 %collective-permute-start.4 = (bf16[72,128]{1,0:T(8,128)(2,1)S(1)}, bf16[72,128]{1,0:T(8,128)(2,1)S(1)}, u32[]{:S(2)}, u32[]{:S(2)}) collective-permute-start(bf16[72,128]{1,0:T(8,128)(2,1)S(1)} %convert_element_type.29), channel_id=1, source_target_pairs={{0,6},{2,4},{4,2},{6,0},{1,7},{3,5},{5,3},{7,1},{8,14},{10,12},{12... | collective-permute-start | bytes 55304 | tf_op jit(solution)/shard_map/ppermute | solution.py:198
  15.4 29.3 %all-to-all-start = ((bf16[32,160,128]{2,1,0:T(8,128)(2,1)}), bf16[32,160,128]{2,1,0:T(8,128)(2,1)S(1)}, u32[]{:S(2)}, u32[]{:S(2)}) async-start(bf16[32,160,128]{2,1,0:T(8,128)(2,1)} %bitcast.24), calls=%async_computation | async-start | bytes 2621440 | tf_op jit(solution)/shard_map/all_to_all | solution.py:220
  22.9 15.9 %collective-permute-start.10 = (bf16[4,72,128]{2,1,0:T(8,128)(2,1)S(1)}, bf16[4,72,128]{2,1,0:T(8,128)(2,1)S(1)}, u32[]{:S(2)}, u32[]{:S(2)}) collective-permute-start(bf16[4,72,128]{2,1,0:T(8,128)(2,1)S(1)} %get-tuple-element.37), channel_id=1, source_target_pairs={{0,24},{8,16},{16,8},{24,0},{1,25},{9,17},{17,9},{25,1},{2,26},{10... | collective-permute-start | bytes 221192 | tf_op jit(solution)/shard_map/ppermute | solution.py:198
  25.5 17.0 %collective-permute-start.9 = (bf16[4,72,128]{2,1,0:T(8,128)(2,1)S(1)}, bf16[4,72,128]{2,1,0:T(8,128)(2,1)S(1)}, u32[]{:S(2)}, u32[]{:S(2)}) collective-permute-start(bf16[4,72,128]{2,1,0:T(8,128)(2,1)S(1)} %get-tuple-element.37), channel_id=1, source_target_pairs={{0,16},{8,24},{16,0},{24,8},{1,17},{9,25},{17,1},{25,9},{2,18},{10... | collective-permute-start | bytes 221192 | tf_op jit(solution)/shard_map/ppermute | solution.py:198
  26.0 16.5 %collective-permute-start.8 = (bf16[4,72,128]{2,1,0:T(8,128)(2,1)S(1)}, bf16[4,72,128]{2,1,0:T(8,128)(2,1)S(1)}, u32[]{:S(2)}, u32[]{:S(2)}) collective-permute-start(bf16[4,72,128]{2,1,0:T(8,128)(2,1)S(1)} %get-tuple-element.37), channel_id=1, source_target_pairs={{0,8},{8,0},{16,24},{24,16},{1,9},{9,1},{17,25},{25,17},{2,10},{10... | collective-permute-start | bytes 221192 | tf_op jit(solution)/shard_map/ppermute | solution.py:198
  42.6 8.2 %collective-permute-start.11 = (bf16[4,4,72,128]{3,2,1,0:T(8,128)(2,1)S(1)}, bf16[4,4,72,128]{3,2,1,0:T(8,128)(2,1)S(1)}, u32[]{:S(2)}, u32[]{:S(2)}) collective-permute-start(bf16[4,4,72,128]{3,2,1,0:T(8,128)(2,1)S(1)} %pad_maximum_fusion.1), channel_id=1, source_target_pairs={{0,160},{160,0},{32,128},{128,32},{1,161},{161,1},{33,129},{129,33... | collective-permute-start | bytes 884744 | tf_op jit(solution)/shard_map/ppermute | solution.py:226
  44.9 5.8 %collective-permute-start.5 = (bf16[160,128]{1,0:T(8,128)(2,1)S(1)}, bf16[160,128]{1,0:T(8,128)(2,1)S(1)}, u32[]{:S(2)}, u32[]{:S(2)}) collective-permute-start(bf16[160,128]{1,0:T(8,128)(2,1)S(1)} %reduce_sum.12), channel_id=1, source_target_pairs={{0,2},{2,0},{4,6},{6,4},{1,3},{3,1},{5,7},{7,5},{8,10},{10,8},{12,... | collective-permute-start | bytes 122888 | tf_op jit(solution)/shard_map/ppermute | solution.py:198
  46.2 6.8 %collective-permute-start.6 = (bf16[160,128]{1,0:T(8,128)(2,1)S(1)}, bf16[160,128]{1,0:T(8,128)(2,1)S(1)}, u32[]{:S(2)}, u32[]{:S(2)}) collective-permute-start(bf16[160,128]{1,0:T(8,128)(2,1)S(1)} %reduce_sum.12), channel_id=1, source_target_pairs={{0,4},{2,6},{4,0},{6,2},{1,5},{3,7},{5,1},{7,3},{8,12},{10,14},{12... | collective-permute-start | bytes 122888 | tf_op jit(solution)/shard_map/ppermute | solution.py:198
  50.5 6.3 %collective-permute-start.7 = (bf16[160,128]{1,0:T(8,128)(2,1)S(1)}, bf16[160,128]{1,0:T(8,128)(2,1)S(1)}, u32[]{:S(2)}, u32[]{:S(2)}) collective-permute-start(bf16[160,128]{1,0:T(8,128)(2,1)S(1)} %reduce_sum.12), channel_id=1, source_target_pairs={{0,6},{2,4},{4,2},{6,0},{1,7},{3,5},{5,3},{7,1},{8,14},{10,12},{12... | collective-permute-start | bytes 122888 | tf_op jit(solution)/shard_map/ppermute | solution.py:198
  58.2 22.5 %all-to-all-start.1 = ((bf16[32,160,128]{2,1,0:T(8,128)(2,1)}), bf16[32,160,128]{2,1,0:T(8,128)(2,1)S(1)}, u32[]{:S(2)}, u32[]{:S(2)}) async-start(bf16[32,160,128]{2,1,0:T(8,128)(2,1)} %broadcast_in_dim.12), calls=%async_computation.1 | async-start | bytes 2621440 | tf_op jit(solution)/shard_map/all_to_all | solution.py:240
  80.6 13.9 %copy-start.1 = (s32[4]{0:T(128)S(1)}, s32[4]{0:T(128)}, u32[]{:S(2)}) copy-start(s32[4]{0:T(128)} %owners.1) | copy-start | bytes 52
  87.0 7.6 %collective-permute-start.12 = (f32[16,1728]{1,0:T(8,128)S(1)}, f32[16,1728]{1,0:T(8,128)S(1)}, u32[]{:S(2)}, u32[]{:S(2)}) collective-permute-start(f32[16,1728]{1,0:T(8,128)S(1)} %get-tuple-element.30.packed), channel_id=1, source_target_pairs={{0,64},{64,0},{1,65},{65,1},{2,66},{66,2},{3,67},{67,3},{4,68},{68... | collective-permute-start | bytes 331784 | tf_op jit(solution)/shard_map/ppermute | solution.py:264
  90.9 2.6 %collective-permute-start.13 = (f32[16,192]{1,0:T(8,128)S(1)}, f32[16,192]{1,0:T(8,128)S(1)}, u32[]{:S(2)}, u32[]{:S(2)}) collective-permute-start(f32[16,192]{1,0:T(8,128)S(1)} %get-tuple-element.32), channel_id=1, source_target_pairs={{0,1},{1,0},{2,3},{3,2},{4,5},{5,4},{6,7},{7,6},{8,9},{9,8},{10,11... | collective-permute-start | bytes 36872 | tf_op jit(solution)/shard_map/ppermute | solution.py:265
  91.4 3.2 %collective-permute-start.14 = (f32[16,192]{1,0:T(8,128)S(1)}, f32[16,192]{1,0:T(8,128)S(1)}, u32[]{:S(2)}, u32[]{:S(2)}) collective-permute-start(f32[16,192]{1,0:T(8,128)S(1)} %get-tuple-element.33), channel_id=1, source_target_pairs={{0,65},{65,0},{1,64},{64,1},{2,67},{67,2},{3,66},{66,3},{4,69},{69... | collective-permute-start | bytes 36872 | tf_op jit(solution)/shard_map/ppermute | solution.py:266

commit v6 on v5

--- a/solution.py
+++ b/solution.py
@@ -236,8 +236,8 @@
     spot = jnp.arange(TILE)[None, :]
     on = within(range(nb - 1))[:, None] & ((at % TILE)[:, None] == spot)
     on |= within((0, 1))[:, None] & ((at % TILE - TILE // 2)[:, None] == spot)
-    damped = (factor + jnp.where(on, DAMPING, 0.0)).astype(bf16)
-    blocks = lax.all_to_all(jnp.broadcast_to(damped[None], (share, rows, TILE)), XYL, 0, 0, tiled=True)
+    damped = jnp.broadcast_to((factor + jnp.where(on, DAMPING, 0.0))[None], (share, rows, TILE)).astype(bf16)
+    blocks = lax.all_to_all(damped, XYL, 0, 0, tiled=True)
     half = feat // nzl
     part = jnp.stack(g).reshape(half, feat)
     k = jnp.arange(half)

time: 96.1 us -> 96.1 us (level)
  no operation moved by 1% of the time
where the time goes in v6:
time: 96.1 us; the launch traced here: 95.8 us
  waiting for transfers between devices  40.8 us (42%)
  starting transfers between devices  38.8 us (40%)
  Pallas kernels  12 us (12%)
  local copies, waits for them, and re-layouts  2.01 us (2%)
    ppermute x9, waiting for transfers between devices, along(): lax.ppermute(a, axis, [(i, i ^ e) for i in range(size)])  22.5 us
    all_to_all x1, waiting for transfers between devices, shards(): blocks = lax.all_to_all(damped, XYL, 0, 0, tiled=True)  16.4 us
    ppermute x9, starting transfers between devices, along(): lax.ppermute(a, axis, [(i, i ^ e) for i in range(size)])  15.5 us
    all_to_all x1, starting transfers between devices, shards(): lax.all_to_all(partial.reshape(share, rows, TILE), XYL, 0, 0, tiled=True)  7.49 us
    pallas_call x1, Pallas kernels, shards(): pl.pallas_call(finish_kernel, out_shape=[jax.ShapeDtypeStruct((own, n), f...  6.32 us
    all_to_all x1, starting transfers between devices, shards(): blocks = lax.all_to_all(damped, XYL, 0, 0, tiled=True)  4.58 us
    pallas_call x1, Pallas kernels, shards(): pl.pallas_call(factor_kernel, out_shape=jax.ShapeDtypeStruct((2 * nblk *...  4.44 us
    ppermute x1, starting transfers between devices, shards(): got = lax.ppermute(packed, 'core', swap)  3.88 us
  transfers between devices with their start and end apart: 17, of which 8 were waited for; matrix products, arithmetic and copies ran while one was open for 2% of the time, Pallas kernels for 5%

profile of v6, /device:TPU:1, one launch (start us, length us, event | category | flops | bytes accessed | tf_op | source)
XLA Modules:
  0.0 95.8 jit_solution(17512654709141996088)
XLA Ops:
  0.6 0.0 copy-start
  0.6 3.3 %collective-permute-start = (bf16[2,512,768]{2,1,0:T(8,128)(2,1)}, bf16[2,512,768]{2,1,0:T(8,128)(2,1)}, u32[]{:S(2)}, u32[]{:S(2)}) collective-permute-start(bf16[2,512,768]{2,1,0:T(8,128)(2,1)} %act.1), channel_id=1, source_target_pairs={{0,64},{64,0},{1,65},{65,1},{2,66},{66,2},{3,67},{67,3},{4,68},{68... | collective-permute-start | bytes 4718600 | tf_op jit(solution)/shard_map/ppermute | solution.py:195
  4.0 0.1 collective-permute-start.1
  4.1 0.0 copy-done
  4.1 0.1 convert_reduce_fusion
  4.2 1.3 %collective-permute-start.2 = (bf16[72,128]{1,0:T(8,128)(2,1)S(1)}, bf16[72,128]{1,0:T(8,128)(2,1)S(1)}, u32[]{:S(2)}, u32[]{:S(2)}) collective-permute-start(bf16[72,128]{1,0:T(8,128)(2,1)S(1)} %convert_element_type.30), channel_id=1, source_target_pairs={{0,2},{2,0},{4,6},{6,4},{1,3},{3,1},{5,7},{7,5},{8,10},{10,8},{12,... | collective-permute-start | bytes 55304 | tf_op jit(solution)/shard_map/ppermute | solution.py:198
  5.6 5.1 %collective-permute-start.3 = (bf16[72,128]{1,0:T(8,128)(2,1)S(1)}, bf16[72,128]{1,0:T(8,128)(2,1)S(1)}, u32[]{:S(2)}, u32[]{:S(2)}) collective-permute-start(bf16[72,128]{1,0:T(8,128)(2,1)S(1)} %convert_element_type.30), channel_id=1, source_target_pairs={{0,4},{2,6},{4,0},{6,2},{1,5},{3,7},{5,1},{7,3},{8,12},{10,14},{12... | collective-permute-start | bytes 55304 | tf_op jit(solution)/shard_map/ppermute | solution.py:198
  10.7 0.0 collective-permute-start.4
  10.7 0.0 collective-permute-done.peer_act
  10.7 0.0 collective-permute-done.1.peer_bg
  10.7 4.4 %shard_map.59 = bf16[5120,128]{1,0:T(8,128)(2,1)} custom-call(s32[1]{0:T(128)} %bitcast.4.core_ref, bf16[2,512,768]{2,1,0:T(8,128)(2,1)} %act.1, bf16[2,512,768]{2,1,0:T(8,128)(2,1)} %bg.1, bf16[2,512,768]{2,1,0:T(8,128)(2,1)} %collective-permute-done.peer_act, bf16[2,512,768]{2,1,0:T(8,128)(2,1)} %collective-permute-done.1.peer_bg), custom_call_target="tpu_custom_call" | custom-call | flops 2415919104 | bytes 3145728 | tf_op jit(solution)/shard_map/pallas_call | solution.py:203
  15.2 0.0 collective-permute-done.2
  15.2 0.0 collective-permute-done.3
  15.2 0.2 collective-permute-done.4
  15.4 7.5 %all-to-all-start = ((bf16[32,160,128]{2,1,0:T(8,128)(2,1)}), bf16[32,160,128]{2,1,0:T(8,128)(2,1)S(1)}, u32[]{:S(2)}, u32[]{:S(2)}) async-start(bf16[32,160,128]{2,1,0:T(8,128)(2,1)} %bitcast.24), calls=%async_computation | async-start | bytes 2621440 | tf_op jit(solution)/shard_map/all_to_all | solution.py:220
  22.9 2.5 %collective-permute-start.10 = (bf16[4,72,128]{2,1,0:T(8,128)(2,1)S(1)}, bf16[4,72,128]{2,1,0:T(8,128)(2,1)S(1)}, u32[]{:S(2)}, u32[]{:S(2)}) collective-permute-start(bf16[4,72,128]{2,1,0:T(8,128)(2,1)S(1)} %get-tuple-element.37), channel_id=1, source_target_pairs={{0,24},{8,16},{16,8},{24,0},{1,25},{9,17},{17,9},{25,1},{2,26},{10... | collective-permute-start | bytes 221192 | tf_op jit(solution)/shard_map/ppermute | solution.py:198
  25.5 0.6 collective-permute-start.9
  26.0 0.2 collective-permute-start.8
  26.3 12.5 %collective-permute-done.10 = bf16[4,72,128]{2,1,0:T(8,128)(2,1)S(1)} collective-permute-done((bf16[4,72,128]{2,1,0:T(8,128)(2,1)S(1)}, bf16[4,72,128]{2,1,0:T(8,128)(2,1)S(1)}, u32[]{:S(2)}, u32[]{:S(2)}) %collective-permute-start.10) | collective-permute-done | bytes 73760 | tf_op jit(solution)/shard_map/ppermute | solution.py:198
  38.8 3.7 %collective-permute-done.9 = bf16[4,72,128]{2,1,0:T(8,128)(2,1)S(1)} collective-permute-done((bf16[4,72,128]{2,1,0:T(8,128)(2,1)S(1)}, bf16[4,72,128]{2,1,0:T(8,128)(2,1)S(1)}, u32[]{:S(2)}, u32[]{:S(2)}) %collective-permute-start.9) | collective-permute-done | bytes 73760 | tf_op jit(solution)/shard_map/ppermute | solution.py:198
  42.5 0.0 collective-permute-done.8
  42.6 2.2 %collective-permute-start.11 = (bf16[4,4,72,128]{3,2,1,0:T(8,128)(2,1)S(1)}, bf16[4,4,72,128]{3,2,1,0:T(8,128)(2,1)S(1)}, u32[]{:S(2)}, u32[]{:S(2)}) collective-permute-start(bf16[4,4,72,128]{3,2,1,0:T(8,128)(2,1)S(1)} %pad_maximum_fusion.1), channel_id=1, source_target_pairs={{0,160},{160,0},{32,128},{128,32},{1,161},{161,1},{33,129},{129,33... | collective-permute-start | bytes 884744 | tf_op jit(solution)/shard_map/ppermute | solution.py:226
  44.7 0.0 all-to-all-done
  44.7 0.2 reduce_sum.12
  44.9 1.3 %collective-permute-start.5 = (bf16[160,128]{1,0:T(8,128)(2,1)S(1)}, bf16[160,128]{1,0:T(8,128)(2,1)S(1)}, u32[]{:S(2)}, u32[]{:S(2)}) collective-permute-start(bf16[160,128]{1,0:T(8,128)(2,1)S(1)} %reduce_sum.12), channel_id=1, source_target_pairs={{0,2},{2,0},{4,6},{6,4},{1,3},{3,1},{5,7},{7,5},{8,10},{10,8},{12,... | collective-permute-start | bytes 122888 | tf_op jit(solution)/shard_map/ppermute | solution.py:198
  46.2 4.2 %collective-permute-start.6 = (bf16[160,128]{1,0:T(8,128)(2,1)S(1)}, bf16[160,128]{1,0:T(8,128)(2,1)S(1)}, u32[]{:S(2)}, u32[]{:S(2)}) collective-permute-start(bf16[160,128]{1,0:T(8,128)(2,1)S(1)} %reduce_sum.12), channel_id=1, source_target_pairs={{0,4},{2,6},{4,0},{6,2},{1,5},{3,7},{5,1},{7,3},{8,12},{10,14},{12... | collective-permute-start | bytes 122888 | tf_op jit(solution)/shard_map/ppermute | solution.py:198
  50.5 0.2 collective-permute-start.7
  50.7 0.0 collective-permute-done.11
  50.7 0.0 collective-permute-done.5
  50.7 2.3 %collective-permute-done.6 = bf16[160,128]{1,0:T(8,128)(2,1)S(1)} collective-permute-done((bf16[160,128]{1,0:T(8,128)(2,1)S(1)}, bf16[160,128]{1,0:T(8,128)(2,1)S(1)}, u32[]{:S(2)}, u32[]{:S(2)}) %collective-permute-start.6) | collective-permute-done | bytes 40992 | tf_op jit(solution)/shard_map/ppermute | solution.py:198
  53.0 3.8 %collective-permute-done.7 = bf16[160,128]{1,0:T(8,128)(2,1)S(1)} collective-permute-done((bf16[160,128]{1,0:T(8,128)(2,1)S(1)}, bf16[160,128]{1,0:T(8,128)(2,1)S(1)}, u32[]{:S(2)}, u32[]{:S(2)}) %collective-permute-start.7) | collective-permute-done | bytes 40992 | tf_op jit(solution)/shard_map/ppermute | solution.py:198
  56.8 0.2 add_convert_fusion
  56.9 1.3 %broadcast_in_dim.12 = bf16[32,160,128]{2,1,0:T(8,128)(2,1)} broadcast(bf16[160,128]{1,0:T(8,128)(2,1)S(1)} %add_convert_fusion), dimensions={1,2} | broadcast | bytes 1351680 | tf_op jit(solution)/shard_map/broadcast_in_dim | solution.py:239
  58.2 4.6 %all-to-all-start.1 = ((bf16[32,160,128]{2,1,0:T(8,128)(2,1)}), bf16[32,160,128]{2,1,0:T(8,128)(2,1)S(1)}, u32[]{:S(2)}, u32[]{:S(2)}) async-start(bf16[32,160,128]{2,1,0:T(8,128)(2,1)} %broadcast_in_dim.12), calls=%async_computation.1 | async-start | bytes 2621440 | tf_op jit(solution)/shard_map/all_to_all | solution.py:240
  62.8 0.1 stack.62.place
  62.9 0.1 pad_maximum_fusion
  63.0 0.5 reshape.147
  63.5 0.8 convolution_convert_fusion.grads
  64.3 16.4 %all-to-all-done.1 = bf16[32,160,128]{2,1,0:T(8,128)(2,1)S(1)} async-done(((bf16[32,160,128]{2,1,0:T(8,128)(2,1)}), bf16[32,160,128]{2,1,0:T(8,128)(2,1)S(1)}, u32[]{:S(2)}, u32[]{:S(2)}) %all-to-all-start.1) | async-done | bytes 1310752 | tf_op jit(solution)/shard_map/all_to_all | solution.py:240
  80.6 6.3 %shard_map.60 = (f32[16,1728]{1,0:T(8,128)S(1)}, f32[16,192]{1,0:T(8,128)S(1)}, f32[16,192]{1,0:T(8,128)S(1)}, f32[16,192]{1,0:T(8,128)S(1)}) custom-call(s32[6]{0:T(128)S(1)} %stack.62.place, bf16[5120,128]{1,0:T(8,128)(2,1)S(1)} %bitcast.23, bf16[768,768]{1,0:T(8,128)(2,1)S(1)} %convolution_convert_fusion.grads), custom_call_target="tpu_custom_call" | custom-call | flops 2717908992 | bytes 4718592 | tf_op jit(solution)/shard_map/pallas_call | solution.py:254
  87.0 3.9 %collective-permute-start.12 = (f32[16,1728]{1,0:T(8,128)S(1)}, f32[16,1728]{1,0:T(8,128)S(1)}, u32[]{:S(2)}, u32[]{:S(2)}) collective-permute-start(f32[16,1728]{1,0:T(8,128)S(1)} %get-tuple-element.30.packed), channel_id=1, source_target_pairs={{0,64},{64,0},{1,65},{65,1},{2,66},{66,2},{3,67},{67,3},{4,68},{68... | collective-permute-start | bytes 331784 | tf_op jit(solution)/shard_map/ppermute | solution.py:264
  90.9 0.5 collective-permute-start.13
  91.4 1.2 %collective-permute-start.14 = (f32[16,192]{1,0:T(8,128)S(1)}, f32[16,192]{1,0:T(8,128)S(1)}, u32[]{:S(2)}, u32[]{:S(2)}) collective-permute-start(f32[16,192]{1,0:T(8,128)S(1)} %get-tuple-element.33), channel_id=1, source_target_pairs={{0,65},{65,0},{1,64},{64,1},{2,67},{67,2},{3,66},{66,3},{4,69},{69... | collective-permute-start | bytes 36872 | tf_op jit(solution)/shard_map/ppermute | solution.py:266
  92.6 0.9 collective-permute-done.13.near
  93.5 1.1 %collective-permute-done.14.cross = f32[16,192]{1,0:T(8,128)S(1)} collective-permute-done((f32[16,192]{1,0:T(8,128)S(1)}, f32[16,192]{1,0:T(8,128)S(1)}, u32[]{:S(2)}, u32[]{:S(2)}) %collective-permute-start.14) | collective-permute-done | bytes 12320 | tf_op jit(solution)/shard_map/ppermute | solution.py:266
  94.5 0.0 collective-permute-done.12.got
  94.5 0.0 copy-done.1
  94.5 1.2 %shard_map.61 = (f32[12,2,192]{2,1,0:T(2,128)}, f32[12,2,768]{2,1,0:T(2,128)}) custom-call(s32[4]{0:T(128)S(1)} %copy-done.1, s32[6]{0:T(128)S(1)} %stack.62.place, f32[16,1728]{1,0:T(8,128)S(1)} %get-tuple-element.30.packed, f32[16,1728]{1,0:T(8,128)S(1)} %collective-permute-done.12.got, f32[16,192]{1,0:T(8,128)S(1)} %get-tuple-element.31.mine, ...), custom_call_target="tpu_custom_call" | custom-call | tf_op jit(solution)/shard_map/pallas_call | solution.py:267
  (7 shorter events, 0.2 us)
Async XLA Ops:
  0.6 3.4 %copy-start = (f32[2,12,768]{2,0,1:T(2,128)S(1)}, f32[2,12,768]{2,0,1:T(2,128)}, u32[]{:S(2)}) copy-start(f32[2,12,768]{2,0,1:T(2,128)} %param.6) | copy-start | bytes 221188
  0.6 10.1 %collective-permute-start = (bf16[2,512,768]{2,1,0:T(8,128)(2,1)}, bf16[2,512,768]{2,1,0:T(8,128)(2,1)}, u32[]{:S(2)}, u32[]{:S(2)}) collective-permute-start(bf16[2,512,768]{2,1,0:T(8,128)(2,1)} %act.1), channel_id=1, source_target_pairs={{0,64},{64,0},{1,65},{65,1},{2,66},{66,2},{3,67},{67,3},{4,68},{68... | collective-permute-start | bytes 4718600 | tf_op jit(solution)/shard_map/ppermute | solution.py:195
  4.0 6.7 %collective-permute-start.1 = (bf16[2,512,768]{2,1,0:T(8,128)(2,1)}, bf16[2,512,768]{2,1,0:T(8,128)(2,1)}, u32[]{:S(2)}, u32[]{:S(2)}) collective-permute-start(bf16[2,512,768]{2,1,0:T(8,128)(2,1)} %bg.1), channel_id=1, source_target_pairs={{0,64},{64,0},{1,65},{65,1},{2,66},{66,2},{3,67},{67,3},{4,68},{68... | collective-permute-start | bytes 4718600 | tf_op jit(solution)/shard_map/ppermute | solution.py:195
  4.2 10.9 %collective-permute-start.2 = (bf16[72,128]{1,0:T(8,128)(2,1)S(1)}, bf16[72,128]{1,0:T(8,128)(2,1)S(1)}, u32[]{:S(2)}, u32[]{:S(2)}) collective-permute-start(bf16[72,128]{1,0:T(8,128)(2,1)S(1)} %convert_element_type.30), channel_id=1, source_target_pairs={{0,2},{2,0},{4,6},{6,4},{1,3},{3,1},{5,7},{7,5},{8,10},{10,8},{12,... | collective-permute-start | bytes 55304 | tf_op jit(solution)/shard_map/ppermute | solution.py:198
  5.6 9.6 %collective-permute-start.3 = (bf16[72,128]{1,0:T(8,128)(2,1)S(1)}, bf16[72,128]{1,0:T(8,128)(2,1)S(1)}, u32[]{:S(2)}, u32[]{:S(2)}) collective-permute-start(bf16[72,128]{1,0:T(8,128)(2,1)S(1)} %convert_element_type.30), channel_id=1, source_target_pairs={{0,4},{2,6},{4,0},{6,2},{1,5},{3,7},{5,1},{7,3},{8,12},{10,14},{12... | collective-permute-start | bytes 55304 | tf_op jit(solution)/shard_map/ppermute | solution.py:198
  10.7 4.7 %collective-permute-start.4 = (bf16[72,128]{1,0:T(8,128)(2,1)S(1)}, bf16[72,128]{1,0:T(8,128)(2,1)S(1)}, u32[]{:S(2)}, u32[]{:S(2)}) collective-permute-start(bf16[72,128]{1,0:T(8,128)(2,1)S(1)} %convert_element_type.30), channel_id=1, source_target_pairs={{0,6},{2,4},{4,2},{6,0},{1,7},{3,5},{5,3},{7,1},{8,14},{10,12},{12... | collective-permute-start | bytes 55304 | tf_op jit(solution)/shard_map/ppermute | solution.py:198
  15.4 29.3 %all-to-all-start = ((bf16[32,160,128]{2,1,0:T(8,128)(2,1)}), bf16[32,160,128]{2,1,0:T(8,128)(2,1)S(1)}, u32[]{:S(2)}, u32[]{:S(2)}) async-start(bf16[32,160,128]{2,1,0:T(8,128)(2,1)} %bitcast.24), calls=%async_computation | async-start | bytes 2621440 | tf_op jit(solution)/shard_map/all_to_all | solution.py:220
  22.9 15.9 %collective-permute-start.10 = (bf16[4,72,128]{2,1,0:T(8,128)(2,1)S(1)}, bf16[4,72,128]{2,1,0:T(8,128)(2,1)S(1)}, u32[]{:S(2)}, u32[]{:S(2)}) collective-permute-start(bf16[4,72,128]{2,1,0:T(8,128)(2,1)S(1)} %get-tuple-element.37), channel_id=1, source_target_pairs={{0,24},{8,16},{16,8},{24,0},{1,25},{9,17},{17,9},{25,1},{2,26},{10... | collective-permute-start | bytes 221192 | tf_op jit(solution)/shard_map/ppermute | solution.py:198
  25.5 17.0 %collective-permute-start.9 = (bf16[4,72,128]{2,1,0:T(8,128)(2,1)S(1)}, bf16[4,72,128]{2,1,0:T(8,128)(2,1)S(1)}, u32[]{:S(2)}, u32[]{:S(2)}) collective-permute-start(bf16[4,72,128]{2,1,0:T(8,128)(2,1)S(1)} %get-tuple-element.37), channel_id=1, source_target_pairs={{0,16},{8,24},{16,0},{24,8},{1,17},{9,25},{17,1},{25,9},{2,18},{10... | collective-permute-start | bytes 221192 | tf_op jit(solution)/shard_map/ppermute | solution.py:198
  26.0 16.5 %collective-permute-start.8 = (bf16[4,72,128]{2,1,0:T(8,128)(2,1)S(1)}, bf16[4,72,128]{2,1,0:T(8,128)(2,1)S(1)}, u32[]{:S(2)}, u32[]{:S(2)}) collective-permute-start(bf16[4,72,128]{2,1,0:T(8,128)(2,1)S(1)} %get-tuple-element.37), channel_id=1, source_target_pairs={{0,8},{8,0},{16,24},{24,16},{1,9},{9,1},{17,25},{25,17},{2,10},{10... | collective-permute-start | bytes 221192 | tf_op jit(solution)/shard_map/ppermute | solution.py:198
  42.6 8.2 %collective-permute-start.11 = (bf16[4,4,72,128]{3,2,1,0:T(8,128)(2,1)S(1)}, bf16[4,4,72,128]{3,2,1,0:T(8,128)(2,1)S(1)}, u32[]{:S(2)}, u32[]{:S(2)}) collective-permute-start(bf16[4,4,72,128]{3,2,1,0:T(8,128)(2,1)S(1)} %pad_maximum_fusion.1), channel_id=1, source_target_pairs={{0,160},{160,0},{32,128},{128,32},{1,161},{161,1},{33,129},{129,33... | collective-permute-start | bytes 884744 | tf_op jit(solution)/shard_map/ppermute | solution.py:226
  44.9 5.8 %collective-permute-start.5 = (bf16[160,128]{1,0:T(8,128)(2,1)S(1)}, bf16[160,128]{1,0:T(8,128)(2,1)S(1)}, u32[]{:S(2)}, u32[]{:S(2)}) collective-permute-start(bf16[160,128]{1,0:T(8,128)(2,1)S(1)} %reduce_sum.12), channel_id=1, source_target_pairs={{0,2},{2,0},{4,6},{6,4},{1,3},{3,1},{5,7},{7,5},{8,10},{10,8},{12,... | collective-permute-start | bytes 122888 | tf_op jit(solution)/shard_map/ppermute | solution.py:198
  46.2 6.8 %collective-permute-start.6 = (bf16[160,128]{1,0:T(8,128)(2,1)S(1)}, bf16[160,128]{1,0:T(8,128)(2,1)S(1)}, u32[]{:S(2)}, u32[]{:S(2)}) collective-permute-start(bf16[160,128]{1,0:T(8,128)(2,1)S(1)} %reduce_sum.12), channel_id=1, source_target_pairs={{0,4},{2,6},{4,0},{6,2},{1,5},{3,7},{5,1},{7,3},{8,12},{10,14},{12... | collective-permute-start | bytes 122888 | tf_op jit(solution)/shard_map/ppermute | solution.py:198
  50.5 6.3 %collective-permute-start.7 = (bf16[160,128]{1,0:T(8,128)(2,1)S(1)}, bf16[160,128]{1,0:T(8,128)(2,1)S(1)}, u32[]{:S(2)}, u32[]{:S(2)}) collective-permute-start(bf16[160,128]{1,0:T(8,128)(2,1)S(1)} %reduce_sum.12), channel_id=1, source_target_pairs={{0,6},{2,4},{4,2},{6,0},{1,7},{3,5},{5,3},{7,1},{8,14},{10,12},{12... | collective-permute-start | bytes 122888 | tf_op jit(solution)/shard_map/ppermute | solution.py:198
  58.2 22.5 %all-to-all-start.1 = ((bf16[32,160,128]{2,1,0:T(8,128)(2,1)}), bf16[32,160,128]{2,1,0:T(8,128)(2,1)S(1)}, u32[]{:S(2)}, u32[]{:S(2)}) async-start(bf16[32,160,128]{2,1,0:T(8,128)(2,1)} %broadcast_in_dim.12), calls=%async_computation.1 | async-start | bytes 2621440 | tf_op jit(solution)/shard_map/all_to_all | solution.py:240
  80.6 13.9 %copy-start.1 = (s32[4]{0:T(128)S(1)}, s32[4]{0:T(128)}, u32[]{:S(2)}) copy-start(s32[4]{0:T(128)} %owners.1) | copy-start | bytes 52
  87.0 7.6 %collective-permute-start.12 = (f32[16,1728]{1,0:T(8,128)S(1)}, f32[16,1728]{1,0:T(8,128)S(1)}, u32[]{:S(2)}, u32[]{:S(2)}) collective-permute-start(f32[16,1728]{1,0:T(8,128)S(1)} %get-tuple-element.30.packed), channel_id=1, source_target_pairs={{0,64},{64,0},{1,65},{65,1},{2,66},{66,2},{3,67},{67,3},{4,68},{68... | collective-permute-start | bytes 331784 | tf_op jit(solution)/shard_map/ppermute | solution.py:264
  90.9 2.6 %collective-permute-start.13 = (f32[16,192]{1,0:T(8,128)S(1)}, f32[16,192]{1,0:T(8,128)S(1)}, u32[]{:S(2)}, u32[]{:S(2)}) collective-permute-start(f32[16,192]{1,0:T(8,128)S(1)} %get-tuple-element.32), channel_id=1, source_target_pairs={{0,1},{1,0},{2,3},{3,2},{4,5},{5,4},{6,7},{7,6},{8,9},{9,8},{10,11... | collective-permute-start | bytes 36872 | tf_op jit(solution)/shard_map/ppermute | solution.py:265
  91.4 3.2 %collective-permute-start.14 = (f32[16,192]{1,0:T(8,128)S(1)}, f32[16,192]{1,0:T(8,128)S(1)}, u32[]{:S(2)}, u32[]{:S(2)}) collective-permute-start(f32[16,192]{1,0:T(8,128)S(1)} %get-tuple-element.33), channel_id=1, source_target_pairs={{0,65},{65,0},{1,64},{64,1},{2,67},{67,2},{3,66},{66,3},{4,69},{69... | collective-permute-start | bytes 36872 | tf_op jit(solution)/shard_map/ppermute | solution.py:266
